TPU v7x, 32 devices: a whole 2x2x4 slice. The times are simulated.
32 devices in a mesh: row: 4 (over y, x), col: 8 (over z, core).
Axes of the slice: x: 2, y: 2, z: 4, core: 2. Of those that a mesh axis runs over, the one named last changes fastest.
Arguments:
- samples: float32 [1024, 64, 128], P(('row', 'col')), may hold values from -6 to 6
- omega: float32 [4, 8, 128, 128, 128], P('row', 'col'), may hold values from -0.12 to 2.12
- block_rows: int32 [4, 8, 128], P('row', 'col'), may hold values from -1 to 1023, as said below
- block_cols: int32 [4, 8, 128], P('row', 'col'), may hold values from -1 to 1023, as said below
Outputs:
- omega_next: float32 [4, 8, 128, 128, 128], P('row', 'col')
Inputs may be any that keep to these rules, and one draw needn't show every extreme that they name: `block_rows`: slots 0 to 31 of the device at (a, b) hold the diagonal blocks I = J = (a * 8 + b) * 32 + k in order of k; the other slots hold distinct off-diagonal blocks whose block row lies in a * 1024 / 4 up to (a + 1) * 1024 / 4 - 1 and whose block column J has (J // 32) % 8 = b; live slots come first and -1 fills the rest; some device has all 128 slots live. `block_cols`: -1 exactly where block_rows is -1.
All inputs are finite; a program needn't handle non-finite values.
Results may differ from a plain program's by a relative error of at most 0.0003.
Values sent between devices are 32-bit elements; how exact they have to be, the bound alone decides.
No kernel may reach another device: no remote copies, remote signals or barrier semaphores. Data moves between devices by JAX's collectives and lax.ppermute only.
A program may use at most 128 MiB of HBM per device.

v0:
```python
import jax
import jax.numpy as jnp
from jax import lax
from jax.sharding import PartitionSpec as P

ITERS = 2


STEP = 0.5
PENALTY = 0.1


def gradient_blocks(left_totals, right_samples, left_samples, right_totals, sample_count):
    forward = jnp.einsum(
        "snb,snk->sbk", left_totals, right_samples, precision=lax.Precision.HIGHEST
    )
    mirrored = jnp.einsum(
        "snb,snk->sbk", left_samples, right_totals, precision=lax.Precision.HIGHEST
    )
    return (forward + mirrored) * (0.5 / sample_count)


def proximal(current, grad, active, on_diagonal):
    stepped = current - STEP * grad
    eye_mask = jnp.eye(current.shape[-1], dtype=bool)[None] & on_diagonal[:, None, None]
    shrunk = jnp.sign(stepped) * jnp.maximum(jnp.abs(stepped) - STEP * PENALTY, 0.0)
    lifted = 0.5 * (stepped + jnp.sqrt(stepped * stepped + 4.0 * STEP))
    updated = jnp.where(eye_mask, lifted, shrunk)
    return jnp.where(active[:, None, None], updated, 0.0)


def shards(samples, omega, block_rows, block_cols):
    col_count = lax.axis_size("col")
    col_index = lax.axis_index("col")
    row_index = lax.axis_index("row")
    slab_blocks = samples.shape[0]
    sample_count = samples.shape[1]
    width = samples.shape[2]
    group_rows = slab_blocks * col_count
    current = omega[0, 0]
    row_ids = block_rows[0, 0]
    col_ids = block_cols[0, 0]
    active = row_ids >= 0
    local_rows = jnp.where(active, row_ids - row_index * group_rows, -1)
    safe_rows = jnp.maximum(local_rows, 0)
    slab_ids = col_ids // slab_blocks
    local_cols = jnp.where(active, slab_ids // col_count * slab_blocks + col_ids % slab_blocks, 0)
    on_diagonal = active & (row_ids == col_ids)
    row_samples = lax.all_gather(samples, "col", axis=0, tiled=True)
    col_samples = lax.all_gather(samples, "row", axis=0, tiled=True)
    picked_cols = col_samples[local_cols]
    picked_rows = row_samples[safe_rows]
    for iteration in range(ITERS):
        products = jnp.einsum("snk,sbk->snb", picked_cols, current, precision=lax.Precision.HIGHEST)
        flattened = products.reshape(products.shape[0], -1)
        selector = (local_rows[None, :] == jnp.arange(group_rows)[:, None]).astype(jnp.float32)
        summed_part = jnp.dot(selector, flattened, precision=lax.Precision.HIGHEST)
        row_totals = lax.psum(summed_part.reshape(group_rows, sample_count, width), "col")
        own_totals = lax.dynamic_slice_in_dim(row_totals, col_index * slab_blocks, slab_blocks, 0)
        col_totals = lax.all_gather(own_totals, "row", axis=0, tiled=True)
        grad = gradient_blocks(
            row_totals[safe_rows], picked_cols, picked_rows, col_totals[local_cols], sample_count
        )
        current = proximal(current, grad, active, on_diagonal)
    return current[None, None]


def solution(mesh):
    return jax.shard_map(
        shards,
        mesh=mesh,
        in_specs=(
            P(("row", "col"), None, None),
            P("row", "col", None, None, None),
            P("row", "col", None),
            P("row", "col", None),
        ),
        out_specs=P("row", "col", None, None, None),
        check_vma=False,
    )
```

profile of v0, /device:TPU:0, one launch (start us, length us, event | category | flops | bytes accessed | tf_op | source)
XLA Modules:
  0.0 774.4 jit_solution(17251935370216293286)
XLA Ops:
  6.5 0.7 all-gather.5.cloned.1.call-update
  8.7 56.0 %all-gather.5.cloned.1.call-done = f32[128,64,128]{2,1,0:T(8,128)} async-done(((f32[32,64,128]{2,1,0:T(8,128)}), f32[128,64,128]{2,1,0:T(8,128)}) %all-gather.5.cloned.1.call-update) | async-done | bytes 4194320 | tf_op jit(solution)/shard_map/all_gather | solution.py:50
  64.6 5.0 gather_fusion
  69.6 19.2 %fusion.3 = f32[128,64,128]{2,1,0:T(8,128)S(1)} fusion(f32[128,64,128]{2,1,0:T(8,128)} %gather_fusion, f32[1,1,128,128,128]{4,3,2,1,0:T(8,128)} %param.5), kind=kOutput, calls=%fused_computation.12 | convolution fusion | flops 1610612736 | bytes 16777216 | tf_op jit(solution)/shard_map/snk,sbk->snb/dot_general | solution.py:54
  88.8 5.3 copy.28
  94.1 5.6 copy.17
  99.7 8.9 %fusion.8 = f32[256,64,128]{2,0,1:T(8,128)} fusion(f32[64,128,128]{2,1,0:T(8,128)} %bitcast.83, s32[128]{0:T(128)S(1)} %bitcast_select_fusion.2), kind=kOutput, calls=%fused_computation.19 | convolution fusion | flops 3221258240 | bytes 12583424 | tf_op jit(solution)/shard_map/dot_general | solution.py:57
  109.4 174.9 %all-reduce.3.cloned.1.call-done = f32[256,64,128]{2,0,1:T(8,128)} async-done(((f32[256,64,128]{2,0,1:T(8,128)}), f32[256,64,128]{2,0,1:T(8,128)}) %all-reduce.3.cloned.1.call-update) | async-done | bytes 8388624 | tf_op jit(solution)/shard_map/psum | solution.py:58
  284.3 2.3 constant_dynamic-slice_fusion.1
  286.6 11.2 %all-reduce.5.cloned.1.call-start = ((), (), s32[]{:S(2)}) async-start(), calls=%async_computation.4 | async-start | bytes 16777216 | tf_op jit(solution)/shard_map/psum | solution.py:58
  297.9 11.6 %copy.18 = f32[256,64,128]{2,1,0:T(8,128)} copy(f32[256,64,128]{2,0,1:T(8,128)} %all-reduce.3.cloned.1.call-done) | data formatting | bytes 16777216 | tf_op jit(solution)/shard_map/psum | solution.py:58
  309.5 6.3 gather_fusion.1
  315.8 17.8 %fusion.17 = f32[128,128,128]{2,1,0:T(8,128)} fusion(f32[128,64,128]{2,1,0:T(8,128)} %gather_fusion.1, f32[128,64,128]{2,1,0:T(8,128)} %gather_fusion), kind=kOutput, calls=%fused_computation.48 | convolution fusion | flops 1610612736 | bytes 16777216 | tf_op jit(solution)/shard_map/snb,snk->sbk/dot_general | solution.py:14
  333.6 34.5 %all-gather.7.cloned.1.call-done = f32[256,64,128]{2,1,0:T(8,128)} async-done(((f32[32,64,128]{2,1,0:T(8,128)}), f32[256,64,128]{2,1,0:T(8,128)}) %all-gather.7.cloned.1.call-update) | async-done | bytes 8388624 | tf_op jit(solution)/shard_map/all_gather | solution.py:49
  368.1 6.2 gather_fusion.2
  374.3 46.8 %all-gather.9.cloned.1.call-done = f32[128,64,128]{2,0,1:T(8,128)} async-done(((f32[32,64,128]{2,0,1:T(8,128)}), f32[128,64,128]{2,0,1:T(8,128)}) %all-gather.9.cloned.1.call-update) | async-done | bytes 4194320 | tf_op jit(solution)/shard_map/all_gather | solution.py:60
  421.1 6.6 copy.19
  427.6 5.0 gather_fusion.3
  432.6 27.2 %fusion = f32[128,128,128]{2,1,0:T(8,128)S(1)} fusion(f32[1,1,128,128,128]{4,3,2,1,0:T(8,128)} %param.5, f32[128,128,128]{2,1,0:T(8,128)} %fusion.17, pred[128]{0:T(512)(128)(4,1)S(1)} %fusion.16, pred[128,128]{1,0:T(8,128)(4,1)S(1)} %iota_compare_fusion.1, pred[128]{0:T(512)(128)(4,1)S(1)} %bitcast_and_fusion, f32[128,64,128]{2,1,0:T(8,128)} %gather_fusion.2, ...), kind=kOutput, calls=%fused_computation.8 | convolution fusion | flops 1642070016 | bytes 33571072 | tf_op jit(solution)/shard_map/snb,snk->sbk/dot_general | solution.py:17
  459.9 16.7 %fusion.18 = f32[128,64,128]{2,1,0:T(8,128)S(1)} fusion(f32[128,64,128]{2,1,0:T(8,128)S(1)} %copy-done, f32[128,128,128]{2,1,0:T(8,128)S(1)} %fusion), kind=kOutput, calls=%fused_computation.49 | convolution fusion | flops 1610612736 | bytes 16777216 | tf_op jit(solution)/shard_map/snk,sbk->snb/dot_general | solution.py:54
  476.6 5.5 copy.27
  482.1 5.6 copy.20
  487.7 8.9 %fusion.6 = f32[256,64,128]{2,0,1:T(8,128)} fusion(f32[64,128,128]{2,1,0:T(8,128)} %bitcast.81, s32[128]{0:T(128)S(1)} %bitcast_select_fusion.2), kind=kOutput, calls=%fused_computation.18 | convolution fusion | flops 3221258240 | bytes 12583424 | tf_op jit(solution)/shard_map/dot_general | solution.py:57
  496.6 175.7 %all-reduce.5.cloned.1.call-done = f32[256,64,128]{2,0,1:T(8,128)} async-done(((f32[256,64,128]{2,0,1:T(8,128)}), f32[256,64,128]{2,0,1:T(8,128)}) %all-reduce.5.cloned.1.call-update) | async-done | bytes 8388624 | tf_op jit(solution)/shard_map/psum | solution.py:58
  672.3 2.3 constant_dynamic-slice_fusion
  674.6 11.5 %copy.21 = f32[256,64,128]{2,1,0:T(8,128)} copy(f32[256,64,128]{2,0,1:T(8,128)} %all-reduce.5.cloned.1.call-done) | data formatting | bytes 16777216 | tf_op jit(solution)/shard_map/psum | solution.py:58
  686.1 6.1 gather_fusion.4
  692.2 18.1 %fusion.19 = f32[128,128,128]{2,1,0:T(8,128)} fusion(f32[128,64,128]{2,1,0:T(8,128)} %gather_fusion.4, f32[128,64,128]{2,1,0:T(8,128)} %gather_fusion), kind=kOutput, calls=%fused_computation.50 | convolution fusion | flops 1610612736 | bytes 16777216 | tf_op jit(solution)/shard_map/snb,snk->sbk/dot_general | solution.py:14
  710.3 17.3 %all-gather.11.cloned.1.call-done = f32[128,64,128]{2,0,1:T(8,128)} async-done(((f32[32,64,128]{2,0,1:T(8,128)}), f32[128,64,128]{2,0,1:T(8,128)}) %all-gather.11.cloned.1.call-update) | async-done | bytes 4194320 | tf_op jit(solution)/shard_map/all_gather | solution.py:60
  727.6 6.5 copy.22
  734.2 5.0 gather_fusion.5
  739.1 28.3 %fusion.2 = f32[1,1,128,128,128]{4,3,2,1,0:T(8,128)} fusion(f32[128,128,128]{2,1,0:T(8,128)} %copy-done.1, f32[128,128,128]{2,1,0:T(8,128)} %fusion.19, pred[128]{0:T(512)(128)(4,1)S(1)} %fusion.16, pred[128,128]{1,0:T(8,128)(4,1)S(1)} %iota_compare_fusion.1, pred[128]{0:T(512)(128)(4,1)S(1)} %bitcast_and_fusion, f32[128,64,128]{2,1,0:T(8,128)} %gather_fusion.2, ...), kind=kOutput, calls=%fused_computation.10 | convolution fusion | flops 1642070016 | bytes 33571072 | tf_op jit(solution)/shard_map/snb,snk->sbk/dot_general | solution.py:17
  (25 shorter events, 2.3 us)
Async XLA Ops:
  6.5 58.1 %all-gather.5.cloned.1.call-start = ((), (), s32[]{:S(2)}) async-start(), calls=%async_computation | async-start | bytes 5242880 | tf_op jit(solution)/shard_map/all_gather | solution.py:50
  7.3 277.0 %all-reduce.3.cloned.1.call-start = ((), (), s32[]{:S(2)}) async-start(), calls=%async_computation.1 | async-start | bytes 16777216 | tf_op jit(solution)/shard_map/psum | solution.py:58
  108.6 189.3 %copy-start.2 = (s32[1,1,128]{2,1,0:T(1,128)S(1)}, s32[1,1,128]{2,1,0:T(1,128)}, u32[]{:S(2)}) copy-start(s32[1,1,128]{2,1,0:T(1,128)} %param.6) | copy-start | bytes 1540
  108.6 189.3 %copy-start.3 = (s32[1,1,128]{2,1,0:T(1,128)S(1)}, s32[1,1,128]{2,1,0:T(1,128)}, u32[]{:S(2)}) copy-start(s32[1,1,128]{2,1,0:T(1,128)} %param.7) | copy-start | bytes 1540
  108.6 259.5 %all-gather.7.cloned.1.call-start = ((), (), s32[]{:S(2)}) async-start(), calls=%async_computation.2 | async-start | bytes 9437184 | tf_op jit(solution)/shard_map/all_gather | solution.py:49
  109.3 311.7 %all-gather.9.cloned.1.call-start = ((), (), s32[]{:S(2)}) async-start(), calls=%async_computation.3 | async-start | bytes 5242880 | tf_op jit(solution)/shard_map/all_gather | solution.py:60
  286.6 385.7 %all-reduce.5.cloned.1.call-start = ((), (), s32[]{:S(2)}) async-start(), calls=%async_computation.4 | async-start | bytes 16777216 | tf_op jit(solution)/shard_map/psum | solution.py:58
  432.6 27.2 %copy-start = (f32[128,64,128]{2,1,0:T(8,128)S(1)}, f32[128,64,128]{2,1,0:T(8,128)}, u32[]{:S(2)}) copy-start(f32[128,64,128]{2,1,0:T(8,128)} %gather_fusion) | copy-start | bytes 12582916
  459.9 16.8 %copy-start.1 = (f32[128,128,128]{2,1,0:T(8,128)}, f32[128,128,128]{2,1,0:T(8,128)S(1)}, u32[]{:S(2)}) copy-start(f32[128,128,128]{2,1,0:T(8,128)S(1)} %fusion) | copy-start | bytes 25165828
  496.6 231.0 %all-gather.11.cloned.1.call-start = ((), (), s32[]{:S(2)}) async-start(), calls=%async_computation.5 | async-start | bytes 5242880 | tf_op jit(solution)/shard_map/all_gather | solution.py:60
Sparse Core Ops, SparseCore 0:
  9.2 55.3 all-gather.4
  108.7 175.5 all-reduce.2
  285.9 82.1 all-gather.6
  369.8 51.2 all-gather.8
  496.7 175.5 all-reduce.4
  674.7 52.8 all-gather.10
where the time goes:
time: 784 us; the launch traced here: 774 us
  waiting for transfers between devices  507 us (65%)
  matrix products  145 us (18%)
  local copies, waits for them, and re-layouts  96.3 us (12%)
  between operations  13.8 us (2%)
  starting transfers between devices  11.3 us (1%)
    psum x2, waiting for transfers between devices, shards(): lax.psum(summed_part.reshape(group_rows, sample_count, width), 'col')  351 us
    all_gather x2, waiting for transfers between devices, shards(): col_totals = lax.all_gather(own_totals, 'row', axis=0, tiled=True)  64.1 us
    all_gather x1, waiting for transfers between devices, shards(): col_samples = lax.all_gather(samples, 'row', axis=0, tiled=True)  56 us
    dot_general x2, matrix products, gradient_blocks(): jnp.einsum('snb,snk->sbk', left_samples, right_totals, precision=lax.Prec...  55.5 us
    dot_general x2, matrix products, shards(): jnp.einsum('snk,sbk->snb', picked_cols, current, precision=lax.Precision....  35.9 us
    dot_general x2, matrix products, gradient_blocks(): jnp.einsum('snb,snk->sbk', left_totals, right_samples, precision=lax.Prec...  35.9 us
    all_gather x1, waiting for transfers between devices, shards(): row_samples = lax.all_gather(samples, 'col', axis=0, tiled=True)  34.5 us
    psum x2, local copies, waits for them, and re-layouts, shards(): lax.psum(summed_part.reshape(group_rows, sample_count, width), 'col')  23.1 us
  transfers between devices with their start and end apart: 6, of which 6 were waited for; matrix products, arithmetic and copies ran while one was open for 10% of the time, Pallas kernels for 0%

commit v1 on v0

v1 whole, which is shorter than its diff:
```python
import functools

import jax
import jax.numpy as jnp
from jax import lax
from jax.experimental import pallas as pl
from jax.experimental.pallas import tpu as pltpu
from jax.sharding import PartitionSpec as P

ITERS = 2
STEP = 0.5
PENALTY = 0.1
VMEM_BYTES = 56 * 1024 * 1024
CORES = 2


def split(x):
    high = x.astype(jnp.bfloat16)
    low = (x - high.astype(jnp.float32)).astype(jnp.bfloat16)
    return high, low


def dot(a, b, dims):
    return lax.dot_general(a, b, (dims, ((), ())), preferred_element_type=jnp.float32)


def product(x, block):
    x_high, x_low = split(x)
    o_high, o_low = split(block)
    count = x.shape[0]
    both = dot(jnp.concatenate([x_high, x_low], 0), o_high, ((1,), (1,)))
    return both[:count] + both[count:] + dot(x_high, o_low, ((1,), (1,)))


def gradient(left_w, right_x, left_x, right_w):
    a_high, a_low = split(jnp.concatenate([left_w, left_x], 0))
    b_high, b_low = split(jnp.concatenate([right_x, right_w], 0))
    dims = ((0,), (0,))
    first = dot(jnp.concatenate([a_high, a_low], 0), jnp.concatenate([b_high, b_high], 0), dims)
    return first + dot(a_high, b_low, dims)


def shrink(v):
    level = STEP * PENALTY
    return v - jnp.clip(v, -level, level)


def lift_diagonal(v, shrunk):
    rows = lax.broadcasted_iota(jnp.int32, v.shape, 0)
    cols = lax.broadcasted_iota(jnp.int32, v.shape, 1)
    eye = rows == cols
    entries = jnp.sum(jnp.where(eye, v, 0.0), axis=0, keepdims=True)
    lifted = 0.5 * (entries + jnp.sqrt(entries * entries + 4.0 * STEP))
    return jnp.where(eye, lifted, shrunk)


def block_count(*sizes):
    for count in (16, 8, 4, 2):
        if all(size % count == 0 for size in sizes):
            return count
    return 1


def diag_products_kernel(x_ref, omega_ref, p_ref):
    for k in range(x_ref.shape[0]):
        p_ref[k] = product(x_ref[k], omega_ref[k])


def diag_update_kernel(scale, last, x_ref, w_ref, omega_ref, out_ref, *p_refs):
    for k in range(x_ref.shape[0]):
        x, w = x_ref[k], w_ref[k]
        v = omega_ref[k] - STEP * (gradient(w, x, x, w) * scale)
        new = lift_diagonal(v, shrink(v))
        out_ref[k] = new
        if not last:
            p_refs[0][k] = product(x, new)


def params():
    return pltpu.CompilerParams(vmem_limit_bytes=VMEM_BYTES)


def cost(slots, dims, passes, extra=0):
    count, width = dims
    return pl.CostEstimate(
        flops=2 * slots * passes * count * width * width,
        bytes_accessed=slots * (2 * width * width + 4 * count * width) * 4 + extra,
        transcendentals=0,
    )


def diag_products(x, omega):
    slab, count, width = x.shape
    size = block_count(slab)
    x_spec = pl.BlockSpec((size, count, width), lambda i: (i, 0, 0))
    o_spec = pl.BlockSpec((size, width, width), lambda i: (i, 0, 0))
    return pl.pallas_call(
        diag_products_kernel,
        grid=(slab // size,),
        in_specs=[x_spec, o_spec],
        out_specs=x_spec,
        out_shape=jax.ShapeDtypeStruct(x.shape, jnp.float32),
        compiler_params=params(),
        cost_estimate=cost(slab, (count, width), 3),
        name="diag_products",
    )(x, omega)


def diag_update(x, w, omega, last):
    slab, count, width = x.shape
    size = block_count(slab)
    x_spec = pl.BlockSpec((size, count, width), lambda i: (i, 0, 0))
    o_spec = pl.BlockSpec((size, width, width), lambda i: (i, 0, 0))
    outs = [jax.ShapeDtypeStruct(omega.shape, jnp.float32)]
    specs = [o_spec]
    if not last:
        outs.append(jax.ShapeDtypeStruct(x.shape, jnp.float32))
        specs.append(x_spec)
    return pl.pallas_call(
        functools.partial(diag_update_kernel, 0.5 / count, last),
        grid=(slab // size,),
        in_specs=[x_spec, x_spec, o_spec],
        out_specs=specs,
        out_shape=outs,
        compiler_params=params(),
        cost_estimate=cost(slab, (count, width), 9),
        name="diag_update",
    )(x, w, omega)


def off_kernel(plan, scalars, *refs):
    update, products, scale, size, slab, n_col, n_row, choices = plan
    steps = pl.num_programs(0)
    step = pl.program_id(0)
    refs = list(refs)
    take = lambda n: [refs.pop(0) for _ in range(n)]
    col_x_parts = take(n_col)
    col_w_parts = take(n_col) if update else []
    row_x_parts = take(n_row) if update else []
    row_w_parts = take(n_row) if update else []
    if update:
        take(1)
    (omega_ref,) = take(1)
    out_refs = take(1) if update else []
    p_refs = take(2) if products else []
    col_x = take(1)[0]
    col_w, row_x, row_w = take(3) if update else (None, None, None)
    acc = take(1)[0] if products else None
    (sems,) = take(1)
    (p_sems,) = take(1) if products else (None,)
    z_index = scalars[3, 0]

    copies = []

    def add(condition, source, target):
        copies.append((condition, pltpu.make_async_copy(source, target, sems.at[len(copies)])))

    def columns(parts, target):
        at = 0
        for part in parts:
            add(None, part, target.at[pl.ds(at, part.shape[0])])
            at += part.shape[0]

    def rows(parts, target):
        for part, (at, wanted) in zip(parts, choices):
            condition = None
            if wanted is not None:
                bound, above = wanted
                condition = z_index < bound if above else z_index >= bound
            add(condition, part, target.at[pl.ds(at, part.shape[0])])

    columns(col_x_parts, col_x)
    if update:
        columns(col_w_parts, col_w)
        rows(row_x_parts, row_x)
        rows(row_w_parts, row_w)

    def each(action):
        for condition, copy in copies:
            if condition is None:
                action(copy)
            else:
                pl.when(condition)(functools.partial(action, copy))

    @pl.when(step == 0)
    def _():
        each(lambda copy: copy.start())
        if products:
            acc[...] = jnp.zeros_like(acc)
        each(lambda copy: copy.wait())

    for k in range(size):
        slot = step * size + k
        target = scalars[0, slot]
        column = scalars[1, slot]
        x = col_x[column]
        block = omega_ref[k]
        if update:
            source = scalars[2, slot]
            grad = gradient(row_w[source], x, row_x[source], col_w[column]) * scale
            block = jnp.where(scalars[4, slot] > 0, shrink(block - STEP * grad), 0.0)
            out_refs[0][k] = block
        if products:
            acc[target] += product(x, block)

    if products:

        @pl.when(step == steps - 1)
        def _():
            half = p_refs[0].shape[0]
            outs = [
                pltpu.make_async_copy(acc.at[pl.ds(side * half, half)], p_refs[side], p_sems.at[side])
                for side in range(2)
            ]
            for copy in outs:
                copy.start()
            for copy in outs:
                copy.wait()


def off_slots(scalars, col_x, omega, slab, half, choices, state=None, products=True):
    update = state is not None
    cap, width = omega.shape[0], omega.shape[1]
    count = col_x[0].shape[1]
    off = cap - slab
    size = block_count(slab, off)
    any_spec = pl.BlockSpec(memory_space=pl.ANY)
    slots = pl.BlockSpec((size, width, width), lambda i, s: (slab // size + i, 0, 0))
    col_blocks = sum(part.shape[0] for part in col_x)
    block = (count, width)
    operands = list(col_x)
    scratch = [pltpu.VMEM((col_blocks,) + block, jnp.float32)]
    copies = len(col_x)
    n_row = 0
    if update:
        col_w, row_x, row_w, buffer = state
        n_row = len(row_x)
        operands += list(col_w) + list(row_x) + list(row_w) + [buffer]
        scratch += [
            pltpu.VMEM((col_blocks,) + block, jnp.float32),
            pltpu.VMEM((2 * half,) + block, jnp.float32),
            pltpu.VMEM((2 * half,) + block, jnp.float32),
        ]
        copies = 2 * len(col_x) + 2 * n_row
    in_specs = [any_spec] * len(operands) + [slots]
    aliases = {len(operands): 0} if update else {}
    outs, out_specs = [], []
    if update:
        outs.append(jax.ShapeDtypeStruct(omega.shape, jnp.float32))
        out_specs.append(slots)
    if products:
        outs += [jax.ShapeDtypeStruct((half,) + block, jnp.float32)] * 2
        out_specs += [any_spec] * 2
        scratch.append(pltpu.VMEM((2 * half + 1,) + block, jnp.float32))
    scratch.append(pltpu.SemaphoreType.DMA((copies,)))
    if products:
        scratch.append(pltpu.SemaphoreType.DMA((2,)))
    plan = (update, products, 0.5 / count, size, slab, len(col_x), n_row, choices)
    return pl.pallas_call(
        functools.partial(off_kernel, plan),
        grid_spec=pltpu.PrefetchScalarGridSpec(
            num_scalar_prefetch=1,
            grid=(off // size,),
            in_specs=in_specs,
            out_specs=out_specs,
            scratch_shapes=scratch,
        ),
        out_shape=outs,
        input_output_aliases=aliases,
        compiler_params=params(),
        cost_estimate=cost(off, block, 3 * (2 * update + products), 2 * half * count * width * 4),
        name="off_update" if update else "off_products",
    )(scalars, *operands, omega)


def gather_columns(v):
    rows = lax.axis_size("row")
    if rows == 4:
        flip = lambda part, bit: lax.ppermute(part, "row", [(i, i ^ bit) for i in range(rows)])
        middle = v.shape[0] // 2
        first, second = flip(v, 1), flip(v, 2)
        return [v, first, second, flip(first[:middle], 2), flip(second[middle:], 1)]
    shift = lambda d: lax.ppermute(v, "row", [((i + d) % rows, i) for i in range(rows)])
    return [v] + [shift(d) for d in range(1, rows)]


def column_place(group, own, rows):
    return group ^ own if rows == 4 else (group - own) % rows


def swap_cores(v):
    return lax.ppermute(v, "col", [(i, i ^ 1) for i in range(lax.axis_size("col"))])


def pass_on(v, up, sources):
    move = CORES if up else -CORES
    return lax.ppermute(v, "col", [(z * CORES + c, z * CORES + c + move) for z in sources for c in range(CORES)])


def gather_rows(v, chips):
    ups, downs = [], []
    up = down = v
    for hop in range(1, chips):
        up = pass_on(up, True, range(hop - 1, chips - 1))
        down = pass_on(down, False, range(1, chips - hop + 1))
        ups.append(up)
        downs.append(down)
    return ups, downs


def row_parts(v, chips, half):
    slab = v.shape[0]
    ups, downs = gather_rows(v, chips)
    parts, choices = [], []
    for side in range(CORES):
        mine = side == 0
        parts.append(v if mine else swap_cores(v))
        choices.append((side * half, None))
        for distance in range(1, chips):
            down, up = downs[distance - 1], ups[distance - 1]
            at = side * half + slab + (distance - 1) * slab
            parts.append(down if mine else swap_cores(down))
            choices.append((at, (chips - distance, True)))
            at = side * half + slab + (chips - distance - 1) * slab
            parts.append(up if mine else swap_cores(up))
            choices.append((at, (distance, False)))
    return parts, tuple(choices)


def scatter_rows(mine, other, slab, chips):
    def part(relative):
        at = slab + (relative - 1) * slab
        return mine[at : at + slab] + other[at : at + slab]

    up = down = None
    for distance in range(chips - 1, 0, -1):
        next_up, next_down = part(distance), part(chips - distance)
        if up is not None:
            next_up, next_down = next_up + up, next_down + down
        up = pass_on(next_up, True, range(0, chips - distance))
        down = pass_on(next_down, False, range(distance, chips))
    return mine[:slab] + other[:slab] + up + down


def shards(samples, omega, block_rows, block_cols):
    n_row, n_col = lax.axis_size("row"), lax.axis_size("col")
    a, b = lax.axis_index("row"), lax.axis_index("col")
    slab = samples.shape[0]
    chips = n_col // CORES
    chip, core = b // CORES, b % CORES
    half = slab * chips
    blocks = omega[0, 0]
    rows = block_rows[0, 0, slab:]
    cols = block_cols[0, 0, slab:]
    live = rows >= 0
    local = rows - a * (slab * n_col)
    owner, inner = local // slab, local % slab
    side = (owner % CORES) ^ core
    relative = (owner // CORES - chip) % chips
    place = jnp.where(live, side * half + relative * slab + inner, 0)
    target = jnp.where(live, place, CORES * half)
    group = column_place(cols // slab // n_col, a, n_row)
    column = jnp.where(live, group * slab + cols % slab, 0)
    scalars = jnp.stack(
        [target, column, place, jnp.full_like(place, chip), live.astype(jnp.int32)]
    ).astype(jnp.int32)

    col_x = gather_columns(samples)
    row_x, choices = row_parts(samples, chips, half)
    p_diag = diag_products(samples, blocks)
    p_mine, p_other = off_slots(scalars, col_x, blocks, slab, half, choices)
    for iteration in range(ITERS):
        last = iteration == ITERS - 1
        own_w = scatter_rows(p_mine, swap_cores(p_other), slab, chips) + p_diag
        col_w = gather_columns(own_w)
        row_w, _ = row_parts(own_w, chips, half)
        if last:
            (buffer,) = diag_update(samples, own_w, blocks, last)
        else:
            buffer, p_diag = diag_update(samples, own_w, blocks, last)
        result = off_slots(
            scalars, col_x, blocks, slab, half, choices, (col_w, row_x, row_w, buffer), not last
        )
        if last:
            blocks = result[0]
        else:
            blocks, p_mine, p_other = result
    return blocks[None, None]


def solution(mesh):
    return jax.shard_map(
        shards,
        mesh=mesh,
        in_specs=(
            P(("row", "col"), None, None),
            P("row", "col", None, None, None),
            P("row", "col", None),
            P("row", "col", None),
        ),
        out_specs=P("row", "col", None, None, None),
        check_vma=False,
    )
```

time: 784 us -> 598 us (0.76); the launches traced: 774 us -> 597 us
  matrix products: 145 us -> 0 us
  waiting for transfers between devices: 507 us -> 404 us
  local copies, waits for them, and re-layouts: 96.3 us -> 5.13 us
  starting transfers between devices: 11.3 us -> 100 us
  Pallas kernels: 0 us -> 74.1 us
  between operations: 13.8 us -> 0.99 us
  other arithmetic: 1.4 us -> 13 us
    ppermute x0 -> x65, waiting for transfers between devices: none -> 404 us  [the longest x30 339 us: pass_on(): lax.ppermute(v, 'col', [(z * CORES + c, z * CORES + c + move) for z in so...]
    psum x2 -> x0, waiting for transfers between devices: 351 us -> none  [shards(): lax.psum(summed_part.reshape(group_rows, sample_count, width), 'col')]
    all_gather x4 -> x0, waiting for transfers between devices: 155 us -> none  [the longest x2 64.1 us: shards(): col_totals = lax.all_gather(own_totals, 'row', axis=0, tiled=True)]
    dot_general x8 -> x0, matrix products: 145 us -> none  [the longest x2 55.5 us: gradient_blocks(): jnp.einsum('snb,snk->sbk', left_samples, right_totals, precision=lax.Prec...]
    ppermute x0 -> x65, starting transfers between devices: none -> 100 us  [the longest x30 79.7 us: pass_on(): lax.ppermute(v, 'col', [(z * CORES + c, z * CORES + c + move) for z in so...]
    pallas_call x0 -> x6, Pallas kernels: none -> 74.1 us  [the longest x3 58.8 us: off_slots(): pl.pallas_call(functools.partial(off_kernel, plan), grid_spec=pltpu.Prefe...]
    gather x6 -> x0, local copies, waits for them, and re-layouts: 33.5 us -> none  [the longest x2 12.4 us: shards(): row_totals[safe_rows]]
    psum x2 -> x0, local copies, waits for them, and re-layouts: 23.1 us -> none  [shards(): lax.psum(summed_part.reshape(group_rows, sample_count, width), 'col')]
  transfers between devices with their start and end apart: 6 -> 65, of which waited for: 6 -> 30; matrix products, arithmetic and copies ran while one was open for 10% -> 1% of each run, Pallas kernels for 0% -> 3%
where the time goes in v1:
time: 598 us; the launch traced here: 597 us
  waiting for transfers between devices  404 us (68%)
  starting transfers between devices  100 us (17%)
  Pallas kernels  74.1 us (12%)
  other arithmetic  13 us (2%)
    ppermute x30, waiting for transfers between devices, pass_on(): lax.ppermute(v, 'col', [(z * CORES + c, z * CORES + c + move) for z in so...  339 us
    ppermute x30, starting transfers between devices, pass_on(): lax.ppermute(v, 'col', [(z * CORES + c, z * CORES + c + move) for z in so...  79.7 us
    pallas_call x3, Pallas kernels, off_slots(): pl.pallas_call(functools.partial(off_kernel, plan), grid_spec=pltpu.Prefe...  58.8 us
    ppermute x12, waiting for transfers between devices, gather_columns(): lax.ppermute(part, 'row', [(i, i ^ bit) for i in range(rows)])  50.2 us
    ppermute x12, starting transfers between devices, gather_columns(): lax.ppermute(part, 'row', [(i, i ^ bit) for i in range(rows)])  16.4 us
    ppermute x23, waiting for transfers between devices, swap_cores(): lax.ppermute(v, 'col', [(i, i ^ 1) for i in range(lax.axis_size('col'))])  14.4 us
  transfers between devices with their start and end apart: 65, of which 30 were waited for; matrix products, arithmetic and copies ran while one was open for 1% of the time, Pallas kernels for 3%

profile of v1, /device:TPU:0, one launch (start us, length us, event | category | flops | bytes accessed | tf_op | source)
XLA Modules:
  0.0 597.0 jit_solution(3163205725901931803)
XLA Ops:
  4.5 21.9 %collective-permute-done.1.refs_2_ = f32[32,64,128]{2,1,0:T(8,128)S(1)} collective-permute-done((f32[32,64,128]{2,1,0:T(8,128)}, f32[32,64,128]{2,1,0:T(8,128)S(1)}, u32[]{:S(2)}, u32[]{:S(2)}) %collective-permute-start.1) | collective-permute-done | bytes 1048608 | tf_op jit(solution)/shard_map/ppermute | solution.py:279
  33.5 7.0 %collective-permute-done.3.refs_4_ = f32[16,64,128]{2,1,0:T(8,128)S(1)} collective-permute-done((f32[16,64,128]{2,1,0:T(8,128)}, f32[16,64,128]{2,1,0:T(8,128)S(1)}, u32[]{:S(2)}, u32[]{:S(2)}) %collective-permute-start.3) | collective-permute-done | bytes 524320 | tf_op jit(solution)/shard_map/ppermute | solution.py:279
  43.4 13.4 %off_products.1 = (f32[128,64,128]{2,1,0:T(8,128)}, f32[128,64,128]{2,1,0:T(8,128)}) custom-call(s32[5,96]{1,0:T(8,128)} %stack.2.scalars, f32[32,64,128]{2,1,0:T(8,128)} %refs_10_.3, f32[32,64,128]{2,1,0:T(8,128)} %copy-done.4, f32[32,64,128]{2,1,0:T(8,128)} %copy-done.3, f32[16,64,128]{2,1,0:T(8,128)} %copy-done.9, f32[16,64,128]{2,1,0:T(8,128)} %copy-done.8, ...), custom_call_target="tpu_custom_call" | custom-call | flops 603979776 | bytes 33554432 | tf_op jit(solution)/shard_map/off_products/pallas_call | solution.py:259
  56.9 7.4 %collective-permute-done.4 = f32[128,64,128]{2,1,0:T(8,128)S(1)} collective-permute-done((f32[128,64,128]{2,1,0:T(8,128)}, f32[128,64,128]{2,1,0:T(8,128)S(1)}, u32[]{:S(2)}, u32[]{:S(2)}) %collective-permute-start.4) | collective-permute-done | bytes 4194336 | tf_op jit(solution)/shard_map/ppermute | solution.py:292
  70.1 22.6 %collective-permute-done.5 = f32[32,64,128]{2,1,0:T(8,128)S(1)} collective-permute-done((f32[32,64,128]{2,1,0:T(8,128)S(1)}, f32[32,64,128]{2,1,0:T(8,128)S(1)}, u32[]{:S(2)}, u32[]{:S(2)}) %collective-permute-start.5) | collective-permute-done | bytes 1048608 | tf_op jit(solution)/shard_map/ppermute | solution.py:297
  94.3 4.5 collective-permute-start.6
  98.7 21.8 %collective-permute-done.6 = f32[32,64,128]{2,1,0:T(8,128)S(1)} collective-permute-done((f32[32,64,128]{2,1,0:T(8,128)S(1)}, f32[32,64,128]{2,1,0:T(8,128)S(1)}, u32[]{:S(2)}, u32[]{:S(2)}) %collective-permute-start.6) | collective-permute-done | bytes 1048608 | tf_op jit(solution)/shard_map/ppermute | solution.py:297
  121.6 4.5 collective-permute-start.16
  128.5 18.4 %collective-permute-done.16.refs_12_ = f32[32,64,128]{2,1,0:T(8,128)S(1)} collective-permute-done((f32[32,64,128]{2,1,0:T(8,128)S(1)}, f32[32,64,128]{2,1,0:T(8,128)S(1)}, u32[]{:S(2)}, u32[]{:S(2)}) %collective-permute-start.16) | collective-permute-done | bytes 1048608 | tf_op jit(solution)/shard_map/ppermute | solution.py:297
  152.4 8.4 %collective-permute-start.7 = (f32[32,64,128]{2,1,0:T(8,128)S(1)}, f32[32,64,128]{2,1,0:T(8,128)S(1)}, u32[]{:S(2)}, u32[]{:S(2)}) collective-permute-start(f32[32,64,128]{2,1,0:T(8,128)S(1)} %get-tuple-element.21), channel_id=1, source_target_pairs={{0,2},{1,3},{2,4},{3,5},{4,6},{5,7},{8,10},{9,11},{10,12},{11,13},... | collective-permute-start | bytes 3145736 | tf_op jit(solution)/shard_map/ppermute | solution.py:297
  162.9 20.0 %collective-permute-done.17.refs_13_ = f32[32,64,128]{2,1,0:T(8,128)} collective-permute-done((f32[32,64,128]{2,1,0:T(8,128)S(1)}, f32[32,64,128]{2,1,0:T(8,128)}, u32[]{:S(2)}, u32[]{:S(2)}) %collective-permute-start.17) | collective-permute-done | bytes 1048608 | tf_op jit(solution)/shard_map/ppermute | solution.py:297
  185.2 19.5 %collective-permute-done.10 = f32[32,64,128]{2,1,0:T(8,128)S(1)} collective-permute-done((f32[32,64,128]{2,1,0:T(8,128)S(1)}, f32[32,64,128]{2,1,0:T(8,128)S(1)}, u32[]{:S(2)}, u32[]{:S(2)}) %collective-permute-start.10) | collective-permute-done | bytes 1048608 | tf_op jit(solution)/shard_map/ppermute | solution.py:297
  213.6 17.6 %collective-permute-start.29 = (f32[32,64,128]{2,1,0:T(8,128)S(1)}, f32[32,64,128]{2,1,0:T(8,128)S(1)}, u32[]{:S(2)}, u32[]{:S(2)}) collective-permute-start(f32[32,64,128]{2,1,0:T(8,128)S(1)} %fusion.5.w_ref.refs_5_.refs_24_), channel_id=1, source_target_pairs={{0,2},{1,3},{2,4},{3,5},{4,6},{5,7},{8,10},{9,11},{10,12},{11,13},... | collective-permute-start | bytes 3145736 | tf_op jit(solution)/shard_map/ppermute | solution.py:297
  234.4 19.0 %collective-permute-done.19.refs_15_ = f32[32,64,128]{2,1,0:T(8,128)S(1)} collective-permute-done((f32[32,64,128]{2,1,0:T(8,128)}, f32[32,64,128]{2,1,0:T(8,128)S(1)}, u32[]{:S(2)}, u32[]{:S(2)}) %collective-permute-start.19) | collective-permute-done | bytes 1048608 | tf_op jit(solution)/shard_map/ppermute | solution.py:297
  255.9 19.9 %collective-permute-done.28.refs_25_ = f32[32,64,128]{2,1,0:T(8,128)} collective-permute-done((f32[32,64,128]{2,1,0:T(8,128)S(1)}, f32[32,64,128]{2,1,0:T(8,128)}, u32[]{:S(2)}, u32[]{:S(2)}) %collective-permute-start.28) | collective-permute-done | bytes 1048608 | tf_op jit(solution)/shard_map/ppermute | solution.py:297
  279.9 23.1 %collective-permute-done.30.refs_27_ = f32[32,64,128]{2,1,0:T(8,128)} collective-permute-done((f32[32,64,128]{2,1,0:T(8,128)}, f32[32,64,128]{2,1,0:T(8,128)}, u32[]{:S(2)}, u32[]{:S(2)}) %collective-permute-start.30) | collective-permute-done | bytes 1048608 | tf_op jit(solution)/shard_map/ppermute | solution.py:297
  306.7 10.8 %collective-permute-done.14.refs_9_ = f32[16,64,128]{2,1,0:T(8,128)S(1)} collective-permute-done((f32[16,64,128]{2,1,0:T(8,128)S(1)}, f32[16,64,128]{2,1,0:T(8,128)S(1)}, u32[]{:S(2)}, u32[]{:S(2)}) %collective-permute-start.14) | collective-permute-done | bytes 524320 | tf_op jit(solution)/shard_map/ppermute | solution.py:279
  319.3 10.0 %collective-permute-done.32.refs_29_ = f32[32,64,128]{2,1,0:T(8,128)} collective-permute-done((f32[32,64,128]{2,1,0:T(8,128)}, f32[32,64,128]{2,1,0:T(8,128)}, u32[]{:S(2)}, u32[]{:S(2)}) %collective-permute-start.32) | collective-permute-done | bytes 1048608 | tf_op jit(solution)/shard_map/ppermute | solution.py:297
  329.3 7.6 %diag_update.2 = (f32[128,128,128]{2,1,0:T(8,128)}, f32[32,64,128]{2,1,0:T(8,128)}) custom-call(f32[32,64,128]{2,1,0:T(8,128)} %refs_10_.3, f32[32,64,128]{2,1,0:T(8,128)} %copy-done.2, f32[128,128,128]{2,1,0:T(8,128)} %bitcast.37), custom_call_target="tpu_custom_call" | custom-call | flops 603979776 | bytes 8388608 | tf_op jit(solution)/shard_map/diag_update/pallas_call | solution.py:119
  337.0 27.9 %off_update.2 = (f32[128,128,128]{2,1,0:T(8,128)}, f32[128,64,128]{2,1,0:T(8,128)}, f32[128,64,128]{2,1,0:T(8,128)}) custom-call(s32[5,96]{1,0:T(8,128)} %stack.2.scalars, f32[32,64,128]{2,1,0:T(8,128)} %refs_10_.3, f32[32,64,128]{2,1,0:T(8,128)} %copy-done.4, f32[32,64,128]{2,1,0:T(8,128)} %copy-done.3, ...), custom_call_target="tpu_custom_call", output_to_operand_aliasing={{0}: (39, {})} | custom-call | flops 1811939328 | bytes 33554432 | tf_op jit(solution)/shard_map/off_update/pallas_call | solution.py:259
  365.4 7.0 %collective-permute-done.41 = f32[128,64,128]{2,1,0:T(8,128)S(1)} collective-permute-done((f32[128,64,128]{2,1,0:T(8,128)}, f32[128,64,128]{2,1,0:T(8,128)S(1)}, u32[]{:S(2)}, u32[]{:S(2)}) %collective-permute-start.41) | collective-permute-done | bytes 4194336 | tf_op jit(solution)/shard_map/ppermute | solution.py:292
  375.4 23.0 %collective-permute-done.42 = f32[32,64,128]{2,1,0:T(8,128)S(1)} collective-permute-done((f32[32,64,128]{2,1,0:T(8,128)S(1)}, f32[32,64,128]{2,1,0:T(8,128)S(1)}, u32[]{:S(2)}, u32[]{:S(2)}) %collective-permute-start.42) | collective-permute-done | bytes 1048608 | tf_op jit(solution)/shard_map/ppermute | solution.py:297
  399.8 4.5 collective-permute-start.43
  404.3 22.2 %collective-permute-done.43 = f32[32,64,128]{2,1,0:T(8,128)S(1)} collective-permute-done((f32[32,64,128]{2,1,0:T(8,128)S(1)}, f32[32,64,128]{2,1,0:T(8,128)S(1)}, u32[]{:S(2)}, u32[]{:S(2)}) %collective-permute-start.43) | collective-permute-done | bytes 1048608 | tf_op jit(solution)/shard_map/ppermute | solution.py:297
  428.8 5.0 collective-permute-start.44
  435.3 19.8 %collective-permute-done.44 = f32[32,64,128]{2,1,0:T(8,128)S(1)} collective-permute-done((f32[32,64,128]{2,1,0:T(8,128)S(1)}, f32[32,64,128]{2,1,0:T(8,128)S(1)}, u32[]{:S(2)}, u32[]{:S(2)}) %collective-permute-start.44) | collective-permute-done | bytes 1048608 | tf_op jit(solution)/shard_map/ppermute | solution.py:297
  455.1 47.4 %collective-permute-done.47 = f32[32,64,128]{2,1,0:T(8,128)S(1)} collective-permute-done((f32[32,64,128]{2,1,0:T(8,128)S(1)}, f32[32,64,128]{2,1,0:T(8,128)S(1)}, u32[]{:S(2)}, u32[]{:S(2)}) %collective-permute-start.47) | collective-permute-done | bytes 1048608 | tf_op jit(solution)/shard_map/ppermute | solution.py:297
  509.7 16.2 %collective-permute-done.53.refs_26_ = f32[32,64,128]{2,1,0:T(8,128)S(1)} collective-permute-done((f32[32,64,128]{2,1,0:T(8,128)S(1)}, f32[32,64,128]{2,1,0:T(8,128)S(1)}, u32[]{:S(2)}, u32[]{:S(2)}) %collective-permute-start.53) | collective-permute-done | bytes 1048608 | tf_op jit(solution)/shard_map/ppermute | solution.py:297
  534.2 19.3 %collective-permute-done.54.refs_27_ = f32[32,64,128]{2,1,0:T(8,128)S(1)} collective-permute-done((f32[32,64,128]{2,1,0:T(8,128)S(1)}, f32[32,64,128]{2,1,0:T(8,128)S(1)}, u32[]{:S(2)}, u32[]{:S(2)}) %collective-permute-start.54) | collective-permute-done | bytes 1048608 | tf_op jit(solution)/shard_map/ppermute | solution.py:297
  557.1 6.9 %collective-permute-done.51.refs_9_ = f32[16,64,128]{2,1,0:T(8,128)S(1)} collective-permute-done((f32[16,64,128]{2,1,0:T(8,128)S(1)}, f32[16,64,128]{2,1,0:T(8,128)S(1)}, u32[]{:S(2)}, u32[]{:S(2)}) %collective-permute-start.51) | collective-permute-done | bytes 524320 | tf_op jit(solution)/shard_map/ppermute | solution.py:279
  565.3 9.8 %collective-permute-done.56.refs_29_ = f32[32,64,128]{2,1,0:T(8,128)} collective-permute-done((f32[32,64,128]{2,1,0:T(8,128)S(1)}, f32[32,64,128]{2,1,0:T(8,128)}, u32[]{:S(2)}, u32[]{:S(2)}) %collective-permute-start.56) | collective-permute-done | bytes 1048608 | tf_op jit(solution)/shard_map/ppermute | solution.py:297
  579.3 17.5 %off_update.3 = f32[128,128,128]{2,1,0:T(8,128)} custom-call(s32[5,96]{1,0:T(8,128)} %stack.2.scalars, f32[32,64,128]{2,1,0:T(8,128)} %refs_10_.3, f32[32,64,128]{2,1,0:T(8,128)} %copy-done.4, f32[32,64,128]{2,1,0:T(8,128)} %copy-done.3, f32[16,64,128]{2,1,0:T(8,128)} %copy-done.9, f32[16,64,128]{2,1,0:T(8,128)} %copy-done.8, ...), custom_call_target="tpu_custom_call", output_to_operand_aliasing={{}: (39, {})} | custom-call | flops 1207959552 | bytes 33554432 | tf_op jit(solution)/shard_map/off_update/pallas_call | solution.py:259
  (198 shorter events, 92.3 us)
Async XLA Ops:
  0.0 26.3 %collective-permute-start.1 = (f32[32,64,128]{2,1,0:T(8,128)}, f32[32,64,128]{2,1,0:T(8,128)S(1)}, u32[]{:S(2)}, u32[]{:S(2)}) collective-permute-start(f32[32,64,128]{2,1,0:T(8,128)} %refs_10_.3), channel_id=1, source_target_pairs={{0,16},{8,24},{16,0},{24,8},{1,17},{9,25},{17,1},{25,9},{2,18},{10... | collective-permute-start | bytes 3145736 | tf_op jit(solution)/shard_map/ppermute | solution.py:279
  3.0 26.0 %collective-permute-start = (f32[32,64,128]{2,1,0:T(8,128)}, f32[32,64,128]{2,1,0:T(8,128)S(1)}, u32[]{:S(2)}, u32[]{:S(2)}) collective-permute-start(f32[32,64,128]{2,1,0:T(8,128)} %refs_10_.3), channel_id=1, source_target_pairs={{0,8},{8,0},{16,24},{24,16},{1,9},{9,1},{17,25},{25,17},{2,10},{10... | collective-permute-start | bytes 3145736 | tf_op jit(solution)/shard_map/ppermute | solution.py:279
  66.4 26.3 %collective-permute-start.5 = (f32[32,64,128]{2,1,0:T(8,128)S(1)}, f32[32,64,128]{2,1,0:T(8,128)S(1)}, u32[]{:S(2)}, u32[]{:S(2)}) collective-permute-start(f32[32,64,128]{2,1,0:T(8,128)S(1)} %slice_add_fusion.4), channel_id=1, source_target_pairs={{0,2},{1,3},{8,10},{9,11},{16,18},{17,19},{24,26},{25,27}} | collective-permute-start | bytes 3145736 | tf_op jit(solution)/shard_map/ppermute | solution.py:297
  94.3 26.3 %collective-permute-start.6 = (f32[32,64,128]{2,1,0:T(8,128)S(1)}, f32[32,64,128]{2,1,0:T(8,128)S(1)}, u32[]{:S(2)}, u32[]{:S(2)}) collective-permute-start(f32[32,64,128]{2,1,0:T(8,128)S(1)} %fusion.7), channel_id=1, source_target_pairs={{0,2},{1,3},{2,4},{3,5},{8,10},{9,11},{10,12},{11,13},{16,18},{17,... | collective-permute-start | bytes 3145736 | tf_op jit(solution)/shard_map/ppermute | solution.py:297
  121.6 25.3 %collective-permute-start.16 = (f32[32,64,128]{2,1,0:T(8,128)S(1)}, f32[32,64,128]{2,1,0:T(8,128)S(1)}, u32[]{:S(2)}, u32[]{:S(2)}) collective-permute-start(f32[32,64,128]{2,1,0:T(8,128)S(1)} %copy-done), channel_id=1, source_target_pairs={{0,2},{1,3},{2,4},{3,5},{4,6},{5,7},{8,10},{9,11},{10,12},{11,13},... | collective-permute-start | bytes 3145736 | tf_op jit(solution)/shard_map/ppermute | solution.py:297
  126.1 25.1 %collective-permute-start.15 = (f32[32,64,128]{2,1,0:T(8,128)S(1)}, f32[32,64,128]{2,1,0:T(8,128)S(1)}, u32[]{:S(2)}, u32[]{:S(2)}) collective-permute-start(f32[32,64,128]{2,1,0:T(8,128)S(1)} %copy-done), channel_id=1, source_target_pairs={{2,0},{3,1},{4,2},{5,3},{6,4},{7,5},{10,8},{11,9},{12,10},{13,11},... | collective-permute-start | bytes 3145736 | tf_op jit(solution)/shard_map/ppermute | solution.py:297
  127.7 33.1 %collective-permute-start.9 = (f32[32,64,128]{2,1,0:T(8,128)S(1)}, f32[32,64,128]{2,1,0:T(8,128)S(1)}, u32[]{:S(2)}, u32[]{:S(2)}) collective-permute-start(f32[32,64,128]{2,1,0:T(8,128)S(1)} %fusion.6), channel_id=1, source_target_pairs={{4,2},{5,3},{6,4},{7,5},{12,10},{13,11},{14,12},{15,13},{20,18},{2... | collective-permute-start | bytes 3145736 | tf_op jit(solution)/shard_map/ppermute | solution.py:297
  128.4 33.8 %collective-permute-start.21 = (f32[32,64,128]{2,1,0:T(8,128)S(1)}, f32[32,64,128]{2,1,0:T(8,128)S(1)}, u32[]{:S(2)}, u32[]{:S(2)}) collective-permute-start(f32[32,64,128]{2,1,0:T(8,128)S(1)} %copy-done), channel_id=1, source_target_pairs={{0,1},{1,0},{2,3},{3,2},{4,5},{5,4},{6,7},{7,6},{8,9},{9,8},{10,11... | collective-permute-start | bytes 3145736 | tf_op jit(solution)/shard_map/ppermute | solution.py:292
  151.1 31.7 %collective-permute-start.17 = (f32[32,64,128]{2,1,0:T(8,128)S(1)}, f32[32,64,128]{2,1,0:T(8,128)}, u32[]{:S(2)}, u32[]{:S(2)}) collective-permute-start(f32[32,64,128]{2,1,0:T(8,128)S(1)} %collective-permute-done.15.refs_11_), channel_id=1, source_target_pairs={{2,0},{3,1},{4,2},{5,3},{10,8},{11,9},{12,10},{13,11},{18,16},{19,... | collective-permute-start | bytes 3145736 | tf_op jit(solution)/shard_map/ppermute | solution.py:297
  152.4 31.1 %collective-permute-start.7 = (f32[32,64,128]{2,1,0:T(8,128)S(1)}, f32[32,64,128]{2,1,0:T(8,128)S(1)}, u32[]{:S(2)}, u32[]{:S(2)}) collective-permute-start(f32[32,64,128]{2,1,0:T(8,128)S(1)} %get-tuple-element.21), channel_id=1, source_target_pairs={{0,2},{1,3},{2,4},{3,5},{4,6},{5,7},{8,10},{9,11},{10,12},{11,13},... | collective-permute-start | bytes 3145736 | tf_op jit(solution)/shard_map/ppermute | solution.py:297
  161.0 43.8 %collective-permute-start.10 = (f32[32,64,128]{2,1,0:T(8,128)S(1)}, f32[32,64,128]{2,1,0:T(8,128)S(1)}, u32[]{:S(2)}, u32[]{:S(2)}) collective-permute-start(f32[32,64,128]{2,1,0:T(8,128)S(1)} %add.229), channel_id=1, source_target_pairs={{2,0},{3,1},{4,2},{5,3},{6,4},{7,5},{10,8},{11,9},{12,10},{13,11},... | collective-permute-start | bytes 3145736 | tf_op jit(solution)/shard_map/ppermute | solution.py:297
  162.3 50.0 %collective-permute-start.23 = (f32[32,64,128]{2,1,0:T(8,128)S(1)}, f32[32,64,128]{2,1,0:T(8,128)}, u32[]{:S(2)}, u32[]{:S(2)}) collective-permute-start(f32[32,64,128]{2,1,0:T(8,128)S(1)} %collective-permute-done.16.refs_12_), channel_id=1, source_target_pairs={{0,1},{1,0},{2,3},{3,2},{4,5},{5,4},{6,7},{7,6},{8,9},{9,8},{10,11... | collective-permute-start | bytes 3145736 | tf_op jit(solution)/shard_map/ppermute | solution.py:292
  162.4 51.2 %collective-permute-start.22 = (f32[32,64,128]{2,1,0:T(8,128)S(1)}, f32[32,64,128]{2,1,0:T(8,128)}, u32[]{:S(2)}, u32[]{:S(2)}) collective-permute-start(f32[32,64,128]{2,1,0:T(8,128)S(1)} %collective-permute-done.15.refs_11_), channel_id=1, source_target_pairs={{0,1},{1,0},{2,3},{3,2},{4,5},{5,4},{6,7},{7,6},{8,9},{9,8},{10,11... | collective-permute-start | bytes 3145736 | tf_op jit(solution)/shard_map/ppermute | solution.py:292
  182.8 48.4 %collective-permute-start.25 = (f32[32,64,128]{2,1,0:T(8,128)}, f32[32,64,128]{2,1,0:T(8,128)}, u32[]{:S(2)}, u32[]{:S(2)}) collective-permute-start(f32[32,64,128]{2,1,0:T(8,128)} %collective-permute-done.18.refs_14_), channel_id=1, source_target_pairs={{0,1},{1,0},{2,3},{3,2},{4,5},{5,4},{6,7},{7,6},{8,9},{9,8},{10,11... | collective-permute-start | bytes 3145736 | tf_op jit(solution)/shard_map/ppermute | solution.py:292
  183.5 49.1 %collective-permute-start.20 = (f32[32,64,128]{2,1,0:T(8,128)}, f32[32,64,128]{2,1,0:T(8,128)}, u32[]{:S(2)}, u32[]{:S(2)}) collective-permute-start(f32[32,64,128]{2,1,0:T(8,128)} %collective-permute-done.18.refs_14_), channel_id=1, source_target_pairs={{4,6},{5,7},{12,14},{13,15},{20,22},{21,23},{28,30},{29,31}} | collective-permute-start | bytes 3145736 | tf_op jit(solution)/shard_map/ppermute | solution.py:297
  205.8 27.1 %collective-permute-start.24 = (f32[32,64,128]{2,1,0:T(8,128)}, f32[32,64,128]{2,1,0:T(8,128)}, u32[]{:S(2)}, u32[]{:S(2)}) collective-permute-start(f32[32,64,128]{2,1,0:T(8,128)} %collective-permute-done.17.refs_13_), channel_id=1, source_target_pairs={{0,1},{1,0},{2,3},{3,2},{4,5},{5,4},{6,7},{7,6},{8,9},{9,8},{10,11... | collective-permute-start | bytes 3145736 | tf_op jit(solution)/shard_map/ppermute | solution.py:292
  212.3 41.1 %collective-permute-start.19 = (f32[32,64,128]{2,1,0:T(8,128)}, f32[32,64,128]{2,1,0:T(8,128)S(1)}, u32[]{:S(2)}, u32[]{:S(2)}) collective-permute-start(f32[32,64,128]{2,1,0:T(8,128)} %collective-permute-done.17.refs_13_), channel_id=1, source_target_pairs={{2,0},{3,1},{10,8},{11,9},{18,16},{19,17},{26,24},{27,25}} | collective-permute-start | bytes 3145736 | tf_op jit(solution)/shard_map/ppermute | solution.py:297
  213.6 40.6 %collective-permute-start.29 = (f32[32,64,128]{2,1,0:T(8,128)S(1)}, f32[32,64,128]{2,1,0:T(8,128)S(1)}, u32[]{:S(2)}, u32[]{:S(2)}) collective-permute-start(f32[32,64,128]{2,1,0:T(8,128)S(1)} %fusion.5.w_ref.refs_5_.refs_24_), channel_id=1, source_target_pairs={{0,2},{1,3},{2,4},{3,5},{4,6},{5,7},{8,10},{9,11},{10,12},{11,13},... | collective-permute-start | bytes 3145736 | tf_op jit(solution)/shard_map/ppermute | solution.py:297
  231.2 44.5 %collective-permute-start.28 = (f32[32,64,128]{2,1,0:T(8,128)S(1)}, f32[32,64,128]{2,1,0:T(8,128)}, u32[]{:S(2)}, u32[]{:S(2)}) collective-permute-start(f32[32,64,128]{2,1,0:T(8,128)S(1)} %fusion.5.w_ref.refs_5_.refs_24_), channel_id=1, source_target_pairs={{2,0},{3,1},{4,2},{5,3},{6,4},{7,5},{10,8},{11,9},{12,10},{13,11},... | collective-permute-start | bytes 3145736 | tf_op jit(solution)/shard_map/ppermute | solution.py:297
  232.5 44.5 %collective-permute-start.27 = (f32[32,64,128]{2,1,0:T(8,128)}, f32[32,64,128]{2,1,0:T(8,128)S(1)}, u32[]{:S(2)}, u32[]{:S(2)}) collective-permute-start(f32[32,64,128]{2,1,0:T(8,128)} %collective-permute-done.20.refs_16_), channel_id=1, source_target_pairs={{0,1},{1,0},{2,3},{3,2},{4,5},{5,4},{6,7},{7,6},{8,9},{9,8},{10,11... | collective-permute-start | bytes 3145736 | tf_op jit(solution)/shard_map/ppermute | solution.py:292
  232.8 44.3 %collective-permute-start.12 = (f32[32,64,128]{2,1,0:T(8,128)S(1)}, f32[32,64,128]{2,1,0:T(8,128)S(1)}, u32[]{:S(2)}, u32[]{:S(2)}) collective-permute-start(f32[32,64,128]{2,1,0:T(8,128)S(1)} %fusion.5.w_ref.refs_5_.refs_24_), channel_id=1, source_target_pairs={{0,16},{8,24},{16,0},{24,8},{1,17},{9,25},{17,1},{25,9},{2,18},{10... | collective-permute-start | bytes 3145736 | tf_op jit(solution)/shard_map/ppermute | solution.py:279
  275.8 27.2 %collective-permute-start.30 = (f32[32,64,128]{2,1,0:T(8,128)}, f32[32,64,128]{2,1,0:T(8,128)}, u32[]{:S(2)}, u32[]{:S(2)}) collective-permute-start(f32[32,64,128]{2,1,0:T(8,128)} %collective-permute-done.28.refs_25_), channel_id=1, source_target_pairs={{2,0},{3,1},{4,2},{5,3},{10,8},{11,9},{12,10},{13,11},{18,16},{19,... | collective-permute-start | bytes 3145736 | tf_op jit(solution)/shard_map/ppermute | solution.py:297
  277.1 27.4 %collective-permute-start.26 = (f32[32,64,128]{2,1,0:T(8,128)S(1)}, f32[32,64,128]{2,1,0:T(8,128)S(1)}, u32[]{:S(2)}, u32[]{:S(2)}) collective-permute-start(f32[32,64,128]{2,1,0:T(8,128)S(1)} %collective-permute-done.19.refs_15_), channel_id=1, source_target_pairs={{0,1},{1,0},{2,3},{3,2},{4,5},{5,4},{6,7},{7,6},{8,9},{9,8},{10,11... | collective-permute-start | bytes 3145736 | tf_op jit(solution)/shard_map/ppermute | solution.py:292
  277.2 28.0 %collective-permute-start.34 = (f32[32,64,128]{2,1,0:T(8,128)S(1)}, f32[32,64,128]{2,1,0:T(8,128)S(1)}, u32[]{:S(2)}, u32[]{:S(2)}) collective-permute-start(f32[32,64,128]{2,1,0:T(8,128)S(1)} %fusion.5.w_ref.refs_5_.refs_24_), channel_id=1, source_target_pairs={{0,1},{1,0},{2,3},{3,2},{4,5},{5,4},{6,7},{7,6},{8,9},{9,8},{10,11... | collective-permute-start | bytes 3145736 | tf_op jit(solution)/shard_map/ppermute | solution.py:292
  278.2 39.8 %collective-permute-start.36 = (f32[32,64,128]{2,1,0:T(8,128)S(1)}, f32[32,64,128]{2,1,0:T(8,128)S(1)}, u32[]{:S(2)}, u32[]{:S(2)}) collective-permute-start(f32[32,64,128]{2,1,0:T(8,128)S(1)} %collective-permute-done.29.refs_26_), channel_id=1, source_target_pairs={{0,1},{1,0},{2,3},{3,2},{4,5},{5,4},{6,7},{7,6},{8,9},{9,8},{10,11... | collective-permute-start | bytes 3145736 | tf_op jit(solution)/shard_map/ppermute | solution.py:292
  278.2 40.8 %collective-permute-start.33 = (f32[32,64,128]{2,1,0:T(8,128)}, f32[32,64,128]{2,1,0:T(8,128)}, u32[]{:S(2)}, u32[]{:S(2)}) collective-permute-start(f32[32,64,128]{2,1,0:T(8,128)} %collective-permute-done.31.refs_28_), channel_id=1, source_target_pairs={{4,6},{5,7},{12,14},{13,15},{20,22},{21,23},{28,30},{29,31}} | collective-permute-start | bytes 3145736 | tf_op jit(solution)/shard_map/ppermute | solution.py:297
  303.0 26.3 %collective-permute-start.32 = (f32[32,64,128]{2,1,0:T(8,128)}, f32[32,64,128]{2,1,0:T(8,128)}, u32[]{:S(2)}, u32[]{:S(2)}) collective-permute-start(f32[32,64,128]{2,1,0:T(8,128)} %collective-permute-done.30.refs_27_), channel_id=1, source_target_pairs={{2,0},{3,1},{10,8},{11,9},{18,16},{19,17},{26,24},{27,25}} | collective-permute-start | bytes 3145736 | tf_op jit(solution)/shard_map/ppermute | solution.py:297
  399.8 26.6 %collective-permute-start.43 = (f32[32,64,128]{2,1,0:T(8,128)S(1)}, f32[32,64,128]{2,1,0:T(8,128)S(1)}, u32[]{:S(2)}, u32[]{:S(2)}) collective-permute-start(f32[32,64,128]{2,1,0:T(8,128)S(1)} %fusion.9), channel_id=1, source_target_pairs={{0,2},{1,3},{2,4},{3,5},{8,10},{9,11},{10,12},{11,13},{16,18},{17,... | collective-permute-start | bytes 3145736 | tf_op jit(solution)/shard_map/ppermute | solution.py:297
  428.8 26.3 %collective-permute-start.44 = (f32[32,64,128]{2,1,0:T(8,128)S(1)}, f32[32,64,128]{2,1,0:T(8,128)S(1)}, u32[]{:S(2)}, u32[]{:S(2)}) collective-permute-start(f32[32,64,128]{2,1,0:T(8,128)S(1)} %get-tuple-element.19), channel_id=1, source_target_pairs={{0,2},{1,3},{2,4},{3,5},{4,6},{5,7},{8,10},{9,11},{10,12},{11,13},... | collective-permute-start | bytes 3145736 | tf_op jit(solution)/shard_map/ppermute | solution.py:297
  434.0 68.5 %collective-permute-start.47 = (f32[32,64,128]{2,1,0:T(8,128)S(1)}, f32[32,64,128]{2,1,0:T(8,128)S(1)}, u32[]{:S(2)}, u32[]{:S(2)}) collective-permute-start(f32[32,64,128]{2,1,0:T(8,128)S(1)} %add.240), channel_id=1, source_target_pairs={{2,0},{3,1},{4,2},{5,3},{6,4},{7,5},{10,8},{11,9},{12,10},{13,11},... | collective-permute-start | bytes 3145736 | tf_op jit(solution)/shard_map/ppermute | solution.py:297
  532.0 32.7 %collective-permute-start.60 = (f32[32,64,128]{2,1,0:T(8,128)S(1)}, f32[32,64,128]{2,1,0:T(8,128)S(1)}, u32[]{:S(2)}, u32[]{:S(2)}) collective-permute-start(f32[32,64,128]{2,1,0:T(8,128)S(1)} %collective-permute-done.53.refs_26_), channel_id=1, source_target_pairs={{0,1},{1,0},{2,3},{3,2},{4,5},{5,4},{6,7},{7,6},{8,9},{9,8},{10,11... | collective-permute-start | bytes 3145736 | tf_op jit(solution)/shard_map/ppermute | solution.py:292
  532.5 32.7 %collective-permute-start.57 = (f32[32,64,128]{2,1,0:T(8,128)S(1)}, f32[32,64,128]{2,1,0:T(8,128)}, u32[]{:S(2)}, u32[]{:S(2)}) collective-permute-start(f32[32,64,128]{2,1,0:T(8,128)S(1)} %collective-permute-done.55.refs_28_), channel_id=1, source_target_pairs={{4,6},{5,7},{12,14},{13,15},{20,22},{21,23},{28,30},{29,31}} | collective-permute-start | bytes 3145736 | tf_op jit(solution)/shard_map/ppermute | solution.py:297
  (69 other events, 1919.7 us)

commit v2 on v1

--- a/solution.py
+++ b/solution.py
@@ -12,6 +12,7 @@
 PENALTY = 0.1
 VMEM_BYTES = 56 * 1024 * 1024
 CORES = 2
+TIERS = ((21, 18, 15), (23, 20, 17), (26, 23, 20), (1 << 30,))
 
 
 def split(x):
@@ -129,15 +130,15 @@
 
 
 def off_kernel(plan, scalars, *refs):
-    update, products, scale, size, slab, n_col, n_row, choices = plan
+    update, products, scale, size, n_col, x_choices, w_choices = plan
     steps = pl.num_programs(0)
     step = pl.program_id(0)
     refs = list(refs)
     take = lambda n: [refs.pop(0) for _ in range(n)]
     col_x_parts = take(n_col)
     col_w_parts = take(n_col) if update else []
-    row_x_parts = take(n_row) if update else []
-    row_w_parts = take(n_row) if update else []
+    row_x_parts = take(len(x_choices)) if update else []
+    row_w_parts = take(len(w_choices)) if update else []
     if update:
         take(1)
     (omega_ref,) = take(1)
@@ -161,7 +162,7 @@
             add(None, part, target.at[pl.ds(at, part.shape[0])])
             at += part.shape[0]
 
-    def rows(parts, target):
+    def rows(parts, choices, target):
         for part, (at, wanted) in zip(parts, choices):
             condition = None
             if wanted is not None:
@@ -172,8 +173,8 @@
     columns(col_x_parts, col_x)
     if update:
         columns(col_w_parts, col_w)
-        rows(row_x_parts, row_x)
-        rows(row_w_parts, row_w)
+        rows(row_x_parts, x_choices, row_x)
+        rows(row_w_parts, w_choices, row_w)
 
     def each(action):
         for condition, copy in copies:
@@ -196,8 +197,8 @@
         x = col_x[column]
         block = omega_ref[k]
         if update:
-            source = scalars[2, slot]
-            grad = gradient(row_w[source], x, row_x[source], col_w[column]) * scale
+            row_at, x_at = scalars[5, slot], scalars[2, slot]
+            grad = gradient(row_w[row_at], x, row_x[x_at], col_w[column]) * scale
             block = jnp.where(scalars[4, slot] > 0, shrink(block - STEP * grad), 0.0)
             out_refs[0][k] = block
         if products:
@@ -218,7 +219,7 @@
                 copy.wait()
 
 
-def off_slots(scalars, col_x, omega, slab, half, choices, state=None, products=True):
+def off_slots(scalars, col_x, omega, slab, half, state=None, products=True):
     update = state is not None
     cap, width = omega.shape[0], omega.shape[1]
     count = col_x[0].shape[1]
@@ -231,17 +232,17 @@
     operands = list(col_x)
     scratch = [pltpu.VMEM((col_blocks,) + block, jnp.float32)]
     copies = len(col_x)
-    n_row = 0
+    x_choices = w_choices = ()
     if update:
-        col_w, row_x, row_w, buffer = state
-        n_row = len(row_x)
+        col_w, (row_x, x_choices), (row_w, w_choices), buffer = state
         operands += list(col_w) + list(row_x) + list(row_w) + [buffer]
+        x_rows = max(at + part.shape[0] for part, (at, _) in zip(row_x, x_choices))
         scratch += [
             pltpu.VMEM((col_blocks,) + block, jnp.float32),
-            pltpu.VMEM((2 * half,) + block, jnp.float32),
-            pltpu.VMEM((2 * half,) + block, jnp.float32),
+            pltpu.VMEM((x_rows,) + block, jnp.float32),
+            pltpu.VMEM((CORES * half,) + block, jnp.float32),
         ]
-        copies = 2 * len(col_x) + 2 * n_row
+        copies = 2 * len(col_x) + len(row_x) + len(row_w)
     in_specs = [any_spec] * len(operands) + [slots]
     aliases = {len(operands): 0} if update else {}
     outs, out_specs = [], []
@@ -251,11 +252,11 @@
     if products:
         outs += [jax.ShapeDtypeStruct((half,) + block, jnp.float32)] * 2
         out_specs += [any_spec] * 2
-        scratch.append(pltpu.VMEM((2 * half + 1,) + block, jnp.float32))
+        scratch.append(pltpu.VMEM((CORES * half + 1,) + block, jnp.float32))
     scratch.append(pltpu.SemaphoreType.DMA((copies,)))
     if products:
         scratch.append(pltpu.SemaphoreType.DMA((2,)))
-    plan = (update, products, 0.5 / count, size, slab, len(col_x), n_row, choices)
+    plan = (update, products, 0.5 / count, size, len(col_x), x_choices, w_choices)
     return pl.pallas_call(
         functools.partial(off_kernel, plan),
         grid_spec=pltpu.PrefetchScalarGridSpec(
@@ -273,15 +274,63 @@
     )(scalars, *operands, omega)
 
 
-def gather_columns(v):
+def combine_kernel(places, mine_ref, other_ref, diag_ref, up_ref, down_ref, w_ref, up_out, down_out):
+    most = up_ref.shape[0]
+    for i in range(w_ref.shape[0]):
+        up_place, down_place = places[0, i], places[1, i]
+        w = mine_ref[i] + other_ref[i] + diag_ref[i]
+        came_up = jnp.where(down_place < most, up_ref[jnp.minimum(down_place, most - 1)], 0.0)
+        came_down = jnp.where(up_place < most, down_ref[jnp.minimum(up_place, most - 1)], 0.0)
+        w = w + (came_up + came_down)
+        w_ref[i] = w
+
+        @pl.when(up_place < most)
+        def _():
+            up_out[up_place] = w
+
+        @pl.when(down_place < most)
+        def _():
+            down_out[down_place] = w
+
+
+def combine(places, mine, other, diag, up, down):
+    slab, most, block = diag.shape[0], up.shape[0], diag.shape[1:]
+    whole = lambda n: pl.BlockSpec((n,) + block, lambda i, s: (0, 0, 0))
+    shape = lambda n: jax.ShapeDtypeStruct((n,) + block, jnp.float32)
+    return pl.pallas_call(
+        combine_kernel,
+        grid_spec=pltpu.PrefetchScalarGridSpec(
+            num_scalar_prefetch=1,
+            grid=(1,),
+            in_specs=[whole(slab)] * 3 + [whole(most)] * 2,
+            out_specs=[whole(slab), whole(most), whole(most)],
+        ),
+        out_shape=[shape(slab), shape(most), shape(most)],
+        compiler_params=params(),
+        name="combine",
+    )(places, mine, other, diag, up, down)
+
+
+def together(*values):
+    return lax.optimization_barrier(values)
+
+
+def flip_row(part, bit):
+    return lax.ppermute(part, "row", [(i, i ^ bit) for i in range(lax.axis_size("row"))])
+
+
+def columns_first(v):
     rows = lax.axis_size("row")
     if rows == 4:
-        flip = lambda part, bit: lax.ppermute(part, "row", [(i, i ^ bit) for i in range(rows)])
-        middle = v.shape[0] // 2
-        first, second = flip(v, 1), flip(v, 2)
-        return [v, first, second, flip(first[:middle], 2), flip(second[middle:], 1)]
-    shift = lambda d: lax.ppermute(v, "row", [((i + d) % rows, i) for i in range(rows)])
-    return [v] + [shift(d) for d in range(1, rows)]
+        return [flip_row(v, 1), flip_row(v, 2)]
+    return [lax.ppermute(v, "row", [((i + d) % rows, i) for i in range(rows)]) for d in range(1, rows)]
+
+
+def columns_second(first):
+    if lax.axis_size("row") != 4:
+        return []
+    middle = first[0].shape[0] // 2
+    return [flip_row(first[0][:middle], 2), flip_row(first[1][middle:], 1)]
 
 
 def column_place(group, own, rows):
@@ -297,49 +346,119 @@
     return lax.ppermute(v, "col", [(z * CORES + c, z * CORES + c + move) for z in sources for c in range(CORES)])
 
 
-def gather_rows(v, chips):
-    ups, downs = [], []
-    up = down = v
-    for hop in range(1, chips):
-        up = pass_on(up, True, range(hop - 1, chips - 1))
-        down = pass_on(down, False, range(1, chips - hop + 1))
-        ups.append(up)
-        downs.append(down)
-    return ups, downs
-
-
-def row_parts(v, chips, half):
-    slab = v.shape[0]
-    ups, downs = gather_rows(v, chips)
+def hop_both(up, down, hop, chips):
+    return (
+        pass_on(up, True, range(hop - 1, chips - 1)),
+        pass_on(down, False, range(1, chips - hop + 1)),
+    )
+
+
+def row_parts(own, ups, downs, most):
+    slab, chips = own[0].shape[0], len(ups) + 1
+    half = slab + (chips - 1) * most
     parts, choices = [], []
     for side in range(CORES):
-        mine = side == 0
-        parts.append(v if mine else swap_cores(v))
+        parts.append(own[side])
         choices.append((side * half, None))
         for distance in range(1, chips):
-            down, up = downs[distance - 1], ups[distance - 1]
-            at = side * half + slab + (distance - 1) * slab
-            parts.append(down if mine else swap_cores(down))
-            choices.append((at, (chips - distance, True)))
-            at = side * half + slab + (chips - distance - 1) * slab
-            parts.append(up if mine else swap_cores(up))
-            choices.append((at, (distance, False)))
+            start = side * half + slab
+            parts.append(downs[distance - 1][side])
+            choices.append((start + (distance - 1) * most, (chips - distance, True)))
+            parts.append(ups[distance - 1][side])
+            choices.append((start + (chips - distance - 1) * most, (distance, False)))
     return parts, tuple(choices)
 
 
-def scatter_rows(mine, other, slab, chips):
-    def part(relative):
-        at = slab + (relative - 1) * slab
-        return mine[at : at + slab] + other[at : at + slab]
+def scatter_rows(mine, other, slab, chips, limits):
+    most = limits[0]
+
+    def part(relative, size):
+        at = slab + (relative - 1) * most
+        return mine[at : at + size] + other[at : at + size]
 
     up = down = None
     for distance in range(chips - 1, 0, -1):
-        next_up, next_down = part(distance), part(chips - distance)
+        size = limits[distance - 1]
+        next_up, next_down = part(distance, size), part(chips - distance, size)
         if up is not None:
-            next_up, next_down = next_up + up, next_down + down
-        up = pass_on(next_up, True, range(0, chips - distance))
-        down = pass_on(next_down, False, range(distance, chips))
-    return mine[:slab] + other[:slab] + up + down
+            next_up, next_down = next_up.at[: up.shape[0]].add(up), next_down.at[: down.shape[0]].add(down)
+        up, down = together(
+            pass_on(next_up, True, range(0, chips - distance)),
+            pass_on(next_down, False, range(distance, chips)),
+        )
+    return up, down
+
+
+def ranks(reach, slab):
+    inner = jnp.arange(slab)
+    key = reach.reshape(-1, slab) * slab + (slab - 1 - inner)
+    ahead = key[:, None, :] > key[:, :, None]
+    return jnp.sum(ahead.astype(jnp.int32), axis=2).reshape(-1)
+
+
+def line_pattern(local, live, slab, chips, chip):
+    group_rows = slab * chips * CORES
+    wanted = jnp.any((local[:, None] == jnp.arange(group_rows)[None, :]) & live[:, None], axis=0)
+    wanted = wanted.astype(jnp.int32)
+    wanted = jnp.maximum(wanted, swap_cores(wanted))
+    ring = lambda d: lax.ppermute(
+        wanted,
+        "col",
+        [((z + d) % chips * CORES + c, z * CORES + c) for z in range(chips) for c in range(CORES)],
+    )
+    by_relative = jnp.stack([wanted] + [ring(d) for d in range(1, chips)])
+    wanters = (chip + jnp.arange(chips)) % chips
+    owners = jnp.arange(group_rows) // (slab * CORES)
+    away = (wanters[:, None] - owners[None, :]) * by_relative
+    return jnp.maximum(jnp.max(away, axis=0), 0), jnp.maximum(-jnp.min(away, axis=0), 0)
+
+
+def list_sizes(up_reach, down_reach, slab, chips):
+    hops = jnp.arange(1, chips)[:, None, None]
+    count = lambda reach: jnp.max(jnp.sum((reach.reshape(1, -1, slab) >= hops).astype(jnp.int32), axis=2), axis=1)
+    sizes = jnp.maximum(count(up_reach), count(down_reach))
+    rows = lax.axis_size("row")
+    others = [lax.ppermute(sizes, "row", [((i + d) % rows, i) for i in range(rows)]) for d in range(1, rows)]
+    return functools.reduce(jnp.maximum, others, sizes)
+
+
+def iterate(limits, slab, chips, scalars, places, samples, blocks, p_diag, col_x, x_own, x_ups, x_downs):
+    most = limits[0]
+    half = slab + (chips - 1) * most
+    p_mine, p_other = off_slots(scalars, col_x, blocks, slab, half)
+    row_x = None
+    for iteration in range(ITERS):
+        last = iteration == ITERS - 1
+        other = swap_cores(p_other)
+        up, down = scatter_rows(p_mine, other, slab, chips, limits)
+        own_w, up, down = combine(places, p_mine, other, p_diag, up, down)
+        if row_x is None:
+            x_up, x_down = hop_both(x_ups[-1][0], x_downs[-1][0], len(x_ups) + 1, chips)
+            x_ups = x_ups + [(x_up, swap_cores(x_up))]
+            x_downs = x_downs + [(x_down, swap_cores(x_down))]
+            row_x = row_parts(x_own, x_ups, x_downs, slab)
+        first = columns_first(own_w)
+        w_own = (own_w, swap_cores(own_w))
+        updated = diag_update(samples, own_w, blocks, last)
+        w_ups, w_downs = [], []
+        for hop in range(1, chips):
+            size = limits[hop - 1]
+            up, down = hop_both(up[:size], down[:size], hop, chips)
+            if hop == chips - 2:
+                up, down, first, w_own, updated, w_ups, w_downs = together(
+                    up, down, first, w_own, updated, w_ups, w_downs
+                )
+            else:
+                up, down = together(up, down)
+            w_ups.append((up, swap_cores(up)))
+            w_downs.append((down, swap_cores(down)))
+        col_w = [own_w] + first + columns_second(first)
+        row_w = row_parts(w_own, w_ups, w_downs, most)
+        result = off_slots(scalars, col_x, blocks, slab, half, (col_w, row_x, row_w, updated[0]), not last)
+        blocks = result[0]
+        if not last:
+            p_diag, (p_mine, p_other) = updated[1], result[1:]
+    return blocks
 
 
 def shards(samples, omega, block_rows, block_cols):
@@ -348,44 +467,65 @@
     slab = samples.shape[0]
     chips = n_col // CORES
     chip, core = b // CORES, b % CORES
-    half = slab * chips
     blocks = omega[0, 0]
     rows = block_rows[0, 0, slab:]
     cols = block_cols[0, 0, slab:]
+
+    first = columns_first(samples)
+    x_own = (samples, swap_cores(samples))
+    x_ups, x_downs = [], []
+    up = down = samples
+    for hop in range(1, chips - 1):
+        up, down = hop_both(up, down, hop, chips)
+        x_ups.append((up, swap_cores(up)))
+        x_downs.append((down, swap_cores(down)))
+    col_x = [samples] + first + columns_second(first)
+    p_diag = diag_products(samples, blocks)
+
     live = rows >= 0
     local = rows - a * (slab * n_col)
+    up_reach, down_reach = line_pattern(local, live, slab, chips, chip)
+    up_rank, down_rank = ranks(up_reach, slab), ranks(down_reach, slab)
     owner, inner = local // slab, local % slab
     side = (owner % CORES) ^ core
     relative = (owner // CORES - chip) % chips
-    place = jnp.where(live, side * half + relative * slab + inner, 0)
-    target = jnp.where(live, place, CORES * half)
+    pick = lambda table: jnp.sum(
+        jnp.where(local[:, None] == jnp.arange(table.shape[0])[None, :], table[None, :], 0), axis=1
+    )
+    listed = jnp.where(owner // CORES > chip, pick(down_rank), pick(up_rank))
     group = column_place(cols // slab // n_col, a, n_row)
     column = jnp.where(live, group * slab + cols % slab, 0)
-    scalars = jnp.stack(
-        [target, column, place, jnp.full_like(place, chip), live.astype(jnp.int32)]
-    ).astype(jnp.int32)
-
-    col_x = gather_columns(samples)
-    row_x, choices = row_parts(samples, chips, half)
-    p_diag = diag_products(samples, blocks)
-    p_mine, p_other = off_slots(scalars, col_x, blocks, slab, half, choices)
-    for iteration in range(ITERS):
-        last = iteration == ITERS - 1
-        own_w = scatter_rows(p_mine, swap_cores(p_other), slab, chips) + p_diag
-        col_w = gather_columns(own_w)
-        row_w, _ = row_parts(own_w, chips, half)
-        if last:
-            (buffer,) = diag_update(samples, own_w, blocks, last)
-        else:
-            buffer, p_diag = diag_update(samples, own_w, blocks, last)
-        result = off_slots(
-            scalars, col_x, blocks, slab, half, choices, (col_w, row_x, row_w, buffer), not last
-        )
-        if last:
-            blocks = result[0]
-        else:
-            blocks, p_mine, p_other = result
-    return blocks[None, None]
+    x_place = jnp.where(live, (side * chips + relative) * slab + inner, 0)
+    own_ranks = lambda table: lax.dynamic_slice_in_dim(table, b * slab, slab)
+    places = jnp.stack([own_ranks(up_rank), own_ranks(down_rank)]).astype(jnp.int32)
+
+    def branch(limits):
+        half = slab + (chips - 1) * limits[0]
+
+        def run(samples, blocks, p_diag, col_x, x_own, x_ups, x_downs):
+            inside = jnp.where(relative == 0, inner, slab + (relative - 1) * limits[0] + listed)
+            place = jnp.where(live, side * half + inside, 0)
+            target = jnp.where(live, place, CORES * half)
+            scalars = jnp.stack(
+                [target, column, x_place, jnp.full_like(place, chip), live.astype(jnp.int32), place]
+            ).astype(jnp.int32)
+            return iterate(limits, slab, chips, scalars, places, samples, blocks, p_diag, col_x, x_own, x_ups, x_downs)
+
+        return run
+
+    tiers = []
+    for tier in TIERS:
+        limits = tuple(min(slab, tier[min(hop, len(tier) - 1)]) for hop in range(chips - 1))
+        if limits not in tiers:
+            tiers.append(limits)
+    state = (samples, blocks, p_diag, col_x, x_own, x_ups, x_downs)
+    if len(tiers) == 1:
+        result = branch(tiers[0])(*state)
+    else:
+        sizes = list_sizes(up_reach, down_reach, slab, chips)
+        too_long = [jnp.any(sizes > jnp.array(limits)).astype(jnp.int32) for limits in tiers[:-1]]
+        result = lax.switch(sum(too_long), [branch(limits) for limits in tiers], *state)
+    return result[None, None]
 
 
 def solution(mesh):

time: 598 us -> 525 us (0.88); the launches traced: 597 us -> 516 us
  waiting for transfers between devices: 404 us -> 302 us
  loops' own time: 0 us -> 14.4 us
  local copies, waits for them, and re-layouts: 5.13 us -> 18.5 us
  starting transfers between devices: 100 us -> 87.2 us
    ppermute x30, waiting for transfers between devices: 339 us -> 212 us  [pass_on(): lax.ppermute(v, 'col', [(z * CORES + c, z * CORES + c + move) for z in so...]
    ppermute x12 -> x18, waiting for transfers between devices: 50.2 us -> 76.3 us  [the longest x12 52 us: flip_row(): lax.ppermute(part, 'row', [(i, i ^ bit) for i in range(lax.axis_size('row...]
    ppermute x30, starting transfers between devices: 79.7 us -> 58.9 us  [pass_on(): lax.ppermute(v, 'col', [(z * CORES + c, z * CORES + c + move) for z in so...]
    another operation x0 -> x1, loops' own time: none -> 14.4 us  [shards(): lax.switch(sum(too_long), [branch(limits) for limits in tiers], *state)]
    pallas_call x0 -> x2, Pallas kernels: none -> 9.85 us  [combine(): pl.pallas_call(combine_kernel, grid_spec=pltpu.PrefetchScalarGridSpec(num...]
    slice x6 -> x14, local copies, waits for them, and re-layouts: 1.97 us -> 11.5 us  [the longest x8 6.53 us: iterate(): up, down = hop_both(up[:size], down[:size], hop, chips)]
    ppermute x12 -> x18, starting transfers between devices: 16.4 us -> 23.9 us  [the longest x12 13.8 us: flip_row(): lax.ppermute(part, 'row', [(i, i ^ bit) for i in range(lax.axis_size('row...]
    ppermute x23 -> x24, waiting for transfers between devices: 14.4 us -> 14.2 us  [swap_cores(): lax.ppermute(v, 'col', [(i, i ^ 1) for i in range(lax.axis_size('col'))])]
  transfers between devices with their start and end apart: 65 -> 72, of which waited for: 30 -> 29; matrix products, arithmetic and copies ran while one was open for 1% -> 3% of each run, Pallas kernels for 3% -> 3%
where the time goes in v2:
time: 525 us; the launch traced here: 516 us
  waiting for transfers between devices  302 us (58%)
  starting transfers between devices  87.2 us (17%)
  Pallas kernels  78.8 us (15%)
  local copies, waits for them, and re-layouts  18.5 us (4%)
  loops' own time  14.4 us (3%)
  other arithmetic  11.6 us (2%)
    ppermute x30, waiting for transfers between devices, pass_on(): lax.ppermute(v, 'col', [(z * CORES + c, z * CORES + c + move) for z in so...  212 us
    ppermute x30, starting transfers between devices, pass_on(): lax.ppermute(v, 'col', [(z * CORES + c, z * CORES + c + move) for z in so...  58.9 us
    pallas_call x3, Pallas kernels, off_slots(): pl.pallas_call(functools.partial(off_kernel, plan), grid_spec=pltpu.Prefe...  53.8 us
    ppermute x12, waiting for transfers between devices, flip_row(): lax.ppermute(part, 'row', [(i, i ^ bit) for i in range(lax.axis_size('row...  52 us
    ppermute x3, waiting for transfers between devices, line_pattern(): lax.ppermute(wanted, 'col', [((z + d) % chips * CORES + c, z * CORES + c)...  18.1 us
    another operation x1, loops' own time, shards(): lax.switch(sum(too_long), [branch(limits) for limits in tiers], *state)  14.4 us
    ppermute x24, waiting for transfers between devices, swap_cores(): lax.ppermute(v, 'col', [(i, i ^ 1) for i in range(lax.axis_size('col'))])  14.2 us
    ppermute x12, starting transfers between devices, flip_row(): lax.ppermute(part, 'row', [(i, i ^ bit) for i in range(lax.axis_size('row...  13.8 us
  transfers between devices with their start and end apart: 72, of which 29 were waited for; matrix products, arithmetic and copies ran while one was open for 3% of the time, Pallas kernels for 3%

profile of v2, /device:TPU:0, one launch (start us, length us, event | category | flops | bytes accessed | tf_op | source)
XLA Modules:
  0.0 515.7 jit_solution(7595856356063875170)
XLA Ops:
  0.0 5.9 %collective-permute-start.221 = (f32[32,64,128]{2,1,0:T(8,128)}, f32[32,64,128]{2,1,0:T(8,128)}, u32[]{:S(2)}, u32[]{:S(2)}) collective-permute-start(f32[32,64,128]{2,1,0:T(8,128)} %x_ref.1), channel_id=1, source_target_pairs={{0,2},{1,3},{2,4},{3,5},{4,6},{5,7},{8,10},{9,11},{10,12},{11,13},... | collective-permute-start | bytes 3145736 | tf_op jit(solution)/shard_map/ppermute | solution.py:346
  15.6 18.1 %collective-permute-done.211 = s32[256]{0:T(256)S(1)} collective-permute-done((s32[256]{0:T(256)S(1)}, s32[256]{0:T(256)S(1)}, u32[]{:S(2)}, u32[]{:S(2)}) %collective-permute-start.211) | collective-permute-done | bytes 1056 | tf_op jit(solution)/shard_map/ppermute | solution.py:404
  41.3 16.1 %collective-permute-done.216 = f32[32,64,128]{2,1,0:T(8,128)S(1)} collective-permute-done((f32[32,64,128]{2,1,0:T(8,128)}, f32[32,64,128]{2,1,0:T(8,128)S(1)}, u32[]{:S(2)}, u32[]{:S(2)}) %collective-permute-start.216) | collective-permute-done | bytes 1048608 | tf_op jit(solution)/shard_map/ppermute | solution.py:319
  83.1 8.0 %collective-permute-done.217 = f32[16,64,128]{2,1,0:T(8,128)} collective-permute-done((f32[16,64,128]{2,1,0:T(8,128)}, f32[16,64,128]{2,1,0:T(8,128)}, u32[]{:S(2)}, u32[]{:S(2)}) %collective-permute-start.217) | collective-permute-done | bytes 524320 | tf_op jit(solution)/shard_map/ppermute | solution.py:319
  91.2 423.4 %conditional.1 = (f32[1,1,128,128,128]{4,3,2,1,0:T(8,128)}) conditional(s32[]{:T(128)} %clamp.3, (s32[96]{0:T(128)S(1)}, pred[96]{0:T(512)(128)(4,1)S(1)}, s32[96]{0:T(128)S(1)}, s32[96]{0:T(128)S(1)}, s32[256]{0:T(256)S(1)}, /*index=5*/pred[96,256]{1,0:T(8,128)(4,1)S(1)}, s32[]{:T(128)}, s32[256]{0:T(256)S(1)}, ...), branch_computations={%region_12.15_spmd, %region_15.18_spmd, %region_18.21_spmd, %regio... | conditional | flops 4835612160 | bytes 562085696 | solution.py:527
  100.7 12.2 %off_products.6 = (f32[110,64,128]{2,1,0:T(8,128)}, f32[110,64,128]{2,1,0:T(8,128)}) custom-call(s32[6,96]{1,0:T(8,128)} %stack.92.scalars, f32[32,64,128]{2,1,0:T(8,128)S(1)} %get-tuple-element.1187.refs_0_.x_ref.refs_10_, f32[32,64,128]{2,1,0:T(8,128)S(1)} %get-tuple-element.1188.refs_1_, f32[32,64,128]{2,1,0:T(8,128)S(1)} %get-tuple-element.1189.refs_2_, ...), custom_call_target="tpu_custom_call" | custom-call | flops 603979776 | bytes 32374784 | tf_op jit(solution)/shard_map/cond/branch_2_fun/off_products/pallas_call | solution.py:260
  113.0 6.5 %collective-permute-done.104.other_ref = f32[110,64,128]{2,1,0:T(8,128)S(1)} collective-permute-done((f32[110,64,128]{2,1,0:T(8,128)}, f32[110,64,128]{2,1,0:T(8,128)S(1)}, u32[]{:S(2)}, u32[]{:S(2)}) %collective-permute-start.104) | collective-permute-done | bytes 3604512 | tf_op jit(solution)/shard_map/cond/branch_2_fun/ppermute | solution.py:341
  124.2 14.3 %collective-permute-done.105 = f32[20,64,128]{2,1,0:T(8,128)S(1)} collective-permute-done((f32[20,64,128]{2,1,0:T(8,128)S(1)}, f32[20,64,128]{2,1,0:T(8,128)S(1)}, u32[]{:S(2)}, u32[]{:S(2)}) %collective-permute-start.105) | collective-permute-done | bytes 655392 | tf_op jit(solution)/shard_map/cond/branch_2_fun/ppermute | solution.py:346
  139.7 5.0 collective-permute-start.107
  145.0 15.5 %collective-permute-done.107 = f32[23,64,128]{2,1,0:T(8,128)S(1)} collective-permute-done((f32[23,64,128]{2,1,0:T(8,128)S(1)}, f32[23,64,128]{2,1,0:T(8,128)S(1)}, u32[]{:S(2)}, u32[]{:S(2)}) %collective-permute-start.107) | collective-permute-done | bytes 753696 | tf_op jit(solution)/shard_map/cond/branch_2_fun/ppermute | solution.py:346
  166.7 15.5 %collective-permute-done.109.up_ref = f32[26,64,128]{2,1,0:T(8,128)S(1)} collective-permute-done((f32[26,64,128]{2,1,0:T(8,128)S(1)}, f32[26,64,128]{2,1,0:T(8,128)S(1)}, u32[]{:S(2)}, u32[]{:S(2)}) %collective-permute-start.109) | collective-permute-done | bytes 852000 | tf_op jit(solution)/shard_map/cond/branch_2_fun/ppermute | solution.py:346
  187.8 4.8 combine.12
  199.6 12.4 %collective-permute-done.111.refs_26_ = f32[26,64,128]{2,1,0:T(8,128)S(1)} collective-permute-done((f32[26,64,128]{2,1,0:T(8,128)}, f32[26,64,128]{2,1,0:T(8,128)S(1)}, u32[]{:S(2)}, u32[]{:S(2)}) %collective-permute-start.111) | collective-permute-done | bytes 852000 | tf_op jit(solution)/shard_map/cond/branch_2_fun/ppermute | solution.py:346
  213.6 6.7 %collective-permute-done.112.refs_25_ = f32[26,64,128]{2,1,0:T(8,128)} collective-permute-done((f32[26,64,128]{2,1,0:T(8,128)}, f32[26,64,128]{2,1,0:T(8,128)}, u32[]{:S(2)}, u32[]{:S(2)}) %collective-permute-start.112) | collective-permute-done | bytes 852000 | tf_op jit(solution)/shard_map/cond/branch_2_fun/ppermute | solution.py:346
  222.1 16.5 %collective-permute-done.122.refs_15_ = f32[32,64,128]{2,1,0:T(8,128)S(1)} collective-permute-done((f32[32,64,128]{2,1,0:T(8,128)}, f32[32,64,128]{2,1,0:T(8,128)S(1)}, u32[]{:S(2)}, u32[]{:S(2)}) %collective-permute-start.122) | collective-permute-done | bytes 1048608 | tf_op jit(solution)/shard_map/cond/branch_2_fun/ppermute | solution.py:346
  244.0 11.3 %collective-permute-done.114.refs_27_ = f32[23,64,128]{2,1,0:T(8,128)} collective-permute-done((f32[23,64,128]{2,1,0:T(8,128)S(1)}, f32[23,64,128]{2,1,0:T(8,128)}, u32[]{:S(2)}, u32[]{:S(2)}) %collective-permute-start.114) | collective-permute-done | bytes 753696 | tf_op jit(solution)/shard_map/cond/branch_2_fun/ppermute | solution.py:346
  255.4 7.5 %diag_update.12 = (f32[128,128,128]{2,1,0:T(8,128)}, f32[32,64,128]{2,1,0:T(8,128)}) custom-call(f32[32,64,128]{2,1,0:T(8,128)S(1)} %get-tuple-element.1187.refs_0_.x_ref.refs_10_, f32[32,64,128]{2,1,0:T(8,128)} %get-tuple-element.1221.w_ref.refs_5_.refs_24_, f32[128,128,128]{2,1,0:T(8,128)} %get-tuple-element.1193.refs_5_.omega_ref.refs_39_), custom_call_target="tpu_custom_call" | custom-call | flops 603979776 | bytes 8388608 | tf_op jit(solution)/shard_map/cond/branch_2_fun/diag_update/pallas_call | solution.py:120
  269.3 15.8 %collective-permute-done.127.refs_29_ = f32[20,64,128]{2,1,0:T(8,128)S(1)} collective-permute-done((f32[20,64,128]{2,1,0:T(8,128)S(1)}, f32[20,64,128]{2,1,0:T(8,128)S(1)}, u32[]{:S(2)}, u32[]{:S(2)}) %collective-permute-start.127) | collective-permute-done | bytes 655392 | tf_op jit(solution)/shard_map/cond/branch_2_fun/ppermute | solution.py:346
  287.4 12.7 %collective-permute-done.120.refs_8_ = f32[16,64,128]{2,1,0:T(8,128)S(1)} collective-permute-done((f32[16,64,128]{2,1,0:T(8,128)S(1)}, f32[16,64,128]{2,1,0:T(8,128)S(1)}, u32[]{:S(2)}, u32[]{:S(2)}) %collective-permute-start.120) | collective-permute-done | bytes 524320 | tf_op jit(solution)/shard_map/cond/branch_2_fun/ppermute | solution.py:319
  301.6 25.8 %off_update.12 = (f32[128,128,128]{2,1,0:T(8,128)}, f32[110,64,128]{2,1,0:T(8,128)}, f32[110,64,128]{2,1,0:T(8,128)}) custom-call(s32[6,96]{1,0:T(8,128)} %stack.92.scalars, f32[32,64,128]{2,1,0:T(8,128)S(1)} %get-tuple-element.1187.refs_0_.x_ref.refs_10_, f32[32,64,128]{2,1,0:T(8,128)S(1)} %get-tuple-element.1188.refs_1_, ...), custom_call_target="tpu_custom_call", output_to_operand_aliasing={{0}: (39, {})} | custom-call | flops 1811939328 | bytes 32374784 | tf_op jit(solution)/shard_map/cond/branch_2_fun/off_update/pallas_call | solution.py:260
  327.5 6.5 %collective-permute-done.132.other_ref = f32[110,64,128]{2,1,0:T(8,128)S(1)} collective-permute-done((f32[110,64,128]{2,1,0:T(8,128)}, f32[110,64,128]{2,1,0:T(8,128)S(1)}, u32[]{:S(2)}, u32[]{:S(2)}) %collective-permute-start.132) | collective-permute-done | bytes 3604512 | tf_op jit(solution)/shard_map/cond/branch_2_fun/ppermute | solution.py:341
  339.1 14.0 %collective-permute-done.133 = f32[20,64,128]{2,1,0:T(8,128)S(1)} collective-permute-done((f32[20,64,128]{2,1,0:T(8,128)S(1)}, f32[20,64,128]{2,1,0:T(8,128)S(1)}, u32[]{:S(2)}, u32[]{:S(2)}) %collective-permute-start.133) | collective-permute-done | bytes 655392 | tf_op jit(solution)/shard_map/cond/branch_2_fun/ppermute | solution.py:346
  354.2 5.4 %collective-permute-start.135 = (f32[23,64,128]{2,1,0:T(8,128)S(1)}, f32[23,64,128]{2,1,0:T(8,128)S(1)}, u32[]{:S(2)}, u32[]{:S(2)}) collective-permute-start(f32[23,64,128]{2,1,0:T(8,128)S(1)} %add_dynamic-update-slice_fusion.9), channel_id=1, source_target_pairs={{0,2},{1,3},{2,4},{3,5},{8,10},{9,11},{10,12},{11,13},{16,18},{17,... | collective-permute-start | bytes 2261000 | tf_op jit(solution)/shard_map/cond/branch_2_fun/ppermute | solution.py:346
  359.9 14.8 %collective-permute-done.135 = f32[23,64,128]{2,1,0:T(8,128)S(1)} collective-permute-done((f32[23,64,128]{2,1,0:T(8,128)S(1)}, f32[23,64,128]{2,1,0:T(8,128)S(1)}, u32[]{:S(2)}, u32[]{:S(2)}) %collective-permute-start.135) | collective-permute-done | bytes 753696 | tf_op jit(solution)/shard_map/cond/branch_2_fun/ppermute | solution.py:346
  380.9 15.2 %collective-permute-done.137.up_ref = f32[26,64,128]{2,1,0:T(8,128)S(1)} collective-permute-done((f32[26,64,128]{2,1,0:T(8,128)S(1)}, f32[26,64,128]{2,1,0:T(8,128)S(1)}, u32[]{:S(2)}, u32[]{:S(2)}) %collective-permute-start.137) | collective-permute-done | bytes 852000 | tf_op jit(solution)/shard_map/cond/branch_2_fun/ppermute | solution.py:346
  396.0 4.7 collective-permute-done.138.down_ref
  401.6 5.1 combine.13
  413.9 16.9 %collective-permute-done.139.refs_26_ = f32[26,64,128]{2,1,0:T(8,128)S(1)} collective-permute-done((f32[26,64,128]{2,1,0:T(8,128)}, f32[26,64,128]{2,1,0:T(8,128)S(1)}, u32[]{:S(2)}, u32[]{:S(2)}) %collective-permute-start.139) | collective-permute-done | bytes 852000 | tf_op jit(solution)/shard_map/cond/branch_2_fun/ppermute | solution.py:346
  443.2 15.0 %collective-permute-done.142.refs_27_ = f32[23,64,128]{2,1,0:T(8,128)S(1)} collective-permute-done((f32[23,64,128]{2,1,0:T(8,128)}, f32[23,64,128]{2,1,0:T(8,128)S(1)}, u32[]{:S(2)}, u32[]{:S(2)}) %collective-permute-start.142) | collective-permute-done | bytes 753696 | tf_op jit(solution)/shard_map/cond/branch_2_fun/ppermute | solution.py:346
  462.5 14.1 %collective-permute-done.151.refs_29_ = f32[20,64,128]{2,1,0:T(8,128)S(1)} collective-permute-done((f32[20,64,128]{2,1,0:T(8,128)S(1)}, f32[20,64,128]{2,1,0:T(8,128)S(1)}, u32[]{:S(2)}, u32[]{:S(2)}) %collective-permute-start.151) | collective-permute-done | bytes 655392 | tf_op jit(solution)/shard_map/cond/branch_2_fun/ppermute | solution.py:346
  478.8 13.3 %collective-permute-done.148.refs_8_ = f32[16,64,128]{2,1,0:T(8,128)S(1)} collective-permute-done((f32[16,64,128]{2,1,0:T(8,128)S(1)}, f32[16,64,128]{2,1,0:T(8,128)S(1)}, u32[]{:S(2)}, u32[]{:S(2)}) %collective-permute-start.148) | collective-permute-done | bytes 524320 | tf_op jit(solution)/shard_map/cond/branch_2_fun/ppermute | solution.py:319
  493.9 15.8 %off_update.13 = f32[128,128,128]{2,1,0:T(8,128)} custom-call(s32[6,96]{1,0:T(8,128)} %stack.92.scalars, f32[32,64,128]{2,1,0:T(8,128)S(1)} %get-tuple-element.1187.refs_0_.x_ref.refs_10_, f32[32,64,128]{2,1,0:T(8,128)S(1)} %get-tuple-element.1188.refs_1_, f32[32,64,128]{2,1,0:T(8,128)S(1)} %get-tuple-element.1189.refs_2_, ...), custom_call_target="tpu_custom_call", output_to_operand_aliasing={{}: (39, {})} | custom-call | flops 1207959552 | bytes 32374784 | tf_op jit(solution)/shard_map/cond/branch_2_fun/off_update/pallas_call | solution.py:260
  (279 shorter events, 126.6 us)
Async XLA Ops:
  0.0 36.7 %collective-permute-start.221 = (f32[32,64,128]{2,1,0:T(8,128)}, f32[32,64,128]{2,1,0:T(8,128)}, u32[]{:S(2)}, u32[]{:S(2)}) collective-permute-start(f32[32,64,128]{2,1,0:T(8,128)} %x_ref.1), channel_id=1, source_target_pairs={{0,2},{1,3},{2,4},{3,5},{4,6},{5,7},{8,10},{9,11},{10,12},{11,13},... | collective-permute-start | bytes 3145736 | tf_op jit(solution)/shard_map/ppermute | solution.py:346
  5.9 32.5 %collective-permute-start.219 = (f32[32,64,128]{2,1,0:T(8,128)}, f32[32,64,128]{2,1,0:T(8,128)}, u32[]{:S(2)}, u32[]{:S(2)}) collective-permute-start(f32[32,64,128]{2,1,0:T(8,128)} %x_ref.1), channel_id=1, source_target_pairs={{2,0},{3,1},{4,2},{5,3},{6,4},{7,5},{10,8},{11,9},{12,10},{13,11},... | collective-permute-start | bytes 3145736 | tf_op jit(solution)/shard_map/ppermute | solution.py:346
  10.0 23.7 %collective-permute-start.211 = (s32[256]{0:T(256)S(1)}, s32[256]{0:T(256)S(1)}, u32[]{:S(2)}, u32[]{:S(2)}) collective-permute-start(s32[256]{0:T(256)S(1)} %convert_maximum_fusion), channel_id=1, source_target_pairs={{6,0},{7,1},{0,2},{1,3},{2,4},{3,5},{4,6},{5,7},{14,8},{15,9},{8,1... | collective-permute-start | bytes 3080 | tf_op jit(solution)/shard_map/ppermute | solution.py:404
  12.6 22.6 %collective-permute-start.210 = (s32[256]{0:T(256)S(1)}, s32[256]{0:T(256)S(1)}, u32[]{:S(2)}, u32[]{:S(2)}) collective-permute-start(s32[256]{0:T(256)S(1)} %convert_maximum_fusion), channel_id=1, source_target_pairs={{4,0},{5,1},{6,2},{7,3},{0,4},{1,5},{2,6},{3,7},{12,8},{13,9},{14,... | collective-permute-start | bytes 3080 | tf_op jit(solution)/shard_map/ppermute | solution.py:404
  15.3 21.5 %collective-permute-start.209 = (s32[256]{0:T(256)S(1)}, s32[256]{0:T(256)S(1)}, u32[]{:S(2)}, u32[]{:S(2)}) collective-permute-start(s32[256]{0:T(256)S(1)} %convert_maximum_fusion), channel_id=1, source_target_pairs={{2,0},{3,1},{4,2},{5,3},{6,4},{7,5},{0,6},{1,7},{10,8},{11,9},{12,... | collective-permute-start | bytes 3080 | tf_op jit(solution)/shard_map/ppermute | solution.py:404
  33.7 23.6 %collective-permute-start.216 = (f32[32,64,128]{2,1,0:T(8,128)}, f32[32,64,128]{2,1,0:T(8,128)S(1)}, u32[]{:S(2)}, u32[]{:S(2)}) collective-permute-start(f32[32,64,128]{2,1,0:T(8,128)} %x_ref.1), channel_id=1, source_target_pairs={{0,16},{8,24},{16,0},{24,8},{1,17},{9,25},{17,1},{25,9},{2,18},{10... | collective-permute-start | bytes 3145736 | tf_op jit(solution)/shard_map/ppermute | solution.py:319
  35.2 35.2 %collective-permute-start.215 = (f32[32,64,128]{2,1,0:T(8,128)}, f32[32,64,128]{2,1,0:T(8,128)S(1)}, u32[]{:S(2)}, u32[]{:S(2)}) collective-permute-start(f32[32,64,128]{2,1,0:T(8,128)} %x_ref.1), channel_id=1, source_target_pairs={{0,8},{8,0},{16,24},{24,16},{1,9},{9,1},{17,25},{25,17},{2,10},{10... | collective-permute-start | bytes 3145736 | tf_op jit(solution)/shard_map/ppermute | solution.py:319
  36.7 33.7 %collective-permute-start.223 = (f32[32,64,128]{2,1,0:T(8,128)}, f32[32,64,128]{2,1,0:T(8,128)S(1)}, u32[]{:S(2)}, u32[]{:S(2)}) collective-permute-start(f32[32,64,128]{2,1,0:T(8,128)} %x_ref.1), channel_id=1, source_target_pairs={{0,1},{1,0},{2,3},{3,2},{4,5},{5,4},{6,7},{7,6},{8,9},{9,8},{10,11... | collective-permute-start | bytes 3145736 | tf_op jit(solution)/shard_map/ppermute | solution.py:341
  36.7 34.2 %collective-permute-start.222 = (f32[32,64,128]{2,1,0:T(8,128)}, f32[32,64,128]{2,1,0:T(8,128)}, u32[]{:S(2)}, u32[]{:S(2)}) collective-permute-start(f32[32,64,128]{2,1,0:T(8,128)} %collective-permute-done.221), channel_id=1, source_target_pairs={{2,4},{3,5},{4,6},{5,7},{10,12},{11,13},{12,14},{13,15},{18,20},{1... | collective-permute-start | bytes 3145736 | tf_op jit(solution)/shard_map/ppermute | solution.py:346
  38.4 32.6 %collective-permute-start.220 = (f32[32,64,128]{2,1,0:T(8,128)}, f32[32,64,128]{2,1,0:T(8,128)}, u32[]{:S(2)}, u32[]{:S(2)}) collective-permute-start(f32[32,64,128]{2,1,0:T(8,128)} %collective-permute-done.219), channel_id=1, source_target_pairs={{2,0},{3,1},{4,2},{5,3},{10,8},{11,9},{12,10},{13,11},{18,16},{19,... | collective-permute-start | bytes 3145736 | tf_op jit(solution)/shard_map/ppermute | solution.py:346
  160.7 21.5 %collective-permute-start.109 = (f32[26,64,128]{2,1,0:T(8,128)S(1)}, f32[26,64,128]{2,1,0:T(8,128)S(1)}, u32[]{:S(2)}, u32[]{:S(2)}) collective-permute-start(f32[26,64,128]{2,1,0:T(8,128)S(1)} %fusion.31), channel_id=1, source_target_pairs={{0,2},{1,3},{2,4},{3,5},{4,6},{5,7},{8,10},{9,11},{10,12},{11,13},... | collective-permute-start | bytes 2555912 | tf_op jit(solution)/shard_map/cond/branch_2_fun/ppermute | solution.py:346
  165.4 21.5 %collective-permute-start.110 = (f32[26,64,128]{2,1,0:T(8,128)S(1)}, f32[26,64,128]{2,1,0:T(8,128)S(1)}, u32[]{:S(2)}, u32[]{:S(2)}) collective-permute-start(f32[26,64,128]{2,1,0:T(8,128)S(1)} %fusion.30), channel_id=1, source_target_pairs={{2,0},{3,1},{4,2},{5,3},{6,4},{7,5},{10,8},{11,9},{12,10},{13,11},... | collective-permute-start | bytes 2555912 | tf_op jit(solution)/shard_map/cond/branch_2_fun/ppermute | solution.py:346
  196.2 24.1 %collective-permute-start.112 = (f32[26,64,128]{2,1,0:T(8,128)}, f32[26,64,128]{2,1,0:T(8,128)}, u32[]{:S(2)}, u32[]{:S(2)}) collective-permute-start(f32[26,64,128]{2,1,0:T(8,128)} %get-tuple-element.1205), channel_id=1, source_target_pairs={{2,0},{3,1},{4,2},{5,3},{6,4},{7,5},{10,8},{11,9},{12,10},{13,11},... | collective-permute-start | bytes 2555912 | tf_op jit(solution)/shard_map/cond/branch_2_fun/ppermute | solution.py:346
  197.5 41.1 %collective-permute-start.122 = (f32[32,64,128]{2,1,0:T(8,128)}, f32[32,64,128]{2,1,0:T(8,128)S(1)}, u32[]{:S(2)}, u32[]{:S(2)}) collective-permute-start(f32[32,64,128]{2,1,0:T(8,128)} %get-tuple-element.1214.refs_13_), channel_id=1, source_target_pairs={{2,0},{3,1},{10,8},{11,9},{18,16},{19,17},{26,24},{27,25}} | collective-permute-start | bytes 3145736 | tf_op jit(solution)/shard_map/cond/branch_2_fun/ppermute | solution.py:346
  198.8 41.1 %collective-permute-start.123 = (f32[32,64,128]{2,1,0:T(8,128)}, f32[32,64,128]{2,1,0:T(8,128)S(1)}, u32[]{:S(2)}, u32[]{:S(2)}) collective-permute-start(f32[32,64,128]{2,1,0:T(8,128)} %get-tuple-element.1215.refs_14_), channel_id=1, source_target_pairs={{4,6},{5,7},{12,14},{13,15},{20,22},{21,23},{28,30},{29,31}} | collective-permute-start | bytes 3145736 | tf_op jit(solution)/shard_map/cond/branch_2_fun/ppermute | solution.py:346
  199.6 40.4 %collective-permute-start.117 = (f32[32,64,128]{2,1,0:T(8,128)}, f32[32,64,128]{2,1,0:T(8,128)S(1)}, u32[]{:S(2)}, u32[]{:S(2)}) collective-permute-start(f32[32,64,128]{2,1,0:T(8,128)} %get-tuple-element.1221.w_ref.refs_5_.refs_24_), channel_id=1, source_target_pairs={{0,1},{1,0},{2,3},{3,2},{4,5},{5,4},{6,7},{7,6},{8,9},{9,8},{10,11... | collective-permute-start | bytes 3145736 | tf_op jit(solution)/shard_map/cond/branch_2_fun/ppermute | solution.py:341
  212.1 29.4 %collective-permute-start.116 = (f32[32,64,128]{2,1,0:T(8,128)}, f32[32,64,128]{2,1,0:T(8,128)S(1)}, u32[]{:S(2)}, u32[]{:S(2)}) collective-permute-start(f32[32,64,128]{2,1,0:T(8,128)} %get-tuple-element.1221.w_ref.refs_5_.refs_24_), channel_id=1, source_target_pairs={{0,16},{8,24},{16,0},{24,8},{1,17},{9,25},{17,1},{25,9},{2,18},{10... | collective-permute-start | bytes 3145736 | tf_op jit(solution)/shard_map/cond/branch_2_fun/ppermute | solution.py:319
  220.3 22.7 %collective-permute-start.115 = (f32[32,64,128]{2,1,0:T(8,128)}, f32[32,64,128]{2,1,0:T(8,128)S(1)}, u32[]{:S(2)}, u32[]{:S(2)}) collective-permute-start(f32[32,64,128]{2,1,0:T(8,128)} %get-tuple-element.1221.w_ref.refs_5_.refs_24_), channel_id=1, source_target_pairs={{0,8},{8,0},{16,24},{24,16},{1,9},{9,1},{17,25},{25,17},{2,10},{10... | collective-permute-start | bytes 3145736 | tf_op jit(solution)/shard_map/cond/branch_2_fun/ppermute | solution.py:319
  239.9 23.0 %collective-permute-start.118 = (f32[26,64,128]{2,1,0:T(8,128)S(1)}, f32[26,64,128]{2,1,0:T(8,128)}, u32[]{:S(2)}, u32[]{:S(2)}) collective-permute-start(f32[26,64,128]{2,1,0:T(8,128)S(1)} %collective-permute-done.111.refs_26_), channel_id=1, source_target_pairs={{0,1},{1,0},{2,3},{3,2},{4,5},{5,4},{6,7},{7,6},{8,9},{9,8},{10,11... | collective-permute-start | bytes 2555912 | tf_op jit(solution)/shard_map/cond/branch_2_fun/ppermute | solution.py:341
  240.0 22.9 %collective-permute-start.119 = (f32[26,64,128]{2,1,0:T(8,128)}, f32[26,64,128]{2,1,0:T(8,128)}, u32[]{:S(2)}, u32[]{:S(2)}) collective-permute-start(f32[26,64,128]{2,1,0:T(8,128)} %collective-permute-done.112.refs_25_), channel_id=1, source_target_pairs={{0,1},{1,0},{2,3},{3,2},{4,5},{5,4},{6,7},{7,6},{8,9},{9,8},{10,11... | collective-permute-start | bytes 2555912 | tf_op jit(solution)/shard_map/cond/branch_2_fun/ppermute | solution.py:341
  243.0 42.0 %collective-permute-start.124 = (f32[32,64,128]{2,1,0:T(8,128)S(1)}, f32[32,64,128]{2,1,0:T(8,128)S(1)}, u32[]{:S(2)}, u32[]{:S(2)}) collective-permute-start(f32[32,64,128]{2,1,0:T(8,128)S(1)} %collective-permute-done.122.refs_15_), channel_id=1, source_target_pairs={{0,1},{1,0},{2,3},{3,2},{4,5},{5,4},{6,7},{7,6},{8,9},{9,8},{10,11... | collective-permute-start | bytes 3145736 | tf_op jit(solution)/shard_map/cond/branch_2_fun/ppermute | solution.py:341
  255.4 30.2 %collective-permute-start.125 = (f32[32,64,128]{2,1,0:T(8,128)S(1)}, f32[32,64,128]{2,1,0:T(8,128)}, u32[]{:S(2)}, u32[]{:S(2)}) collective-permute-start(f32[32,64,128]{2,1,0:T(8,128)S(1)} %collective-permute-done.123.refs_16_), channel_id=1, source_target_pairs={{0,1},{1,0},{2,3},{3,2},{4,5},{5,4},{6,7},{7,6},{8,9},{9,8},{10,11... | collective-permute-start | bytes 3145736 | tf_op jit(solution)/shard_map/cond/branch_2_fun/ppermute | solution.py:341
  269.0 31.0 %collective-permute-start.128 = (f32[23,64,128]{2,1,0:T(8,128)}, f32[23,64,128]{2,1,0:T(8,128)S(1)}, u32[]{:S(2)}, u32[]{:S(2)}) collective-permute-start(f32[23,64,128]{2,1,0:T(8,128)} %collective-permute-done.114.refs_27_), channel_id=1, source_target_pairs={{0,1},{1,0},{2,3},{3,2},{4,5},{5,4},{6,7},{7,6},{8,9},{9,8},{10,11... | collective-permute-start | bytes 2261000 | tf_op jit(solution)/shard_map/cond/branch_2_fun/ppermute | solution.py:341
  406.7 30.5 %collective-permute-start.145 = (f32[32,64,128]{2,1,0:T(8,128)}, f32[32,64,128]{2,1,0:T(8,128)S(1)}, u32[]{:S(2)}, u32[]{:S(2)}) collective-permute-start(f32[32,64,128]{2,1,0:T(8,128)} %get-tuple-element.1249.w_ref.refs_5_.refs_24_), channel_id=1, source_target_pairs={{0,1},{1,0},{2,3},{3,2},{4,5},{5,4},{6,7},{7,6},{8,9},{9,8},{10,11... | collective-permute-start | bytes 3145736 | tf_op jit(solution)/shard_map/cond/branch_2_fun/ppermute | solution.py:341
  406.7 31.8 %collective-permute-start.144 = (f32[32,64,128]{2,1,0:T(8,128)}, f32[32,64,128]{2,1,0:T(8,128)}, u32[]{:S(2)}, u32[]{:S(2)}) collective-permute-start(f32[32,64,128]{2,1,0:T(8,128)} %get-tuple-element.1249.w_ref.refs_5_.refs_24_), channel_id=1, source_target_pairs={{0,16},{8,24},{16,0},{24,8},{1,17},{9,25},{17,1},{25,9},{2,18},{10... | collective-permute-start | bytes 3145736 | tf_op jit(solution)/shard_map/cond/branch_2_fun/ppermute | solution.py:319
  408.2 22.5 %collective-permute-start.139 = (f32[26,64,128]{2,1,0:T(8,128)}, f32[26,64,128]{2,1,0:T(8,128)S(1)}, u32[]{:S(2)}, u32[]{:S(2)}) collective-permute-start(f32[26,64,128]{2,1,0:T(8,128)} %get-tuple-element.1242), channel_id=1, source_target_pairs={{0,2},{1,3},{2,4},{3,5},{4,6},{5,7},{8,10},{9,11},{10,12},{11,13},... | collective-permute-start | bytes 2555912 | tf_op jit(solution)/shard_map/cond/branch_2_fun/ppermute | solution.py:346
  411.9 22.9 %collective-permute-start.140 = (f32[26,64,128]{2,1,0:T(8,128)}, f32[26,64,128]{2,1,0:T(8,128)S(1)}, u32[]{:S(2)}, u32[]{:S(2)}) collective-permute-start(f32[26,64,128]{2,1,0:T(8,128)} %get-tuple-element.1243), channel_id=1, source_target_pairs={{2,0},{3,1},{4,2},{5,3},{6,4},{7,5},{10,8},{11,9},{12,10},{13,11},... | collective-permute-start | bytes 2555912 | tf_op jit(solution)/shard_map/cond/branch_2_fun/ppermute | solution.py:346
  413.2 29.9 %collective-permute-start.143 = (f32[32,64,128]{2,1,0:T(8,128)}, f32[32,64,128]{2,1,0:T(8,128)}, u32[]{:S(2)}, u32[]{:S(2)}) collective-permute-start(f32[32,64,128]{2,1,0:T(8,128)} %get-tuple-element.1249.w_ref.refs_5_.refs_24_), channel_id=1, source_target_pairs={{0,8},{8,0},{16,24},{24,16},{1,9},{9,1},{17,25},{25,17},{2,10},{10... | collective-permute-start | bytes 3145736 | tf_op jit(solution)/shard_map/cond/branch_2_fun/ppermute | solution.py:319
  434.8 23.3 %collective-permute-start.146 = (f32[26,64,128]{2,1,0:T(8,128)S(1)}, f32[26,64,128]{2,1,0:T(8,128)S(1)}, u32[]{:S(2)}, u32[]{:S(2)}) collective-permute-start(f32[26,64,128]{2,1,0:T(8,128)S(1)} %collective-permute-done.139.refs_26_), channel_id=1, source_target_pairs={{0,1},{1,0},{2,3},{3,2},{4,5},{5,4},{6,7},{7,6},{8,9},{9,8},{10,11... | collective-permute-start | bytes 2555912 | tf_op jit(solution)/shard_map/cond/branch_2_fun/ppermute | solution.py:341
  434.8 23.3 %collective-permute-start.147 = (f32[26,64,128]{2,1,0:T(8,128)S(1)}, f32[26,64,128]{2,1,0:T(8,128)}, u32[]{:S(2)}, u32[]{:S(2)}) collective-permute-start(f32[26,64,128]{2,1,0:T(8,128)S(1)} %collective-permute-done.140.refs_25_), channel_id=1, source_target_pairs={{0,1},{1,0},{2,3},{3,2},{4,5},{5,4},{6,7},{7,6},{8,9},{9,8},{10,11... | collective-permute-start | bytes 2555912 | tf_op jit(solution)/shard_map/cond/branch_2_fun/ppermute | solution.py:341
  462.0 30.2 %collective-permute-start.152 = (f32[23,64,128]{2,1,0:T(8,128)S(1)}, f32[23,64,128]{2,1,0:T(8,128)S(1)}, u32[]{:S(2)}, u32[]{:S(2)}) collective-permute-start(f32[23,64,128]{2,1,0:T(8,128)S(1)} %collective-permute-done.142.refs_27_), channel_id=1, source_target_pairs={{0,1},{1,0},{2,3},{3,2},{4,5},{5,4},{6,7},{7,6},{8,9},{9,8},{10,11... | collective-permute-start | bytes 2261000 | tf_op jit(solution)/shard_map/cond/branch_2_fun/ppermute | solution.py:341
  462.0 30.2 %collective-permute-start.153 = (f32[23,64,128]{2,1,0:T(8,128)S(1)}, f32[23,64,128]{2,1,0:T(8,128)S(1)}, u32[]{:S(2)}, u32[]{:S(2)}) collective-permute-start(f32[23,64,128]{2,1,0:T(8,128)S(1)} %collective-permute-done.141.refs_28_), channel_id=1, source_target_pairs={{0,1},{1,0},{2,3},{3,2},{4,5},{5,4},{6,7},{7,6},{8,9},{9,8},{10,11... | collective-permute-start | bytes 2261000 | tf_op jit(solution)/shard_map/cond/branch_2_fun/ppermute | solution.py:341
  (83 other events, 1179.2 us)

commit v3 on v1

--- a/solution.py
+++ b/solution.py
@@ -12,6 +12,9 @@
 PENALTY = 0.1
 VMEM_BYTES = 56 * 1024 * 1024
 CORES = 2
+UNROLL = 4
+TIERS = (15, 17, 19, 1 << 30)
+MOST_COLUMNS = 24
 
 
 def split(x):
@@ -61,19 +64,34 @@
     return 1
 
 
+def each(count, one):
+    unroll = UNROLL if count % UNROLL == 0 else 1
+
+    def some(i, carry):
+        for j in range(unroll):
+            one(i * unroll + j)
+        return carry
+
+    lax.fori_loop(0, count // unroll, some, 0)
+
+
 def diag_products_kernel(x_ref, omega_ref, p_ref):
-    for k in range(x_ref.shape[0]):
+    def one(k):
         p_ref[k] = product(x_ref[k], omega_ref[k])
 
+    each(x_ref.shape[0], one)
+
 
 def diag_update_kernel(scale, last, x_ref, w_ref, omega_ref, out_ref, *p_refs):
-    for k in range(x_ref.shape[0]):
+    def one(k):
         x, w = x_ref[k], w_ref[k]
         v = omega_ref[k] - STEP * (gradient(w, x, x, w) * scale)
         new = lift_diagonal(v, shrink(v))
         out_ref[k] = new
         if not last:
             p_refs[0][k] = product(x, new)
+
+    each(x_ref.shape[0], one)
 
 
 def params():
@@ -129,15 +147,15 @@
 
 
 def off_kernel(plan, scalars, *refs):
-    update, products, scale, size, slab, n_col, n_row, choices = plan
+    update, products, scale, size, n_col, n_col_w, x_choices, w_choices = plan
     steps = pl.num_programs(0)
     step = pl.program_id(0)
     refs = list(refs)
     take = lambda n: [refs.pop(0) for _ in range(n)]
     col_x_parts = take(n_col)
-    col_w_parts = take(n_col) if update else []
-    row_x_parts = take(n_row) if update else []
-    row_w_parts = take(n_row) if update else []
+    col_w_parts = take(n_col_w)
+    row_x_parts = take(len(x_choices)) if update else []
+    row_w_parts = take(len(w_choices)) if update else []
     if update:
         take(1)
     (omega_ref,) = take(1)
@@ -161,7 +179,7 @@
             add(None, part, target.at[pl.ds(at, part.shape[0])])
             at += part.shape[0]
 
-    def rows(parts, target):
+    def rows(parts, choices, target):
         for part, (at, wanted) in zip(parts, choices):
             condition = None
             if wanted is not None:
@@ -172,10 +190,10 @@
     columns(col_x_parts, col_x)
     if update:
         columns(col_w_parts, col_w)
-        rows(row_x_parts, row_x)
-        rows(row_w_parts, row_w)
-
-    def each(action):
+        rows(row_x_parts, x_choices, row_x)
+        rows(row_w_parts, w_choices, row_w)
+
+    def for_all(action):
         for condition, copy in copies:
             if condition is None:
                 action(copy)
@@ -184,24 +202,26 @@
 
     @pl.when(step == 0)
     def _():
-        each(lambda copy: copy.start())
+        for_all(lambda copy: copy.start())
         if products:
             acc[...] = jnp.zeros_like(acc)
-        each(lambda copy: copy.wait())
-
-    for k in range(size):
+        for_all(lambda copy: copy.wait())
+
+    def one_slot(k):
         slot = step * size + k
         target = scalars[0, slot]
         column = scalars[1, slot]
         x = col_x[column]
         block = omega_ref[k]
         if update:
-            source = scalars[2, slot]
-            grad = gradient(row_w[source], x, row_x[source], col_w[column]) * scale
+            row_at, x_at = scalars[2, slot], scalars[5, slot]
+            grad = gradient(row_w[row_at], x, row_x[x_at], col_w[scalars[6, slot]]) * scale
             block = jnp.where(scalars[4, slot] > 0, shrink(block - STEP * grad), 0.0)
             out_refs[0][k] = block
         if products:
             acc[target] += product(x, block)
+
+    each(size, one_slot)
 
     if products:
 
@@ -218,7 +238,7 @@
                 copy.wait()
 
 
-def off_slots(scalars, col_x, omega, slab, half, choices, state=None, products=True):
+def off_slots(scalars, col_x, omega, slab, half, state=None, products=True):
     update = state is not None
     cap, width = omega.shape[0], omega.shape[1]
     count = col_x[0].shape[1]
@@ -231,17 +251,17 @@
     operands = list(col_x)
     scratch = [pltpu.VMEM((col_blocks,) + block, jnp.float32)]
     copies = len(col_x)
-    n_row = 0
+    col_w, x_choices, w_choices = (), (), ()
     if update:
-        col_w, row_x, row_w, buffer = state
-        n_row = len(row_x)
+        col_w, (row_x, x_choices), (row_w, w_choices), buffer = state
         operands += list(col_w) + list(row_x) + list(row_w) + [buffer]
+        row_blocks = lambda parts, choices: max(at + part.shape[0] for part, (at, _) in zip(parts, choices))
         scratch += [
-            pltpu.VMEM((col_blocks,) + block, jnp.float32),
-            pltpu.VMEM((2 * half,) + block, jnp.float32),
-            pltpu.VMEM((2 * half,) + block, jnp.float32),
+            pltpu.VMEM((sum(part.shape[0] for part in col_w),) + block, jnp.float32),
+            pltpu.VMEM((row_blocks(row_x, x_choices),) + block, jnp.float32),
+            pltpu.VMEM((row_blocks(row_w, w_choices),) + block, jnp.float32),
         ]
-        copies = 2 * len(col_x) + 2 * n_row
+        copies = len(col_x) + len(col_w) + len(row_x) + len(row_w)
     in_specs = [any_spec] * len(operands) + [slots]
     aliases = {len(operands): 0} if update else {}
     outs, out_specs = [], []
@@ -251,11 +271,11 @@
     if products:
         outs += [jax.ShapeDtypeStruct((half,) + block, jnp.float32)] * 2
         out_specs += [any_spec] * 2
-        scratch.append(pltpu.VMEM((2 * half + 1,) + block, jnp.float32))
+        scratch.append(pltpu.VMEM((CORES * half + 1,) + block, jnp.float32))
     scratch.append(pltpu.SemaphoreType.DMA((copies,)))
     if products:
         scratch.append(pltpu.SemaphoreType.DMA((2,)))
-    plan = (update, products, 0.5 / count, size, slab, len(col_x), n_row, choices)
+    plan = (update, products, 0.5 / count, size, len(col_x), len(col_w), x_choices, w_choices)
     return pl.pallas_call(
         functools.partial(off_kernel, plan),
         grid_spec=pltpu.PrefetchScalarGridSpec(
@@ -273,15 +293,71 @@
     )(scalars, *operands, omega)
 
 
-def gather_columns(v):
+def combine_kernel(chips, places, mine_ref, other_ref, diag_ref, *refs):
+    came, (w_ref, *sends) = refs[: chips - 1], refs[chips - 1 :]
+    most = came[0].shape[0]
+    def one(i):
+        at = [places[r, i] for r in range(len(sends))]
+        w = mine_ref[i] + other_ref[i] + diag_ref[i]
+        for r in range(1, chips):
+            place = at[chips - r - 1]
+            w = w + jnp.where(place < most, came[r - 1][jnp.minimum(place, most - 1)], 0.0)
+        w_ref[i] = w
+        for place, send in zip(at, sends):
+
+            @pl.when(place < send.shape[0])
+            def _(place=place, send=send):
+                send[place] = w
+
+    each(w_ref.shape[0], one)
+
+
+def combine(places, mine, other, diag, came, most_columns):
+    slab, most, block = diag.shape[0], came[0].shape[0], diag.shape[1:]
+    chips = len(came) + 1
+    sizes = [slab] + [most] * (chips - 1) + [most_columns] * (places.shape[0] - chips + 1)
+    whole = lambda n: pl.BlockSpec((n,) + block, lambda i, s: (0, 0, 0))
+    own, *sends = pl.pallas_call(
+        functools.partial(combine_kernel, chips),
+        grid_spec=pltpu.PrefetchScalarGridSpec(
+            num_scalar_prefetch=1,
+            grid=(1,),
+            in_specs=[whole(slab)] * 3 + [whole(most)] * (chips - 1),
+            out_specs=[whole(n) for n in sizes],
+        ),
+        out_shape=[jax.ShapeDtypeStruct((n,) + block, jnp.float32) for n in sizes],
+        compiler_params=params(),
+        name="combine",
+    )(places, mine, other, diag, *came)
+    return own, sends[: chips - 1], sends[chips - 1 :]
+
+
+def together(*values):
+    return lax.optimization_barrier(values)
+
+
+def flip_row(part, bit):
+    return lax.ppermute(part, "row", [(i, i ^ bit) for i in range(lax.axis_size("row"))])
+
+
+def from_row(v, d, back=False):
     rows = lax.axis_size("row")
     if rows == 4:
-        flip = lambda part, bit: lax.ppermute(part, "row", [(i, i ^ bit) for i in range(rows)])
-        middle = v.shape[0] // 2
-        first, second = flip(v, 1), flip(v, 2)
-        return [v, first, second, flip(first[:middle], 2), flip(second[middle:], 1)]
-    shift = lambda d: lax.ppermute(v, "row", [((i + d) % rows, i) for i in range(rows)])
-    return [v] + [shift(d) for d in range(1, rows)]
+        return flip_row(v, d)
+    pairs = [((i + d) % rows, i) for i in range(rows)]
+    return lax.ppermute(v, "row", [pair[::-1] for pair in pairs] if back else pairs)
+
+
+def columns_first(v):
+    rows = lax.axis_size("row")
+    return [from_row(v, d) for d in range(1, 3 if rows == 4 else rows)]
+
+
+def columns_second(first):
+    if lax.axis_size("row") != 4:
+        return []
+    middle = first[0].shape[0] // 2
+    return [flip_row(first[0][:middle], 2), flip_row(first[1][middle:], 1)]
 
 
 def column_place(group, own, rows):
@@ -297,49 +373,116 @@
     return lax.ppermute(v, "col", [(z * CORES + c, z * CORES + c + move) for z in sources for c in range(CORES)])
 
 
-def gather_rows(v, chips):
-    ups, downs = [], []
-    up = down = v
-    for hop in range(1, chips):
-        up = pass_on(up, True, range(hop - 1, chips - 1))
-        down = pass_on(down, False, range(1, chips - hop + 1))
-        ups.append(up)
-        downs.append(down)
-    return ups, downs
-
-
-def row_parts(v, chips, half):
-    slab = v.shape[0]
-    ups, downs = gather_rows(v, chips)
+def hop_both(up, down, hop, chips):
+    return (
+        pass_on(up, True, range(hop - 1, chips - 1)),
+        pass_on(down, False, range(1, chips - hop + 1)),
+    )
+
+
+def row_parts(own, ups, downs, most):
+    slab, chips = own[0].shape[0], len(ups) + 1
+    half = slab + (chips - 1) * most
     parts, choices = [], []
     for side in range(CORES):
-        mine = side == 0
-        parts.append(v if mine else swap_cores(v))
+        parts.append(own[side])
         choices.append((side * half, None))
         for distance in range(1, chips):
-            down, up = downs[distance - 1], ups[distance - 1]
-            at = side * half + slab + (distance - 1) * slab
-            parts.append(down if mine else swap_cores(down))
-            choices.append((at, (chips - distance, True)))
-            at = side * half + slab + (chips - distance - 1) * slab
-            parts.append(up if mine else swap_cores(up))
-            choices.append((at, (distance, False)))
+            start = side * half + slab
+            parts.append(downs[distance - 1][side])
+            choices.append((start + (distance - 1) * most, (chips - distance, True)))
+            parts.append(ups[distance - 1][side])
+            choices.append((start + (chips - distance - 1) * most, (distance, False)))
     return parts, tuple(choices)
 
 
-def scatter_rows(mine, other, slab, chips):
-    def part(relative):
-        at = slab + (relative - 1) * slab
-        return mine[at : at + slab] + other[at : at + slab]
-
-    up = down = None
-    for distance in range(chips - 1, 0, -1):
-        next_up, next_down = part(distance), part(chips - distance)
-        if up is not None:
-            next_up, next_down = next_up + up, next_down + down
-        up = pass_on(next_up, True, range(0, chips - distance))
-        down = pass_on(next_down, False, range(distance, chips))
-    return mine[:slab] + other[:slab] + up + down
+def ring_parts(own, came, most):
+    slab, chips = own[0].shape[0], len(came) + 1
+    half = slab + (chips - 1) * most
+    parts, choices = [], []
+    for side in range(CORES):
+        parts.append(own[side])
+        choices.append((side * half, None))
+        for r in range(1, chips):
+            parts.append(came[r - 1][side])
+            choices.append((side * half + slab + (chips - r - 1) * most, None))
+    return parts, tuple(choices)
+
+
+def round_ring(v, r, chips):
+    pairs = [(z * CORES + c, (z + r) % chips * CORES + c) for z in range(chips) for c in range(CORES)]
+    return lax.ppermute(v, "col", pairs)
+
+
+def line_pattern(wanted, chip):
+    chips = lax.axis_size("col") // CORES
+    wanted = jnp.maximum(wanted, swap_cores(wanted))
+    table = jnp.where(jnp.arange(chips)[:, None] == chip, wanted[None], 0)
+    steps = chips.bit_length() - 1 if chips & (chips - 1) == 0 else chips - 1
+    for step in range(steps):
+        there = (lambda z: z ^ 1 << step) if steps < chips - 1 else (lambda z: (z + 1) % chips)
+        pairs = [(z * CORES + c, there(z) * CORES + c) for z in range(chips) for c in range(CORES)]
+        table = jnp.maximum(table, lax.ppermute(table, "col", pairs))
+    return wanted, table
+
+
+def places_in_lists(wanted, slab):
+    before = jnp.arange(slab)[:, None] > jnp.arange(slab)[None, :]
+    place = jnp.sum(jnp.where(before, wanted[..., None, :], 0), axis=-1)
+    return jnp.where(wanted > 0, place, slab)
+
+
+def longest_list(table, slab):
+    chips = table.shape[0]
+    counts = jnp.sum(table.reshape(chips, -1, slab), axis=2)
+    own = jnp.arange(chips)[:, None] == jnp.arange(counts.shape[1])[None, :] // CORES
+    return jnp.max(jnp.where(own, 0, counts))
+
+
+def place_of(listed, relative, inner, side, live, slab, chips, most):
+    inside = jnp.where(relative == 0, inner, slab + (relative - 1) * most + listed)
+    return jnp.where(live, side * (slab + (chips - 1) * most) + inside, 0)
+
+
+def both_cores(flow):
+    return [(part, swap_cores(part)) for part in flow]
+
+
+def iterate(most, most_columns, stride, slab, chips, scalars, places, samples, blocks, p_diag, col_x, x_own, x_ups, x_downs, p_mine, other):
+    half = slab + (chips - 1) * most
+    row_x = None
+    for iteration in range(ITERS):
+        last = iteration == ITERS - 1
+        if iteration > 0:
+            other = swap_cores(p_other)
+        came = []
+        for r in range(1, chips):
+            at = slab + (r - 1) * stride
+            came.append(round_ring(p_mine[at : at + most] + other[at : at + most], r, chips))
+        if row_x is None:
+            came, flow = together(came, hop_both(x_ups[-1], x_downs[-1], chips - 1, chips))
+            x_ups, x_downs = x_ups + [flow[0]], x_downs + [flow[1]]
+        own_w, sends, column_sends = combine(places, p_mine, other, p_diag, together(*came), most_columns)
+        came = [round_ring(send, r, chips) for r, send in enumerate(sends, 1)]
+        w_columns = [from_row(send, d) for d, send in enumerate(column_sends, 1)]
+        w_own = (own_w, swap_cores(own_w))
+        updated = diag_update(samples, own_w, blocks, last)
+        longest = chips // 2 - 1
+        rest = came[:longest] + came[longest + 1 :]
+        if row_x is None:
+            rest, w_columns, updated = together(rest, w_columns, updated)
+            row_x = row_parts(x_own, both_cores(x_ups), both_cores(x_downs), slab)
+        else:
+            rest, w_columns, updated = together(rest, w_columns, updated)
+        rest = both_cores(rest)
+        came = rest[:longest] + both_cores([came[longest]]) + rest[longest:]
+        row_w = ring_parts(w_own, came, most)
+        state = ([own_w] + w_columns, row_x, row_w, updated[0])
+        result = off_slots(scalars, col_x, blocks, slab, half, state, not last)
+        blocks = result[0]
+        if not last:
+            p_diag, (p_mine, p_other), stride = updated[1], result[1:], most
+    return blocks
 
 
 def shards(samples, omega, block_rows, block_cols):
@@ -348,44 +491,84 @@
     slab = samples.shape[0]
     chips = n_col // CORES
     chip, core = b // CORES, b % CORES
-    half = slab * chips
     blocks = omega[0, 0]
     rows = block_rows[0, 0, slab:]
     cols = block_cols[0, 0, slab:]
+
+    first = columns_first(samples)
+    x_own = (samples, swap_cores(samples))
+    x_ups, x_downs = ([part] for part in hop_both(samples, samples, 1, chips))
+
     live = rows >= 0
     local = rows - a * (slab * n_col)
     owner, inner = local // slab, local % slab
     side = (owner % CORES) ^ core
     relative = (owner // CORES - chip) % chips
-    place = jnp.where(live, side * half + relative * slab + inner, 0)
-    target = jnp.where(live, place, CORES * half)
-    group = column_place(cols // slab // n_col, a, n_row)
-    column = jnp.where(live, group * slab + cols % slab, 0)
-    scalars = jnp.stack(
-        [target, column, place, jnp.full_like(place, chip), live.astype(jnp.int32)]
-    ).astype(jnp.int32)
-
-    col_x = gather_columns(samples)
-    row_x, choices = row_parts(samples, chips, half)
+    group, column_inner = column_place(cols // slab // n_col, a, n_row), cols % slab
+    column = jnp.where(live, group * slab + column_inner, 0)
+
     p_diag = diag_products(samples, blocks)
-    p_mine, p_other = off_slots(scalars, col_x, blocks, slab, half, choices)
-    for iteration in range(ITERS):
-        last = iteration == ITERS - 1
-        own_w = scatter_rows(p_mine, swap_cores(p_other), slab, chips) + p_diag
-        col_w = gather_columns(own_w)
-        row_w, _ = row_parts(own_w, chips, half)
-        if last:
-            (buffer,) = diag_update(samples, own_w, blocks, last)
-        else:
-            buffer, p_diag = diag_update(samples, own_w, blocks, last)
-        result = off_slots(
-            scalars, col_x, blocks, slab, half, choices, (col_w, row_x, row_w, buffer), not last
+    among = lambda ids, count: jnp.any((ids[:, None] == jnp.arange(count)[None, :]) & live[:, None], axis=0).astype(jnp.int32)
+    columns = among(column, n_row * slab).reshape(n_row, slab)
+    longest_columns = jnp.max(jnp.sum(columns[1:], axis=1))
+    wanted, table = line_pattern(jnp.concatenate([among(local, n_col * slab), longest_columns[None]]), chip)
+    x_ups, x_downs, table, first, p_diag = together(x_ups, x_downs, table, first, p_diag)
+    for hop in range(2, chips - 1):
+        up, down = hop_both(x_ups[-1], x_downs[-1], hop, chips)
+        x_ups, x_downs = x_ups + [up], x_downs + [down]
+    col_x = [samples] + first + columns_second(first)
+    longest_columns = jnp.max(table[:, -1])
+    longest = longest_list(table[:, :-1], slab)
+    told = [from_row(jnp.concatenate([columns[d], longest[None], longest_columns[None]]), d, True) for d in range(1, n_row)]
+    longest, longest_columns = functools.reduce(jnp.maximum, [each[slab:] for each in told], jnp.stack([longest, longest_columns]))
+    mine = lax.dynamic_slice_in_dim(table, b * slab, slab, 1)
+    ahead = jnp.arange(chips)[None, :] == (chip + jnp.arange(1, chips)[:, None]) % chips
+    lists = list(jnp.sum(jnp.where(ahead[:, :, None], mine[None], 0), axis=1)) + [each[:slab] for each in told]
+    places = places_in_lists(jnp.stack(lists), slab).astype(jnp.int32)
+
+    pick = lambda table, ids: jnp.sum(jnp.where(ids[:, None] == jnp.arange(table.size)[None, :], table.reshape(1, -1), 0), axis=1)
+    listed = pick(places_in_lists(wanted[:-1].reshape(-1, slab), slab), local)
+    column_listed = pick(places_in_lists(columns, slab), column)
+    place = lambda inner_place, most: place_of(inner_place, relative, inner, side, live, slab, chips, most)
+    x_place = place(inner, slab)
+
+    def scalars_of(most, most_columns):
+        half = slab + (chips - 1) * most
+        at = place(listed, most)
+        target = jnp.where(live, at, CORES * half)
+        w_column = jnp.where(group == 0, column_inner, slab + (group - 1) * most_columns + column_listed)
+        w_column = jnp.where(live, w_column, 0)
+        rows = [target, column, at, jnp.full_like(at, chip), live, x_place, w_column]
+        return jnp.stack([row.astype(jnp.int32) for row in rows])
+
+    def branch(most):
+        most_columns = slab if most == slab else min(slab, MOST_COLUMNS)
+
+        def run(*state):
+            scalars = scalars_of(most, most_columns)
+            return iterate(most, most_columns, slab, slab, chips, scalars, places, *state)
+
+        return run
+
+    tiers = sorted({min(tier, slab) for tier in TIERS})
+    longest = jnp.where(longest_columns > MOST_COLUMNS, slab, longest)
+    scalars = scalars_of(slab, slab)
+    x_ups, x_downs, col_x, longest, scalars = together(x_ups, x_downs, col_x, longest, scalars)
+    p_mine, p_other = off_slots(scalars, col_x, blocks, slab, slab * chips)
+    state = (samples, blocks, p_diag, col_x, x_own, x_ups, x_downs, p_mine, swap_cores(p_other))
+
+    def choose(tiers, longest, state):
+        if len(tiers) == 1:
+            return branch(tiers[0])(*state)
+        middle = len(tiers) // 2
+        return lax.cond(
+            longest <= tiers[middle - 1],
+            lambda state: choose(tiers[:middle], longest, state),
+            lambda state: choose(tiers[middle:], longest, state),
+            state,
         )
-        if last:
-            blocks = result[0]
-        else:
-            blocks, p_mine, p_other = result
-    return blocks[None, None]
+
+    return choose(tiers, longest, state)[None, None]
 
 
 def solution(mesh):

time: 598 us -> 393 us (0.66)
  waiting for transfers between devices: 404 us -> 197 us
  starting transfers between devices: 100 us -> 75 us
  Pallas kernels: 74.1 us -> 91.3 us
  other arithmetic: 13 us -> 20.2 us
    ppermute x30 -> x6, waiting for transfers between devices: 339 us -> 9.75 us  [pass_on(): lax.ppermute(v, 'col', [(z * CORES + c, z * CORES + c + move) for z in so...]
    ppermute x12 -> x27, waiting for transfers between devices: 50.2 us -> 168 us  [the longest x12 136 us: round_ring(): return lax.ppermute(v, 'col', pairs)]
    ppermute x30 -> x6, starting transfers between devices: 79.7 us -> 12.7 us  [pass_on(): lax.ppermute(v, 'col', [(z * CORES + c, z * CORES + c + move) for z in so...]
    ppermute x12 -> x27, starting transfers between devices: 16.4 us -> 59.2 us  [the longest x12 38 us: round_ring(): return lax.ppermute(v, 'col', pairs)]
    pallas_call x0 -> x2, Pallas kernels: none -> 13.1 us  [combine(): pl.pallas_call(functools.partial(combine_kernel, chips), grid_spec=pltpu....]
    add x12 -> x2, other arithmetic: 11.5 us -> 4.99 us  [iterate(): p_mine[at:at + most] + other[at:at + most]]
    ppermute x23 -> x18, waiting for transfers between devices: 14.4 us -> 18.8 us  [swap_cores(): lax.ppermute(v, 'col', [(i, i ^ 1) for i in range(lax.axis_size('col'))])]
  transfers between devices with their start and end apart: 65 -> 51, of which waited for: 30 -> 24; matrix products, arithmetic and copies ran while one was open for 1% -> 5% of each run, Pallas kernels for 3% -> 6%
where the time goes in v3:
time: 393 us; the launch traced here: 392 us
  waiting for transfers between devices  197 us (50%)
  Pallas kernels  91.3 us (23%)
  starting transfers between devices  75 us (19%)
  other arithmetic  20.2 us (5%)
  local copies, waits for them, and re-layouts  6.76 us (2%)
    ppermute x12, waiting for transfers between devices, round_ring(): return lax.ppermute(v, 'col', pairs)  136 us
    pallas_call x3, Pallas kernels, off_slots(): pl.pallas_call(functools.partial(off_kernel, plan), grid_spec=pltpu.Prefe...  59.7 us
    ppermute x12, starting transfers between devices, round_ring(): return lax.ppermute(v, 'col', pairs)  38 us
    ppermute x18, waiting for transfers between devices, swap_cores(): lax.ppermute(v, 'col', [(i, i ^ 1) for i in range(lax.axis_size('col'))])  18.8 us
    ppermute x13, starting transfers between devices, flip_row(): lax.ppermute(part, 'row', [(i, i ^ bit) for i in range(lax.axis_size('row...  17 us
    ppermute x13, waiting for transfers between devices, flip_row(): lax.ppermute(part, 'row', [(i, i ^ bit) for i in range(lax.axis_size('row...  16.4 us
    ppermute x2, waiting for transfers between devices, line_pattern(): table = jnp.maximum(table, lax.ppermute(table, 'col', pairs))  15.4 us
    pallas_call x2, Pallas kernels, diag_update(): pl.pallas_call(functools.partial(diag_update_kernel, 0.5 / count, last),...  13.9 us
  transfers between devices with their start and end apart: 51, of which 24 were waited for; matrix products, arithmetic and copies ran while one was open for 5% of the time, Pallas kernels for 6%

profile of v3, /device:TPU:0, one launch (start us, length us, event | category | flops | bytes accessed | tf_op | source)
XLA Modules:
  0.0 391.8 jit_solution(3496752381414351734)
XLA Ops:
  5.7 5.6 %collective-permute-start.140 = (f32[32,64,128]{2,1,0:T(8,128)}, f32[32,64,128]{2,1,0:T(8,128)}, u32[]{:S(2)}, u32[]{:S(2)}) collective-permute-start(f32[32,64,128]{2,1,0:T(8,128)} %refs_0_), channel_id=1, source_target_pairs={{0,2},{1,3},{2,4},{3,5},{4,6},{5,7},{8,10},{9,11},{10,12},{11,13},... | collective-permute-start | bytes 3145736 | tf_op jit(solution)/shard_map/ppermute | solution.py:373
  18.3 4.6 %diag_products.1 = f32[32,64,128]{2,1,0:T(8,128)} custom-call(f32[32,64,128]{2,1,0:T(8,128)} %refs_0_, f32[128,128,128]{2,1,0:T(8,128)} %bitcast.126), custom_call_target="tpu_custom_call" | custom-call | flops 201326592 | bytes 8388608 | tf_op jit(solution)/shard_map/diag_products/pallas_call | solution.py:115
  24.7 10.3 %collective-permute-done.143 = s32[4,257]{0,1:T(8,128)S(1)} collective-permute-done((s32[4,257]{0,1:T(8,128)S(1)}, s32[4,257]{0,1:T(8,128)S(1)}, u32[]{:S(2)}, u32[]{:S(2)}) %collective-permute-start.143) | collective-permute-done | bytes 4144 | tf_op jit(solution)/shard_map/ppermute | solution.py:425
  35.1 3.6 collective-permute-start.144
  38.9 5.1 %collective-permute-done.144 = s32[4,257]{0,1:T(8,128)S(1)} collective-permute-done((s32[4,257]{0,1:T(8,128)S(1)}, s32[4,257]{0,1:T(8,128)S(1)}, u32[]{:S(2)}, u32[]{:S(2)}) %collective-permute-start.144) | collective-permute-done | bytes 4144 | tf_op jit(solution)/shard_map/ppermute | solution.py:425
  58.5 3.0 collective-permute-done.153
  70.4 13.9 %off_products.1 = (f32[128,64,128]{2,1,0:T(8,128)}, f32[128,64,128]{2,1,0:T(8,128)}) custom-call(s32[7,96]{1,0:T(8,128)} %stack.130.scalars, f32[32,64,128]{2,1,0:T(8,128)S(1)} %copy-done, f32[32,64,128]{2,1,0:T(8,128)S(1)} %collective-permute-done.145.refs_1_, f32[32,64,128]{2,1,0:T(8,128)S(1)} %collective-permute-done.146.refs_2_, ...), custom_call_target="tpu_custom_call" | custom-call | flops 603979776 | bytes 33554432 | tf_op jit(solution)/shard_map/off_products/pallas_call | solution.py:279
  85.3 7.6 %collective-permute-done.155 = f32[32,64,128]{2,1,0:T(8,128)} collective-permute-done((f32[32,64,128]{2,1,0:T(8,128)S(1)}, f32[32,64,128]{2,1,0:T(8,128)}, u32[]{:S(2)}, u32[]{:S(2)}) %collective-permute-start.155) | collective-permute-done | bytes 1048608 | tf_op jit(solution)/shard_map/ppermute | solution.py:368
  93.4 298.2 %conditional.3 = ((f32[1,1,128,128,128]{4,3,2,1,0:T(8,128)})) conditional(s32[]{:T(128)} %convert_element_type.46, (s32[]{:T(128)}, s32[96]{0:T(128)S(1)}, s32[96]{0:T(128)S(1)}, s32[96]{0:T(128)S(1)}, pred[96]{0:T(512)(128)(4,1)S(1)}, /*index=5*/s32[96]{0:T(128)S(1)}, s32[96]{0:T(128)S(1)}, s32[96]{0:T(128)S(1)}, s32[96]{0:T(128)S(1)}, ...), branch_computations={%region_12.16_spmd, %region_16.20_spmd} | conditional | flops 4229448192 | bytes 337667072 | solution.py:564
  93.6 298.0 %conditional.1 = (f32[1,1,128,128,128]{4,3,2,1,0:T(8,128)}) conditional(s32[]{:T(128)} %convert_element_type.36, (s32[96]{0:T(128)S(1)}, s32[96]{0:T(128)S(1)}, s32[96]{0:T(128)S(1)}, s32[96]{0:T(128)S(1)}, pred[96]{0:T(512)(128)(4,1)S(1)}, /*index=5*/s32[96]{0:T(128)S(1)}, s32[]{:T(128)}, s32[96]{0:T(128)S(1)}, s32[96]{0:T(128)S(1)}, ...), branch_computations={%region_18.18_spmd, %region_19.19_spmd} | conditional | flops 4228695808 | bytes 261172896 | solution.py:564
  105.3 6.4 %collective-permute-done.72.refs_2_ = f32[17,64,128]{2,1,0:T(8,128)S(1)} collective-permute-done((f32[17,64,128]{2,1,0:T(8,128)S(1)}, f32[17,64,128]{2,1,0:T(8,128)S(1)}, u32[]{:S(2)}, u32[]{:S(2)}) %collective-permute-start.72) | collective-permute-done | bytes 557088 | tf_op jit(solution)/shard_map/cond/branch_1_fun/cond/branch_0_fun/ppermute | solution.py:414
  111.7 37.6 %collective-permute-done.71.refs_1_ = f32[17,64,128]{2,1,0:T(8,128)} collective-permute-done((f32[17,64,128]{2,1,0:T(8,128)S(1)}, f32[17,64,128]{2,1,0:T(8,128)}, u32[]{:S(2)}, u32[]{:S(2)}) %collective-permute-start.71) | collective-permute-done | bytes 557088 | tf_op jit(solution)/shard_map/cond/branch_1_fun/cond/branch_0_fun/ppermute | solution.py:414
  149.8 7.8 %collective-permute-done.74.refs_14_ = f32[32,64,128]{2,1,0:T(8,128)} collective-permute-done((f32[32,64,128]{2,1,0:T(8,128)}, f32[32,64,128]{2,1,0:T(8,128)}, u32[]{:S(2)}, u32[]{:S(2)}) %collective-permute-start.74) | collective-permute-done | bytes 1048608 | tf_op jit(solution)/shard_map/cond/branch_1_fun/cond/branch_0_fun/ppermute | solution.py:373
  157.6 6.4 %combine.12 = (f32[32,64,128]{2,1,0:T(8,128)}, f32[17,64,128]{2,1,0:T(8,128)}, f32[17,64,128]{2,1,0:T(8,128)}, f32[17,64,128]{2,1,0:T(8,128)}, f32[24,64,128]{2,...) custom-call(s32[6,32]{1,0:T(8,128)S(1)} %get-tuple-element.620.places, f32[128,64,128]{2,1,0:T(8,128)S(1)} %copy-done.3, ...), custom_call_target="tpu_custom_call" | custom-call | tf_op jit(solution)/shard_map/cond/branch_1_fun/cond/branch_0_fun/combine/pallas_call | solution.py:320
  164.0 3.8 collective-permute-start.76
  171.4 10.3 %collective-permute-done.75.refs_24_ = f32[17,64,128]{2,1,0:T(8,128)} collective-permute-done((f32[17,64,128]{2,1,0:T(8,128)}, f32[17,64,128]{2,1,0:T(8,128)}, u32[]{:S(2)}, u32[]{:S(2)}) %collective-permute-start.75) | collective-permute-done | bytes 557088 | tf_op jit(solution)/shard_map/cond/branch_1_fun/cond/branch_0_fun/ppermute | solution.py:414
  181.7 9.5 %collective-permute-done.76.refs_26_ = f32[17,64,128]{2,1,0:T(8,128)} collective-permute-done((f32[17,64,128]{2,1,0:T(8,128)}, f32[17,64,128]{2,1,0:T(8,128)}, u32[]{:S(2)}, u32[]{:S(2)}) %collective-permute-start.76) | collective-permute-done | bytes 557088 | tf_op jit(solution)/shard_map/cond/branch_1_fun/cond/branch_0_fun/ppermute | solution.py:414
  193.4 11.9 %collective-permute-done.78.refs_7_ = f32[24,64,128]{2,1,0:T(8,128)} collective-permute-done((f32[24,64,128]{2,1,0:T(8,128)}, f32[24,64,128]{2,1,0:T(8,128)}, u32[]{:S(2)}, u32[]{:S(2)}) %collective-permute-start.78) | collective-permute-done | bytes 786464 | tf_op jit(solution)/shard_map/cond/branch_1_fun/cond/branch_0_fun/ppermute | solution.py:340
  205.8 8.7 %diag_update.12 = (f32[128,128,128]{2,1,0:T(8,128)}, f32[32,64,128]{2,1,0:T(8,128)}) custom-call(f32[32,64,128]{2,1,0:T(8,128)S(1)} %get-tuple-element.615.refs_0_, f32[32,64,128]{2,1,0:T(8,128)} %get-tuple-element.632.w_ref.refs_5_.refs_23_, f32[128,128,128]{2,1,0:T(8,128)} %get-tuple-element.639.omega_ref.refs_32_), custom_call_target="tpu_custom_call" | custom-call | flops 603979776 | bytes 8388608 | tf_op jit(solution)/shard_map/cond/branch_1_fun/cond/branch_0_fun/diag_update/pallas_call | solution.py:137
  214.5 4.9 %collective-permute-done.86.refs_25_ = f32[17,64,128]{2,1,0:T(8,128)} collective-permute-done((f32[17,64,128]{2,1,0:T(8,128)}, f32[17,64,128]{2,1,0:T(8,128)}, u32[]{:S(2)}, u32[]{:S(2)}) %collective-permute-start.86) | collective-permute-done | bytes 557088 | tf_op jit(solution)/shard_map/cond/branch_1_fun/cond/branch_0_fun/ppermute | solution.py:414
  223.2 28.0 %off_update.12 = (f32[128,128,128]{2,1,0:T(8,128)}, f32[83,64,128]{2,1,0:T(8,128)}, f32[83,64,128]{2,1,0:T(8,128)}) custom-call(s32[7,96]{1,0:T(8,128)} %stack.110.scalars, f32[32,64,128]{2,1,0:T(8,128)S(1)} %get-tuple-element.615.refs_0_, f32[32,64,128]{2,1,0:T(8,128)S(1)} %get-tuple-element.616.refs_1_, ...), custom_call_target="tpu_custom_call", output_to_operand_aliasing={{0}: (32, {})} | custom-call | flops 1811939328 | bytes 30605312 | tf_op jit(solution)/shard_map/cond/branch_1_fun/cond/branch_0_fun/off_update/pallas_call | solution.py:279
  251.4 5.1 %collective-permute-done.91.other_ref = f32[83,64,128]{2,1,0:T(8,128)S(1)} collective-permute-done((f32[83,64,128]{2,1,0:T(8,128)}, f32[83,64,128]{2,1,0:T(8,128)S(1)}, u32[]{:S(2)}, u32[]{:S(2)}) %collective-permute-start.91) | collective-permute-done | bytes 2719776 | tf_op jit(solution)/shard_map/cond/branch_1_fun/cond/branch_0_fun/ppermute | solution.py:368
  259.2 3.2 collective-permute-start.94
  263.0 12.4 %collective-permute-done.94.refs_2_ = f32[17,64,128]{2,1,0:T(8,128)S(1)} collective-permute-done((f32[17,64,128]{2,1,0:T(8,128)S(1)}, f32[17,64,128]{2,1,0:T(8,128)S(1)}, u32[]{:S(2)}, u32[]{:S(2)}) %collective-permute-start.94) | collective-permute-done | bytes 557088 | tf_op jit(solution)/shard_map/cond/branch_1_fun/cond/branch_0_fun/ppermute | solution.py:414
  275.5 34.0 %collective-permute-done.93.refs_1_ = f32[17,64,128]{2,1,0:T(8,128)S(1)} collective-permute-done((f32[17,64,128]{2,1,0:T(8,128)S(1)}, f32[17,64,128]{2,1,0:T(8,128)S(1)}, u32[]{:S(2)}, u32[]{:S(2)}) %collective-permute-start.93) | collective-permute-done | bytes 557088 | tf_op jit(solution)/shard_map/cond/branch_1_fun/cond/branch_0_fun/ppermute | solution.py:414
  311.1 6.7 %combine.13 = (f32[32,64,128]{2,1,0:T(8,128)}, f32[17,64,128]{2,1,0:T(8,128)}, f32[17,64,128]{2,1,0:T(8,128)}, f32[17,64,128]{2,1,0:T(8,128)}, f32[24,64,128]{2,...) custom-call(s32[6,32]{1,0:T(8,128)S(1)} %get-tuple-element.620.places, ...), custom_call_target="tpu_custom_call" | custom-call | tf_op jit(solution)/shard_map/cond/branch_1_fun/cond/branch_0_fun/combine/pallas_call | solution.py:320
  318.6 3.0 collective-permute-start.96
  325.1 10.3 %collective-permute-done.95.refs_24_ = f32[17,64,128]{2,1,0:T(8,128)S(1)} collective-permute-done((f32[17,64,128]{2,1,0:T(8,128)}, f32[17,64,128]{2,1,0:T(8,128)S(1)}, u32[]{:S(2)}, u32[]{:S(2)}) %collective-permute-start.95) | collective-permute-done | bytes 557088 | tf_op jit(solution)/shard_map/cond/branch_1_fun/cond/branch_0_fun/ppermute | solution.py:414
  335.4 17.9 %collective-permute-start.100 = (f32[17,64,128]{2,1,0:T(8,128)}, f32[17,64,128]{2,1,0:T(8,128)S(1)}, u32[]{:S(2)}, u32[]{:S(2)}) collective-permute-start(f32[17,64,128]{2,1,0:T(8,128)} %get-tuple-element.671), channel_id=1, source_target_pairs={{0,4},{1,5},{2,6},{3,7},{4,0},{5,1},{6,2},{7,3},{8,12},{9,13},{10,... | collective-permute-start | bytes 1671176 | tf_op jit(solution)/shard_map/cond/branch_1_fun/cond/branch_0_fun/ppermute | solution.py:414
  353.3 5.3 %diag_update.13.refs_31_ = f32[128,128,128]{2,1,0:T(8,128)} custom-call(f32[32,64,128]{2,1,0:T(8,128)S(1)} %get-tuple-element.615.refs_0_, f32[32,64,128]{2,1,0:T(8,128)} %get-tuple-element.660.w_ref.refs_5_.refs_23_, f32[128,128,128]{2,1,0:T(8,128)} %get-tuple-element.666.omega_ref.refs_32_), custom_call_target="tpu_custom_call" | custom-call | flops 603979776 | bytes 8388608 | tf_op jit(solution)/shard_map/cond/branch_1_fun/cond/branch_0_fun/diag_update/pallas_call | solution.py:137
  358.6 10.8 %collective-permute-done.100.refs_25_ = f32[17,64,128]{2,1,0:T(8,128)S(1)} collective-permute-done((f32[17,64,128]{2,1,0:T(8,128)}, f32[17,64,128]{2,1,0:T(8,128)S(1)}, u32[]{:S(2)}, u32[]{:S(2)}) %collective-permute-start.100) | collective-permute-done | bytes 557088 | tf_op jit(solution)/shard_map/cond/branch_1_fun/cond/branch_0_fun/ppermute | solution.py:414
  373.8 17.8 %off_update.13 = f32[128,128,128]{2,1,0:T(8,128)} custom-call(s32[7,96]{1,0:T(8,128)} %stack.110.scalars, f32[32,64,128]{2,1,0:T(8,128)S(1)} %get-tuple-element.615.refs_0_, f32[32,64,128]{2,1,0:T(8,128)S(1)} %get-tuple-element.616.refs_1_, f32[32,64,128]{2,1,0:T(8,128)S(1)} %get-tuple-element.617.refs_2_, ...), custom_call_target="tpu_custom_call", output_to_operand_aliasing={{}: (32, {})} | custom-call | flops 1207959552 | bytes 30605312 | tf_op jit(solution)/shard_map/cond/branch_1_fun/cond/branch_0_fun/off_update/pallas_call | solution.py:279
  (185 shorter events, 74.3 us)
Async XLA Ops:
  0.0 44.1 %collective-permute-start.146 = (f32[32,64,128]{2,1,0:T(8,128)}, f32[32,64,128]{2,1,0:T(8,128)S(1)}, u32[]{:S(2)}, u32[]{:S(2)}) collective-permute-start(f32[32,64,128]{2,1,0:T(8,128)} %refs_0_), channel_id=1, source_target_pairs={{0,16},{8,24},{16,0},{24,8},{1,17},{9,25},{17,1},{25,9},{2,18},{10... | collective-permute-start | bytes 3145736 | tf_op jit(solution)/shard_map/ppermute | solution.py:340
  3.0 41.1 %collective-permute-start.145 = (f32[32,64,128]{2,1,0:T(8,128)}, f32[32,64,128]{2,1,0:T(8,128)S(1)}, u32[]{:S(2)}, u32[]{:S(2)}) collective-permute-start(f32[32,64,128]{2,1,0:T(8,128)} %refs_0_), channel_id=1, source_target_pairs={{0,8},{8,0},{16,24},{24,16},{1,9},{9,1},{17,25},{25,17},{2,10},{10... | collective-permute-start | bytes 3145736 | tf_op jit(solution)/shard_map/ppermute | solution.py:340
  4.5 39.7 %collective-permute-start.141 = (f32[32,64,128]{2,1,0:T(8,128)}, f32[32,64,128]{2,1,0:T(8,128)}, u32[]{:S(2)}, u32[]{:S(2)}) collective-permute-start(f32[32,64,128]{2,1,0:T(8,128)} %refs_0_), channel_id=1, source_target_pairs={{2,0},{3,1},{4,2},{5,3},{6,4},{7,5},{10,8},{11,9},{12,10},{13,11},... | collective-permute-start | bytes 3145736 | tf_op jit(solution)/shard_map/ppermute | solution.py:373
  5.7 38.4 %collective-permute-start.140 = (f32[32,64,128]{2,1,0:T(8,128)}, f32[32,64,128]{2,1,0:T(8,128)}, u32[]{:S(2)}, u32[]{:S(2)}) collective-permute-start(f32[32,64,128]{2,1,0:T(8,128)} %refs_0_), channel_id=1, source_target_pairs={{0,2},{1,3},{2,4},{3,5},{4,6},{5,7},{8,10},{9,11},{10,12},{11,13},... | collective-permute-start | bytes 3145736 | tf_op jit(solution)/shard_map/ppermute | solution.py:373
  44.1 24.3 %collective-permute-start.147 = (f32[32,64,128]{2,1,0:T(8,128)}, f32[32,64,128]{2,1,0:T(8,128)}, u32[]{:S(2)}, u32[]{:S(2)}) collective-permute-start(f32[32,64,128]{2,1,0:T(8,128)} %collective-permute-done.140), channel_id=1, source_target_pairs={{2,4},{3,5},{4,6},{5,7},{10,12},{11,13},{12,14},{13,15},{18,20},{1... | collective-permute-start | bytes 3145736 | tf_op jit(solution)/shard_map/ppermute | solution.py:373
  45.8 24.6 %collective-permute-start.148 = (f32[32,64,128]{2,1,0:T(8,128)}, f32[32,64,128]{2,1,0:T(8,128)}, u32[]{:S(2)}, u32[]{:S(2)}) collective-permute-start(f32[32,64,128]{2,1,0:T(8,128)} %collective-permute-done.141), channel_id=1, source_target_pairs={{2,0},{3,1},{4,2},{5,3},{10,8},{11,9},{12,10},{13,11},{18,16},{19,... | collective-permute-start | bytes 3145736 | tf_op jit(solution)/shard_map/ppermute | solution.py:373
  52.2 16.2 %collective-permute-start.150 = (f32[16,64,128]{2,1,0:T(8,128)}, f32[16,64,128]{2,1,0:T(8,128)}, u32[]{:S(2)}, u32[]{:S(2)}) collective-permute-start(f32[16,64,128]{2,1,0:T(8,128)} %slice.209), channel_id=1, source_target_pairs={{0,8},{8,0},{16,24},{24,16},{1,9},{9,1},{17,25},{25,17},{2,10},{10... | collective-permute-start | bytes 1572872 | tf_op jit(solution)/shard_map/ppermute | solution.py:340
  98.4 50.9 %collective-permute-start.71 = (f32[17,64,128]{2,1,0:T(8,128)S(1)}, f32[17,64,128]{2,1,0:T(8,128)}, u32[]{:S(2)}, u32[]{:S(2)}) collective-permute-start(f32[17,64,128]{2,1,0:T(8,128)S(1)} %get-tuple-element.930), channel_id=1, source_target_pairs={{0,4},{1,5},{2,6},{3,7},{4,0},{5,1},{6,2},{7,3},{8,12},{9,13},{10,... | collective-permute-start | bytes 1671176 | tf_op jit(solution)/shard_map/cond/branch_1_fun/cond/branch_0_fun/ppermute | solution.py:414
  100.4 48.9 %collective-permute-start.70 = (f32[17,64,128]{2,1,0:T(8,128)S(1)}, f32[17,64,128]{2,1,0:T(8,128)}, u32[]{:S(2)}, u32[]{:S(2)}) collective-permute-start(f32[17,64,128]{2,1,0:T(8,128)S(1)} %get-tuple-element.931), channel_id=1, source_target_pairs={{0,2},{1,3},{2,4},{3,5},{4,6},{5,7},{6,0},{7,1},{8,10},{9,11},{10,... | collective-permute-start | bytes 1671176 | tf_op jit(solution)/shard_map/cond/branch_1_fun/cond/branch_0_fun/ppermute | solution.py:414
  102.4 47.4 %collective-permute-start.73 = (f32[32,64,128]{2,1,0:T(8,128)}, f32[32,64,128]{2,1,0:T(8,128)}, u32[]{:S(2)}, u32[]{:S(2)}) collective-permute-start(f32[32,64,128]{2,1,0:T(8,128)} %get-tuple-element.624.refs_13_), channel_id=1, source_target_pairs={{4,6},{5,7},{12,14},{13,15},{20,22},{21,23},{28,30},{29,31}} | collective-permute-start | bytes 3145736 | tf_op jit(solution)/shard_map/cond/branch_1_fun/cond/branch_0_fun/ppermute | solution.py:373
  104.0 53.6 %collective-permute-start.74 = (f32[32,64,128]{2,1,0:T(8,128)}, f32[32,64,128]{2,1,0:T(8,128)}, u32[]{:S(2)}, u32[]{:S(2)}) collective-permute-start(f32[32,64,128]{2,1,0:T(8,128)} %get-tuple-element.625.refs_12_), channel_id=1, source_target_pairs={{2,0},{3,1},{10,8},{11,9},{18,16},{19,17},{26,24},{27,25}} | collective-permute-start | bytes 3145736 | tf_op jit(solution)/shard_map/cond/branch_1_fun/cond/branch_0_fun/ppermute | solution.py:373
  111.7 56.2 %collective-permute-start.80 = (f32[32,64,128]{2,1,0:T(8,128)}, f32[32,64,128]{2,1,0:T(8,128)}, u32[]{:S(2)}, u32[]{:S(2)}) collective-permute-start(f32[32,64,128]{2,1,0:T(8,128)} %get-tuple-element.645.refs_10_), channel_id=1, source_target_pairs={{0,1},{1,0},{2,3},{3,2},{4,5},{5,4},{6,7},{7,6},{8,9},{9,8},{10,11... | collective-permute-start | bytes 3145736 | tf_op jit(solution)/shard_map/cond/branch_1_fun/cond/branch_0_fun/ppermute | solution.py:368
  149.3 20.1 %collective-permute-start.81 = (f32[32,64,128]{2,1,0:T(8,128)}, f32[32,64,128]{2,1,0:T(8,128)}, u32[]{:S(2)}, u32[]{:S(2)}) collective-permute-start(f32[32,64,128]{2,1,0:T(8,128)} %get-tuple-element.646.refs_11_), channel_id=1, source_target_pairs={{0,1},{1,0},{2,3},{3,2},{4,5},{5,4},{6,7},{7,6},{8,9},{9,8},{10,11... | collective-permute-start | bytes 3145736 | tf_op jit(solution)/shard_map/cond/branch_1_fun/cond/branch_0_fun/ppermute | solution.py:368
  149.3 21.6 %collective-permute-start.83 = (f32[32,64,128]{2,1,0:T(8,128)}, f32[32,64,128]{2,1,0:T(8,128)}, u32[]{:S(2)}, u32[]{:S(2)}) collective-permute-start(f32[32,64,128]{2,1,0:T(8,128)} %get-tuple-element.624.refs_13_), channel_id=1, source_target_pairs={{0,1},{1,0},{2,3},{3,2},{4,5},{5,4},{6,7},{7,6},{8,9},{9,8},{10,11... | collective-permute-start | bytes 3145736 | tf_op jit(solution)/shard_map/cond/branch_1_fun/cond/branch_0_fun/ppermute | solution.py:368
  164.0 17.6 %collective-permute-start.75 = (f32[17,64,128]{2,1,0:T(8,128)}, f32[17,64,128]{2,1,0:T(8,128)}, u32[]{:S(2)}, u32[]{:S(2)}) collective-permute-start(f32[17,64,128]{2,1,0:T(8,128)} %get-tuple-element.633), channel_id=1, source_target_pairs={{0,2},{1,3},{2,4},{3,5},{4,6},{5,7},{6,0},{7,1},{8,10},{9,11},{10,... | collective-permute-start | bytes 1671176 | tf_op jit(solution)/shard_map/cond/branch_1_fun/cond/branch_0_fun/ppermute | solution.py:414
  164.0 27.1 %collective-permute-start.76 = (f32[17,64,128]{2,1,0:T(8,128)}, f32[17,64,128]{2,1,0:T(8,128)}, u32[]{:S(2)}, u32[]{:S(2)}) collective-permute-start(f32[17,64,128]{2,1,0:T(8,128)} %get-tuple-element.634), channel_id=1, source_target_pairs={{0,6},{1,7},{2,0},{3,1},{4,2},{5,3},{6,4},{7,5},{8,14},{9,15},{10,... | collective-permute-start | bytes 1671176 | tf_op jit(solution)/shard_map/cond/branch_1_fun/cond/branch_0_fun/ppermute | solution.py:414
  167.9 23.3 %collective-permute-start.77 = (f32[24,64,128]{2,1,0:T(8,128)}, f32[24,64,128]{2,1,0:T(8,128)}, u32[]{:S(2)}, u32[]{:S(2)}) collective-permute-start(f32[24,64,128]{2,1,0:T(8,128)} %get-tuple-element.635), channel_id=1, source_target_pairs={{0,8},{8,0},{16,24},{24,16},{1,9},{9,1},{17,25},{25,17},{2,10},{10... | collective-permute-start | bytes 2359304 | tf_op jit(solution)/shard_map/cond/branch_1_fun/cond/branch_0_fun/ppermute | solution.py:340
  169.4 35.9 %collective-permute-start.78 = (f32[24,64,128]{2,1,0:T(8,128)}, f32[24,64,128]{2,1,0:T(8,128)}, u32[]{:S(2)}, u32[]{:S(2)}) collective-permute-start(f32[24,64,128]{2,1,0:T(8,128)} %get-tuple-element.636), channel_id=1, source_target_pairs={{0,16},{8,24},{16,0},{24,8},{1,17},{9,25},{17,1},{25,9},{2,18},{10... | collective-permute-start | bytes 2359304 | tf_op jit(solution)/shard_map/cond/branch_1_fun/cond/branch_0_fun/ppermute | solution.py:340
  170.9 34.4 %collective-permute-start.79 = (f32[24,64,128]{2,1,0:T(8,128)}, f32[24,64,128]{2,1,0:T(8,128)}, u32[]{:S(2)}, u32[]{:S(2)}) collective-permute-start(f32[24,64,128]{2,1,0:T(8,128)} %get-tuple-element.637), channel_id=1, source_target_pairs={{0,24},{8,16},{16,8},{24,0},{1,25},{9,17},{17,9},{25,1},{2,26},{10... | collective-permute-start | bytes 2359304 | tf_op jit(solution)/shard_map/cond/branch_1_fun/cond/branch_0_fun/ppermute | solution.py:340
  181.7 37.7 %collective-permute-start.82 = (f32[32,64,128]{2,1,0:T(8,128)}, f32[32,64,128]{2,1,0:T(8,128)}, u32[]{:S(2)}, u32[]{:S(2)}) collective-permute-start(f32[32,64,128]{2,1,0:T(8,128)} %get-tuple-element.625.refs_12_), channel_id=1, source_target_pairs={{0,1},{1,0},{2,3},{3,2},{4,5},{5,4},{6,7},{7,6},{8,9},{9,8},{10,11... | collective-permute-start | bytes 3145736 | tf_op jit(solution)/shard_map/cond/branch_1_fun/cond/branch_0_fun/ppermute | solution.py:368
  191.2 28.7 %collective-permute-start.87 = (f32[32,64,128]{2,1,0:T(8,128)}, f32[32,64,128]{2,1,0:T(8,128)}, u32[]{:S(2)}, u32[]{:S(2)}) collective-permute-start(f32[32,64,128]{2,1,0:T(8,128)} %get-tuple-element.632.w_ref.refs_5_.refs_23_), channel_id=1, source_target_pairs={{0,1},{1,0},{2,3},{3,2},{4,5},{5,4},{6,7},{7,6},{8,9},{9,8},{10,11... | collective-permute-start | bytes 3145736 | tf_op jit(solution)/shard_map/cond/branch_1_fun/cond/branch_0_fun/ppermute | solution.py:368
  191.2 28.2 %collective-permute-start.86 = (f32[17,64,128]{2,1,0:T(8,128)}, f32[17,64,128]{2,1,0:T(8,128)}, u32[]{:S(2)}, u32[]{:S(2)}) collective-permute-start(f32[17,64,128]{2,1,0:T(8,128)} %get-tuple-element.651), channel_id=1, source_target_pairs={{0,4},{1,5},{2,6},{3,7},{4,0},{5,1},{6,2},{7,3},{8,12},{9,13},{10,... | collective-permute-start | bytes 1671176 | tf_op jit(solution)/shard_map/cond/branch_1_fun/cond/branch_0_fun/ppermute | solution.py:414
  259.2 16.2 %collective-permute-start.94 = (f32[17,64,128]{2,1,0:T(8,128)S(1)}, f32[17,64,128]{2,1,0:T(8,128)S(1)}, u32[]{:S(2)}, u32[]{:S(2)}) collective-permute-start(f32[17,64,128]{2,1,0:T(8,128)S(1)} %get-tuple-element.932), channel_id=1, source_target_pairs={{0,6},{1,7},{2,0},{3,1},{4,2},{5,3},{6,4},{7,5},{8,14},{9,15},{10,... | collective-permute-start | bytes 1671176 | tf_op jit(solution)/shard_map/cond/branch_1_fun/cond/branch_0_fun/ppermute | solution.py:414
  262.4 47.1 %collective-permute-start.93 = (f32[17,64,128]{2,1,0:T(8,128)S(1)}, f32[17,64,128]{2,1,0:T(8,128)S(1)}, u32[]{:S(2)}, u32[]{:S(2)}) collective-permute-start(f32[17,64,128]{2,1,0:T(8,128)S(1)} %get-tuple-element.933), channel_id=1, source_target_pairs={{0,4},{1,5},{2,6},{3,7},{4,0},{5,1},{6,2},{7,3},{8,12},{9,13},{10,... | collective-permute-start | bytes 1671176 | tf_op jit(solution)/shard_map/cond/branch_1_fun/cond/branch_0_fun/ppermute | solution.py:414
  262.4 47.1 %collective-permute-start.92 = (f32[17,64,128]{2,1,0:T(8,128)S(1)}, f32[17,64,128]{2,1,0:T(8,128)S(1)}, u32[]{:S(2)}, u32[]{:S(2)}) collective-permute-start(f32[17,64,128]{2,1,0:T(8,128)S(1)} %get-tuple-element.934), channel_id=1, source_target_pairs={{0,2},{1,3},{2,4},{3,5},{4,6},{5,7},{6,0},{7,1},{8,10},{9,11},{10,... | collective-permute-start | bytes 1671176 | tf_op jit(solution)/shard_map/cond/branch_1_fun/cond/branch_0_fun/ppermute | solution.py:414
  317.8 17.6 %collective-permute-start.95 = (f32[17,64,128]{2,1,0:T(8,128)}, f32[17,64,128]{2,1,0:T(8,128)S(1)}, u32[]{:S(2)}, u32[]{:S(2)}) collective-permute-start(f32[17,64,128]{2,1,0:T(8,128)} %get-tuple-element.661), channel_id=1, source_target_pairs={{0,2},{1,3},{2,4},{3,5},{4,6},{5,7},{6,0},{7,1},{8,10},{9,11},{10,... | collective-permute-start | bytes 1671176 | tf_op jit(solution)/shard_map/cond/branch_1_fun/cond/branch_0_fun/ppermute | solution.py:414
  318.6 34.7 %collective-permute-start.96 = (f32[17,64,128]{2,1,0:T(8,128)}, f32[17,64,128]{2,1,0:T(8,128)S(1)}, u32[]{:S(2)}, u32[]{:S(2)}) collective-permute-start(f32[17,64,128]{2,1,0:T(8,128)} %get-tuple-element.662), channel_id=1, source_target_pairs={{0,6},{1,7},{2,0},{3,1},{4,2},{5,3},{6,4},{7,5},{8,14},{9,15},{10,... | collective-permute-start | bytes 1671176 | tf_op jit(solution)/shard_map/cond/branch_1_fun/cond/branch_0_fun/ppermute | solution.py:414
  321.6 47.8 %collective-permute-start.97 = (f32[24,64,128]{2,1,0:T(8,128)}, f32[24,64,128]{2,1,0:T(8,128)S(1)}, u32[]{:S(2)}, u32[]{:S(2)}) collective-permute-start(f32[24,64,128]{2,1,0:T(8,128)} %get-tuple-element.663), channel_id=1, source_target_pairs={{0,8},{8,0},{16,24},{24,16},{1,9},{9,1},{17,25},{25,17},{2,10},{10... | collective-permute-start | bytes 2359304 | tf_op jit(solution)/shard_map/cond/branch_1_fun/cond/branch_0_fun/ppermute | solution.py:340
  323.1 46.4 %collective-permute-start.98 = (f32[24,64,128]{2,1,0:T(8,128)}, f32[24,64,128]{2,1,0:T(8,128)S(1)}, u32[]{:S(2)}, u32[]{:S(2)}) collective-permute-start(f32[24,64,128]{2,1,0:T(8,128)} %get-tuple-element.664), channel_id=1, source_target_pairs={{0,16},{8,24},{16,0},{24,8},{1,17},{9,25},{17,1},{25,9},{2,18},{10... | collective-permute-start | bytes 2359304 | tf_op jit(solution)/shard_map/cond/branch_1_fun/cond/branch_0_fun/ppermute | solution.py:340
  324.6 44.9 %collective-permute-start.99 = (f32[24,64,128]{2,1,0:T(8,128)}, f32[24,64,128]{2,1,0:T(8,128)S(1)}, u32[]{:S(2)}, u32[]{:S(2)}) collective-permute-start(f32[24,64,128]{2,1,0:T(8,128)} %get-tuple-element.665), channel_id=1, source_target_pairs={{0,24},{8,16},{16,8},{24,0},{1,25},{9,17},{17,9},{25,1},{2,26},{10... | collective-permute-start | bytes 2359304 | tf_op jit(solution)/shard_map/cond/branch_1_fun/cond/branch_0_fun/ppermute | solution.py:340
  335.4 34.0 %collective-permute-start.100 = (f32[17,64,128]{2,1,0:T(8,128)}, f32[17,64,128]{2,1,0:T(8,128)S(1)}, u32[]{:S(2)}, u32[]{:S(2)}) collective-permute-start(f32[17,64,128]{2,1,0:T(8,128)} %get-tuple-element.671), channel_id=1, source_target_pairs={{0,4},{1,5},{2,6},{3,7},{4,0},{5,1},{6,2},{7,3},{8,12},{9,13},{10,... | collective-permute-start | bytes 1671176 | tf_op jit(solution)/shard_map/cond/branch_1_fun/cond/branch_0_fun/ppermute | solution.py:414
  353.3 16.8 %collective-permute-start.101 = (f32[32,64,128]{2,1,0:T(8,128)}, f32[32,64,128]{2,1,0:T(8,128)S(1)}, u32[]{:S(2)}, u32[]{:S(2)}) collective-permute-start(f32[32,64,128]{2,1,0:T(8,128)} %get-tuple-element.660.w_ref.refs_5_.refs_23_), channel_id=1, source_target_pairs={{0,1},{1,0},{2,3},{3,2},{4,5},{5,4},{6,7},{7,6},{8,9},{9,8},{10,11... | collective-permute-start | bytes 3145736 | tf_op jit(solution)/shard_map/cond/branch_1_fun/cond/branch_0_fun/ppermute | solution.py:368
  (36 other events, 496.9 us)

commit v4 on v3

--- a/solution.py
+++ b/solution.py
@@ -1,4 +1,5 @@
 import functools
+import math
 
 import jax
 import jax.numpy as jnp
@@ -10,9 +11,9 @@
 ITERS = 2
 STEP = 0.5
 PENALTY = 0.1
-VMEM_BYTES = 56 * 1024 * 1024
+VMEM_SPARE = 20 * 1024 * 1024
 CORES = 2
-UNROLL = 4
+UNROLL = 8
 TIERS = (15, 17, 19, 1 << 30)
 MOST_COLUMNS = 24
 
@@ -31,16 +32,16 @@
     x_high, x_low = split(x)
     o_high, o_low = split(block)
     count = x.shape[0]
-    both = dot(jnp.concatenate([x_high, x_low], 0), o_high, ((1,), (1,)))
-    return both[:count] + both[count:] + dot(x_high, o_low, ((1,), (1,)))
+    dims = ((1,), (1,))
+    both = dot(o_high, jnp.concatenate([x_high, x_low], 0), dims)
+    return (both[:, :count] + both[:, count:] + dot(o_low, x_high, dims)).T
 
 
 def gradient(left_w, right_x, left_x, right_w):
     a_high, a_low = split(jnp.concatenate([left_w, left_x], 0))
     b_high, b_low = split(jnp.concatenate([right_x, right_w], 0))
     dims = ((0,), (0,))
-    first = dot(jnp.concatenate([a_high, a_low], 0), jnp.concatenate([b_high, b_high], 0), dims)
-    return first + dot(a_high, b_low, dims)
+    return dot(a_high, b_high, dims) + dot(a_low, b_high, dims) + dot(a_high, b_low, dims)
 
 
 def shrink(v):
@@ -94,8 +95,9 @@
     each(x_ref.shape[0], one)
 
 
-def params():
-    return pltpu.CompilerParams(vmem_limit_bytes=VMEM_BYTES)
+def params(*shapes):
+    held = sum(4 * math.prod(shape) for shape in shapes)
+    return pltpu.CompilerParams(vmem_limit_bytes=held + VMEM_SPARE)
 
 
 def cost(slots, dims, passes, extra=0):
@@ -118,7 +120,7 @@
         in_specs=[x_spec, o_spec],
         out_specs=x_spec,
         out_shape=jax.ShapeDtypeStruct(x.shape, jnp.float32),
-        compiler_params=params(),
+        compiler_params=params(*[(2 * size, count, width)] * 2, (2 * size, width, width)),
         cost_estimate=cost(slab, (count, width), 3),
         name="diag_products",
     )(x, omega)
@@ -140,7 +142,7 @@
         in_specs=[x_spec, x_spec, o_spec],
         out_specs=specs,
         out_shape=outs,
-        compiler_params=params(),
+        compiler_params=params(*[(2 * size, count, width)] * 3, *[(2 * size, width, width)] * 2),
         cost_estimate=cost(slab, (count, width), 9),
         name="diag_update",
     )(x, w, omega)
@@ -275,6 +277,7 @@
     scratch.append(pltpu.SemaphoreType.DMA((copies,)))
     if products:
         scratch.append(pltpu.SemaphoreType.DMA((2,)))
+    held = [(4 * size, width, width)] + [each.shape for each in scratch if each.dtype == jnp.float32]
     plan = (update, products, 0.5 / count, size, len(col_x), len(col_w), x_choices, w_choices)
     return pl.pallas_call(
         functools.partial(off_kernel, plan),
@@ -287,7 +290,7 @@
         ),
         out_shape=outs,
         input_output_aliases=aliases,
-        compiler_params=params(),
+        compiler_params=params(*held),
         cost_estimate=cost(off, block, 3 * (2 * update + products), 2 * half * count * width * 4),
         name="off_update" if update else "off_products",
     )(scalars, *operands, omega)
@@ -326,7 +329,7 @@
             out_specs=[whole(n) for n in sizes],
         ),
         out_shape=[jax.ShapeDtypeStruct((n,) + block, jnp.float32) for n in sizes],
-        compiler_params=params(),
+        compiler_params=params(*[(2 * n,) + block for n in sizes], *[(2 * slab,) + block] * 3, *[(2 * most,) + block] * chips),
         name="combine",
     )(places, mine, other, diag, *came)
     return own, sends[: chips - 1], sends[chips - 1 :]
@@ -467,15 +470,10 @@
         w_columns = [from_row(send, d) for d, send in enumerate(column_sends, 1)]
         w_own = (own_w, swap_cores(own_w))
         updated = diag_update(samples, own_w, blocks, last)
-        longest = chips // 2 - 1
-        rest = came[:longest] + came[longest + 1 :]
+        rest, w_columns, updated = together(came[:-1], w_columns, updated)
         if row_x is None:
-            rest, w_columns, updated = together(rest, w_columns, updated)
             row_x = row_parts(x_own, both_cores(x_ups), both_cores(x_downs), slab)
-        else:
-            rest, w_columns, updated = together(rest, w_columns, updated)
-        rest = both_cores(rest)
-        came = rest[:longest] + both_cores([came[longest]]) + rest[longest:]
+        came = both_cores(rest) + both_cores(came[-1:])
         row_w = ring_parts(w_own, came, most)
         state = ([own_w] + w_columns, row_x, row_w, updated[0])
         result = off_slots(scalars, col_x, blocks, slab, half, state, not last)

time: 393 us -> 380 us (0.967)
  starting transfers between devices: 75 us -> 54.9 us
  waiting for transfers between devices: 197 us -> 217 us
  Pallas kernels: 91.3 us -> 71.5 us
    ppermute x12, waiting for transfers between devices: 136 us -> 167 us  [round_ring(): return lax.ppermute(v, 'col', pairs)]
    ppermute x12, starting transfers between devices: 38 us -> 18.6 us  [round_ring(): return lax.ppermute(v, 'col', pairs)]
    ppermute x13, waiting for transfers between devices: 16.4 us -> 5.33 us  [flip_row(): lax.ppermute(part, 'row', [(i, i ^ bit) for i in range(lax.axis_size('row...]
    pallas_call x3, Pallas kernels: 59.7 us -> 52.5 us  [off_slots(): pl.pallas_call(functools.partial(off_kernel, plan), grid_spec=pltpu.Prefe...]
    pallas_call x2, Pallas kernels: 13.9 us -> 6.78 us  [diag_update(): pl.pallas_call(functools.partial(diag_update_kernel, 0.5 / count, last),...]
    pallas_call x2, Pallas kernels: 13.1 us -> 7.35 us  [combine(): pl.pallas_call(functools.partial(combine_kernel, chips), grid_spec=pltpu....]
    cond x30 -> x54, local copies, waits for them, and re-layouts: 2.44 us -> 6.83 us
  transfers between devices with their start and end apart: 51 -> 51, of which waited for: 24 -> 25; matrix products, arithmetic and copies ran while one was open for 5% -> 5% of each run, Pallas kernels for 6% -> 4%
where the time goes in v4:
time: 380 us; the launch traced here: 375 us
  waiting for transfers between devices  217 us (57%)
  Pallas kernels  71.5 us (19%)
  starting transfers between devices  54.9 us (14%)
  other arithmetic  19.6 us (5%)
  local copies, waits for them, and re-layouts  9.89 us (3%)
    ppermute x12, waiting for transfers between devices, round_ring(): return lax.ppermute(v, 'col', pairs)  167 us
    pallas_call x3, Pallas kernels, off_slots(): pl.pallas_call(functools.partial(off_kernel, plan), grid_spec=pltpu.Prefe...  52.5 us
    ppermute x12, starting transfers between devices, round_ring(): return lax.ppermute(v, 'col', pairs)  18.6 us
    ppermute x18, waiting for transfers between devices, swap_cores(): lax.ppermute(v, 'col', [(i, i ^ 1) for i in range(lax.axis_size('col'))])  18.5 us
    ppermute x13, starting transfers between devices, flip_row(): lax.ppermute(part, 'row', [(i, i ^ bit) for i in range(lax.axis_size('row...  17 us
    ppermute x2, waiting for transfers between devices, line_pattern(): table = jnp.maximum(table, lax.ppermute(table, 'col', pairs))  15.1 us
    ppermute x6, starting transfers between devices, pass_on(): lax.ppermute(v, 'col', [(z * CORES + c, z * CORES + c + move) for z in so...  11.8 us
    ppermute x6, waiting for transfers between devices, pass_on(): lax.ppermute(v, 'col', [(z * CORES + c, z * CORES + c + move) for z in so...  10.4 us
  transfers between devices with their start and end apart: 51, of which 25 were waited for; matrix products, arithmetic and copies ran while one was open for 5% of the time, Pallas kernels for 4%

profile of v4, /device:TPU:0, one launch (start us, length us, event | category | flops | bytes accessed | tf_op | source)
XLA Modules:
  0.0 375.3 jit_solution(12412783914704514842)
XLA Ops:
  0.0 3.0 collective-permute-start.146
  5.7 5.6 %collective-permute-start.140 = (f32[32,64,128]{2,1,0:T(8,128)}, f32[32,64,128]{2,1,0:T(8,128)}, u32[]{:S(2)}, u32[]{:S(2)}) collective-permute-start(f32[32,64,128]{2,1,0:T(8,128)} %refs_0_), channel_id=1, source_target_pairs={{0,2},{1,3},{2,4},{3,5},{4,6},{5,7},{8,10},{9,11},{10,12},{11,13},... | collective-permute-start | bytes 3145736 | tf_op jit(solution)/shard_map/ppermute | solution.py:376
  18.3 4.8 %diag_products.1 = f32[32,64,128]{2,1,0:T(8,128)} custom-call(f32[32,64,128]{2,1,0:T(8,128)} %refs_0_, f32[128,128,128]{2,1,0:T(8,128)} %bitcast.128), custom_call_target="tpu_custom_call" | custom-call | flops 201326592 | bytes 8388608 | tf_op jit(solution)/shard_map/diag_products/pallas_call | solution.py:117
  25.0 10.0 %collective-permute-done.143 = s32[4,257]{0,1:T(8,128)S(1)} collective-permute-done((s32[4,257]{0,1:T(8,128)S(1)}, s32[4,257]{0,1:T(8,128)S(1)}, u32[]{:S(2)}, u32[]{:S(2)}) %collective-permute-start.143) | collective-permute-done | bytes 4144 | tf_op jit(solution)/shard_map/ppermute | solution.py:428
  35.1 3.6 collective-permute-start.144
  38.9 5.1 %collective-permute-done.144 = s32[4,257]{0,1:T(8,128)S(1)} collective-permute-done((s32[4,257]{0,1:T(8,128)S(1)}, s32[4,257]{0,1:T(8,128)S(1)}, u32[]{:S(2)}, u32[]{:S(2)}) %collective-permute-start.144) | collective-permute-done | bytes 4144 | tf_op jit(solution)/shard_map/ppermute | solution.py:428
  58.1 3.3 collective-permute-done.153
  70.5 14.6 %off_products.1 = (f32[128,64,128]{2,1,0:T(8,128)}, f32[128,64,128]{2,1,0:T(8,128)}) custom-call(s32[7,96]{1,0:T(8,128)S(1)} %stack.130.scalars, f32[32,64,128]{2,1,0:T(8,128)S(1)} %copy-done.48, f32[32,64,128]{2,1,0:T(8,128)} %copy-done.68, f32[32,64,128]{2,1,0:T(8,128)S(1)} %collective-permute-done.146.refs_2_, ...), custom_call_target="tpu_custom_call" | custom-call | flops 603979776 | bytes 33554432 | tf_op jit(solution)/shard_map/off_products/pallas_call | solution.py:282
  86.0 7.6 %collective-permute-done.155 = f32[32,64,128]{2,1,0:T(8,128)} collective-permute-done((f32[32,64,128]{2,1,0:T(8,128)S(1)}, f32[32,64,128]{2,1,0:T(8,128)}, u32[]{:S(2)}, u32[]{:S(2)}) %collective-permute-start.155) | collective-permute-done | bytes 1048608 | tf_op jit(solution)/shard_map/ppermute | solution.py:371
  94.2 280.9 %conditional.3 = ((f32[1,1,128,128,128]{4,3,2,1,0:T(8,128)})) conditional(s32[]{:T(128)} %convert_element_type.46, (s32[]{:T(128)}, s32[96]{0:T(128)S(1)}, s32[96]{0:T(128)S(1)}, s32[96]{0:T(128)S(1)}, pred[96]{0:T(512)(128)(4,1)S(1)}, /*index=5*/s32[96]{0:T(128)S(1)}, s32[96]{0:T(128)S(1)}, s32[96]{0:T(128)S(1)}, s32[96]{0:T(128)S(1)}, ...), branch_computations={%region_12.16_spmd, %region_16.20_spmd} | conditional | flops 4229448192 | bytes 467701760 | solution.py:562
  94.4 280.3 %conditional.1 = (f32[1,1,128,128,128]{4,3,2,1,0:T(8,128)}) conditional(s32[]{:T(128)} %convert_element_type.36, (s32[96]{0:T(128)S(1)}, s32[96]{0:T(128)S(1)}, s32[96]{0:T(128)S(1)}, s32[96]{0:T(128)S(1)}, pred[96]{0:T(512)(128)(4,1)S(1)}, /*index=5*/s32[96]{0:T(128)S(1)}, s32[]{:T(128)}, s32[96]{0:T(128)S(1)}, s32[96]{0:T(128)S(1)}, ...), branch_computations={%region_18.18_spmd, %region_19.19_spmd} | conditional | flops 4228695808 | bytes 406401088 | solution.py:562
  94.4 3.1 slice_add_fusion.15
  105.4 7.6 %collective-permute-done.72.refs_2_ = f32[17,64,128]{2,1,0:T(8,128)S(1)} collective-permute-done((f32[17,64,128]{2,1,0:T(8,128)S(1)}, f32[17,64,128]{2,1,0:T(8,128)S(1)}, u32[]{:S(2)}, u32[]{:S(2)}) %collective-permute-start.72) | collective-permute-done | bytes 557088 | tf_op jit(solution)/shard_map/cond/branch_1_fun/cond/branch_0_fun/ppermute | solution.py:417
  113.0 37.2 %collective-permute-done.71.refs_1_ = f32[17,64,128]{2,1,0:T(8,128)S(1)} collective-permute-done((f32[17,64,128]{2,1,0:T(8,128)S(1)}, f32[17,64,128]{2,1,0:T(8,128)S(1)}, u32[]{:S(2)}, u32[]{:S(2)}) %collective-permute-start.71) | collective-permute-done | bytes 557088 | tf_op jit(solution)/shard_map/cond/branch_1_fun/cond/branch_0_fun/ppermute | solution.py:417
  150.7 7.9 %collective-permute-done.74.refs_14_ = f32[32,64,128]{2,1,0:T(8,128)S(1)} collective-permute-done((f32[32,64,128]{2,1,0:T(8,128)}, f32[32,64,128]{2,1,0:T(8,128)S(1)}, u32[]{:S(2)}, u32[]{:S(2)}) %collective-permute-start.74) | collective-permute-done | bytes 1048608 | tf_op jit(solution)/shard_map/cond/branch_1_fun/cond/branch_0_fun/ppermute | solution.py:376
  158.6 4.3 %combine.12 = (f32[32,64,128]{2,1,0:T(8,128)S(1)}, f32[17,64,128]{2,1,0:T(8,128)S(1)}, f32[17,64,128]{2,1,0:T(8,128)S(1)}, f32[17,64,128]{2,1,0:T(8,128)S(1)}, f...) custom-call(s32[6,32]{1,0:T(8,128)S(1)} %get-tuple-element.620.places, ...), custom_call_target="tpu_custom_call" | custom-call | tf_op jit(solution)/shard_map/cond/branch_1_fun/cond/branch_0_fun/combine/pallas_call | solution.py:323
  163.0 4.6 %collective-permute-start.76 = (f32[17,64,128]{2,1,0:T(8,128)S(1)}, f32[17,64,128]{2,1,0:T(8,128)}, u32[]{:S(2)}, u32[]{:S(2)}) collective-permute-start(f32[17,64,128]{2,1,0:T(8,128)S(1)} %get-tuple-element.634), channel_id=1, source_target_pairs={{0,4},{1,5},{2,6},{3,7},{4,0},{5,1},{6,2},{7,3},{8,12},{9,13},{10,... | collective-permute-start | bytes 1671176 | tf_op jit(solution)/shard_map/cond/branch_1_fun/cond/branch_0_fun/ppermute | solution.py:417
  171.1 9.6 %collective-permute-done.75.refs_24_ = f32[17,64,128]{2,1,0:T(8,128)} collective-permute-done((f32[17,64,128]{2,1,0:T(8,128)S(1)}, f32[17,64,128]{2,1,0:T(8,128)}, u32[]{:S(2)}, u32[]{:S(2)}) %collective-permute-start.75) | collective-permute-done | bytes 557088 | tf_op jit(solution)/shard_map/cond/branch_1_fun/cond/branch_0_fun/ppermute | solution.py:417
  180.7 23.2 %collective-permute-done.76.refs_25_ = f32[17,64,128]{2,1,0:T(8,128)} collective-permute-done((f32[17,64,128]{2,1,0:T(8,128)S(1)}, f32[17,64,128]{2,1,0:T(8,128)}, u32[]{:S(2)}, u32[]{:S(2)}) %collective-permute-start.76) | collective-permute-done | bytes 557088 | tf_op jit(solution)/shard_map/cond/branch_1_fun/cond/branch_0_fun/ppermute | solution.py:417
  205.9 4.0 %diag_update.12 = (f32[128,128,128]{2,1,0:T(8,128)S(1)}, f32[32,64,128]{2,1,0:T(8,128)S(1)}) custom-call(f32[32,64,128]{2,1,0:T(8,128)S(1)} %copy-done.55, f32[32,64,128]{2,1,0:T(8,128)S(1)} %get-tuple-element.632.w_ref.refs_5_.refs_23_, f32[128,128,128]{2,1,0:T(8,128)S(1)} %bitcast.135), custom_call_target="tpu_custom_call" | custom-call | flops 603979776 | bytes 8388608 | tf_op jit(solution)/shard_map/cond/branch_1_fun/cond/branch_0_fun/diag_update/pallas_call | solution.py:139
  209.9 3.2 copy-done.3
  214.1 4.8 %collective-permute-done.86.refs_26_ = f32[17,64,128]{2,1,0:T(8,128)} collective-permute-done((f32[17,64,128]{2,1,0:T(8,128)S(1)}, f32[17,64,128]{2,1,0:T(8,128)}, u32[]{:S(2)}, u32[]{:S(2)}) %collective-permute-start.86) | collective-permute-done | bytes 557088 | tf_op jit(solution)/shard_map/cond/branch_1_fun/cond/branch_0_fun/ppermute | solution.py:417
  224.0 24.0 %off_update.12 = (f32[128,128,128]{2,1,0:T(8,128)}, f32[83,64,128]{2,1,0:T(8,128)}, f32[83,64,128]{2,1,0:T(8,128)}) custom-call(s32[7,96]{1,0:T(8,128)S(1)} %stack.110.scalars, f32[32,64,128]{2,1,0:T(8,128)} %copy-done.54, f32[32,64,128]{2,1,0:T(8,128)} %get-tuple-element.616.refs_1_, f32[32,64,128]{2,1,0:T(8,128)} %copy-done.65, ...), custom_call_target="tpu_custom_call", output_to_operand_aliasing={{0}: (32, {})} | custom-call | flops 1811939328 | bytes 30605312 | tf_op jit(solution)/shard_map/cond/branch_1_fun/cond/branch_0_fun/off_update/pallas_call | solution.py:282
  248.2 5.1 %collective-permute-done.91.other_ref = f32[83,64,128]{2,1,0:T(8,128)S(1)} collective-permute-done((f32[83,64,128]{2,1,0:T(8,128)}, f32[83,64,128]{2,1,0:T(8,128)S(1)}, u32[]{:S(2)}, u32[]{:S(2)}) %collective-permute-start.91) | collective-permute-done | bytes 2719776 | tf_op jit(solution)/shard_map/cond/branch_1_fun/cond/branch_0_fun/ppermute | solution.py:371
  258.6 13.5 %collective-permute-done.94.refs_2_ = f32[17,64,128]{2,1,0:T(8,128)S(1)} collective-permute-done((f32[17,64,128]{2,1,0:T(8,128)S(1)}, f32[17,64,128]{2,1,0:T(8,128)S(1)}, u32[]{:S(2)}, u32[]{:S(2)}) %collective-permute-start.94) | collective-permute-done | bytes 557088 | tf_op jit(solution)/shard_map/cond/branch_1_fun/cond/branch_0_fun/ppermute | solution.py:417
  272.1 32.6 %collective-permute-done.93.refs_1_ = f32[17,64,128]{2,1,0:T(8,128)S(1)} collective-permute-done((f32[17,64,128]{2,1,0:T(8,128)S(1)}, f32[17,64,128]{2,1,0:T(8,128)S(1)}, u32[]{:S(2)}, u32[]{:S(2)}) %collective-permute-start.93) | collective-permute-done | bytes 557088 | tf_op jit(solution)/shard_map/cond/branch_1_fun/cond/branch_0_fun/ppermute | solution.py:417
  304.7 3.0 combine.13
  315.1 10.3 %collective-permute-done.95.refs_24_ = f32[17,64,128]{2,1,0:T(8,128)S(1)} collective-permute-done((f32[17,64,128]{2,1,0:T(8,128)}, f32[17,64,128]{2,1,0:T(8,128)S(1)}, u32[]{:S(2)}, u32[]{:S(2)}) %collective-permute-start.95) | collective-permute-done | bytes 557088 | tf_op jit(solution)/shard_map/cond/branch_1_fun/cond/branch_0_fun/ppermute | solution.py:417
  325.4 22.1 %collective-permute-done.96.refs_25_ = f32[17,64,128]{2,1,0:T(8,128)S(1)} collective-permute-done((f32[17,64,128]{2,1,0:T(8,128)S(1)}, f32[17,64,128]{2,1,0:T(8,128)S(1)}, u32[]{:S(2)}, u32[]{:S(2)}) %collective-permute-start.96) | collective-permute-done | bytes 557088 | tf_op jit(solution)/shard_map/cond/branch_1_fun/cond/branch_0_fun/ppermute | solution.py:417
  347.6 2.8 diag_update.13.refs_31_
  350.4 6.5 %collective-permute-done.100.refs_26_ = f32[17,64,128]{2,1,0:T(8,128)S(1)} collective-permute-done((f32[17,64,128]{2,1,0:T(8,128)S(1)}, f32[17,64,128]{2,1,0:T(8,128)S(1)}, u32[]{:S(2)}, u32[]{:S(2)}) %collective-permute-start.100) | collective-permute-done | bytes 557088 | tf_op jit(solution)/shard_map/cond/branch_1_fun/cond/branch_0_fun/ppermute | solution.py:417
  360.5 13.9 %off_update.13 = f32[128,128,128]{2,1,0:T(8,128)} custom-call(s32[7,96]{1,0:T(8,128)S(1)} %stack.110.scalars, f32[32,64,128]{2,1,0:T(8,128)S(1)} %copy-done.57, f32[32,64,128]{2,1,0:T(8,128)} %get-tuple-element.616.refs_1_, f32[32,64,128]{2,1,0:T(8,128)} %copy-done.65, f32[16,64,128]{2,1,0:T(8,128)} %get-tuple-element.618.refs_3_, ...), custom_call_target="tpu_custom_call", output_to_operand_aliasing={{}: (32, {})} | custom-call | flops 1207959552 | bytes 30605312 | tf_op jit(solution)/shard_map/cond/branch_1_fun/cond/branch_0_fun/off_update/pallas_call | solution.py:282
  (212 shorter events, 71.7 us)
Async XLA Ops:
  0.0 44.1 %collective-permute-start.146 = (f32[32,64,128]{2,1,0:T(8,128)}, f32[32,64,128]{2,1,0:T(8,128)S(1)}, u32[]{:S(2)}, u32[]{:S(2)}) collective-permute-start(f32[32,64,128]{2,1,0:T(8,128)} %refs_0_), channel_id=1, source_target_pairs={{0,16},{8,24},{16,0},{24,8},{1,17},{9,25},{17,1},{25,9},{2,18},{10... | collective-permute-start | bytes 3145736 | tf_op jit(solution)/shard_map/ppermute | solution.py:343
  3.0 41.2 %collective-permute-start.145 = (f32[32,64,128]{2,1,0:T(8,128)}, f32[32,64,128]{2,1,0:T(8,128)S(1)}, u32[]{:S(2)}, u32[]{:S(2)}) collective-permute-start(f32[32,64,128]{2,1,0:T(8,128)} %refs_0_), channel_id=1, source_target_pairs={{0,8},{8,0},{16,24},{24,16},{1,9},{9,1},{17,25},{25,17},{2,10},{10... | collective-permute-start | bytes 3145736 | tf_op jit(solution)/shard_map/ppermute | solution.py:343
  4.5 39.7 %collective-permute-start.141 = (f32[32,64,128]{2,1,0:T(8,128)}, f32[32,64,128]{2,1,0:T(8,128)}, u32[]{:S(2)}, u32[]{:S(2)}) collective-permute-start(f32[32,64,128]{2,1,0:T(8,128)} %refs_0_), channel_id=1, source_target_pairs={{2,0},{3,1},{4,2},{5,3},{6,4},{7,5},{10,8},{11,9},{12,10},{13,11},... | collective-permute-start | bytes 3145736 | tf_op jit(solution)/shard_map/ppermute | solution.py:376
  5.7 38.4 %collective-permute-start.140 = (f32[32,64,128]{2,1,0:T(8,128)}, f32[32,64,128]{2,1,0:T(8,128)}, u32[]{:S(2)}, u32[]{:S(2)}) collective-permute-start(f32[32,64,128]{2,1,0:T(8,128)} %refs_0_), channel_id=1, source_target_pairs={{0,2},{1,3},{2,4},{3,5},{4,6},{5,7},{8,10},{9,11},{10,12},{11,13},... | collective-permute-start | bytes 3145736 | tf_op jit(solution)/shard_map/ppermute | solution.py:376
  44.2 23.8 %collective-permute-start.147 = (f32[32,64,128]{2,1,0:T(8,128)}, f32[32,64,128]{2,1,0:T(8,128)}, u32[]{:S(2)}, u32[]{:S(2)}) collective-permute-start(f32[32,64,128]{2,1,0:T(8,128)} %collective-permute-done.140), channel_id=1, source_target_pairs={{2,4},{3,5},{4,6},{5,7},{10,12},{11,13},{12,14},{13,15},{18,20},{1... | collective-permute-start | bytes 3145736 | tf_op jit(solution)/shard_map/ppermute | solution.py:376
  45.8 24.6 %collective-permute-start.148 = (f32[32,64,128]{2,1,0:T(8,128)}, f32[32,64,128]{2,1,0:T(8,128)}, u32[]{:S(2)}, u32[]{:S(2)}) collective-permute-start(f32[32,64,128]{2,1,0:T(8,128)} %collective-permute-done.141), channel_id=1, source_target_pairs={{2,0},{3,1},{4,2},{5,3},{10,8},{11,9},{12,10},{13,11},{18,16},{19,... | collective-permute-start | bytes 3145736 | tf_op jit(solution)/shard_map/ppermute | solution.py:376
  52.1 15.9 %collective-permute-start.150 = (f32[16,64,128]{2,1,0:T(8,128)}, f32[16,64,128]{2,1,0:T(8,128)}, u32[]{:S(2)}, u32[]{:S(2)}) collective-permute-start(f32[16,64,128]{2,1,0:T(8,128)} %slice.209), channel_id=1, source_target_pairs={{0,8},{8,0},{16,24},{24,16},{1,9},{9,1},{17,25},{25,17},{2,10},{10... | collective-permute-start | bytes 1572872 | tf_op jit(solution)/shard_map/ppermute | solution.py:343
  97.5 15.5 %collective-permute-start.72 = (f32[17,64,128]{2,1,0:T(8,128)S(1)}, f32[17,64,128]{2,1,0:T(8,128)S(1)}, u32[]{:S(2)}, u32[]{:S(2)}) collective-permute-start(f32[17,64,128]{2,1,0:T(8,128)S(1)} %get-tuple-element.929), channel_id=1, source_target_pairs={{0,6},{1,7},{2,0},{3,1},{4,2},{5,3},{6,4},{7,5},{8,14},{9,15},{10,... | collective-permute-start | bytes 1671176 | tf_op jit(solution)/shard_map/cond/branch_1_fun/cond/branch_0_fun/ppermute | solution.py:417
  99.4 50.8 %collective-permute-start.71 = (f32[17,64,128]{2,1,0:T(8,128)S(1)}, f32[17,64,128]{2,1,0:T(8,128)S(1)}, u32[]{:S(2)}, u32[]{:S(2)}) collective-permute-start(f32[17,64,128]{2,1,0:T(8,128)S(1)} %get-tuple-element.930), channel_id=1, source_target_pairs={{0,4},{1,5},{2,6},{3,7},{4,0},{5,1},{6,2},{7,3},{8,12},{9,13},{10,... | collective-permute-start | bytes 1671176 | tf_op jit(solution)/shard_map/cond/branch_1_fun/cond/branch_0_fun/ppermute | solution.py:417
  101.4 48.8 %collective-permute-start.70 = (f32[17,64,128]{2,1,0:T(8,128)S(1)}, f32[17,64,128]{2,1,0:T(8,128)S(1)}, u32[]{:S(2)}, u32[]{:S(2)}) collective-permute-start(f32[17,64,128]{2,1,0:T(8,128)S(1)} %get-tuple-element.931), channel_id=1, source_target_pairs={{0,2},{1,3},{2,4},{3,5},{4,6},{5,7},{6,0},{7,1},{8,10},{9,11},{10,... | collective-permute-start | bytes 1671176 | tf_op jit(solution)/shard_map/cond/branch_1_fun/cond/branch_0_fun/ppermute | solution.py:417
  103.4 47.3 %collective-permute-start.73 = (f32[32,64,128]{2,1,0:T(8,128)}, f32[32,64,128]{2,1,0:T(8,128)S(1)}, u32[]{:S(2)}, u32[]{:S(2)}) collective-permute-start(f32[32,64,128]{2,1,0:T(8,128)} %get-tuple-element.624.refs_13_), channel_id=1, source_target_pairs={{4,6},{5,7},{12,14},{13,15},{20,22},{21,23},{28,30},{29,31}} | collective-permute-start | bytes 3145736 | tf_op jit(solution)/shard_map/cond/branch_1_fun/cond/branch_0_fun/ppermute | solution.py:376
  104.1 54.5 %collective-permute-start.74 = (f32[32,64,128]{2,1,0:T(8,128)}, f32[32,64,128]{2,1,0:T(8,128)S(1)}, u32[]{:S(2)}, u32[]{:S(2)}) collective-permute-start(f32[32,64,128]{2,1,0:T(8,128)} %get-tuple-element.625.refs_12_), channel_id=1, source_target_pairs={{2,0},{3,1},{10,8},{11,9},{18,16},{19,17},{26,24},{27,25}} | collective-permute-start | bytes 3145736 | tf_op jit(solution)/shard_map/cond/branch_1_fun/cond/branch_0_fun/ppermute | solution.py:376
  113.0 54.6 %collective-permute-start.80 = (f32[32,64,128]{2,1,0:T(8,128)}, f32[32,64,128]{2,1,0:T(8,128)S(1)}, u32[]{:S(2)}, u32[]{:S(2)}) collective-permute-start(f32[32,64,128]{2,1,0:T(8,128)} %get-tuple-element.645.refs_10_), channel_id=1, source_target_pairs={{0,1},{1,0},{2,3},{3,2},{4,5},{5,4},{6,7},{7,6},{8,9},{9,8},{10,11... | collective-permute-start | bytes 3145736 | tf_op jit(solution)/shard_map/cond/branch_1_fun/cond/branch_0_fun/ppermute | solution.py:371
  150.2 18.9 %collective-permute-start.81 = (f32[32,64,128]{2,1,0:T(8,128)}, f32[32,64,128]{2,1,0:T(8,128)}, u32[]{:S(2)}, u32[]{:S(2)}) collective-permute-start(f32[32,64,128]{2,1,0:T(8,128)} %get-tuple-element.646.refs_11_), channel_id=1, source_target_pairs={{0,1},{1,0},{2,3},{3,2},{4,5},{5,4},{6,7},{7,6},{8,9},{9,8},{10,11... | collective-permute-start | bytes 3145736 | tf_op jit(solution)/shard_map/cond/branch_1_fun/cond/branch_0_fun/ppermute | solution.py:371
  150.2 20.4 %collective-permute-start.83 = (f32[32,64,128]{2,1,0:T(8,128)}, f32[32,64,128]{2,1,0:T(8,128)}, u32[]{:S(2)}, u32[]{:S(2)}) collective-permute-start(f32[32,64,128]{2,1,0:T(8,128)} %get-tuple-element.624.refs_13_), channel_id=1, source_target_pairs={{0,1},{1,0},{2,3},{3,2},{4,5},{5,4},{6,7},{7,6},{8,9},{9,8},{10,11... | collective-permute-start | bytes 3145736 | tf_op jit(solution)/shard_map/cond/branch_1_fun/cond/branch_0_fun/ppermute | solution.py:371
  162.9 17.7 %collective-permute-start.75 = (f32[17,64,128]{2,1,0:T(8,128)S(1)}, f32[17,64,128]{2,1,0:T(8,128)}, u32[]{:S(2)}, u32[]{:S(2)}) collective-permute-start(f32[17,64,128]{2,1,0:T(8,128)S(1)} %get-tuple-element.633), channel_id=1, source_target_pairs={{0,2},{1,3},{2,4},{3,5},{4,6},{5,7},{6,0},{7,1},{8,10},{9,11},{10,... | collective-permute-start | bytes 1671176 | tf_op jit(solution)/shard_map/cond/branch_1_fun/cond/branch_0_fun/ppermute | solution.py:417
  163.0 40.8 %collective-permute-start.76 = (f32[17,64,128]{2,1,0:T(8,128)S(1)}, f32[17,64,128]{2,1,0:T(8,128)}, u32[]{:S(2)}, u32[]{:S(2)}) collective-permute-start(f32[17,64,128]{2,1,0:T(8,128)S(1)} %get-tuple-element.634), channel_id=1, source_target_pairs={{0,4},{1,5},{2,6},{3,7},{4,0},{5,1},{6,2},{7,3},{8,12},{9,13},{10,... | collective-permute-start | bytes 1671176 | tf_op jit(solution)/shard_map/cond/branch_1_fun/cond/branch_0_fun/ppermute | solution.py:417
  167.6 36.2 %collective-permute-start.77 = (f32[24,64,128]{2,1,0:T(8,128)S(1)}, f32[24,64,128]{2,1,0:T(8,128)S(1)}, u32[]{:S(2)}, u32[]{:S(2)}) collective-permute-start(f32[24,64,128]{2,1,0:T(8,128)S(1)} %get-tuple-element.635), channel_id=1, source_target_pairs={{0,8},{8,0},{16,24},{24,16},{1,9},{9,1},{17,25},{25,17},{2,10},{10... | collective-permute-start | bytes 2359304 | tf_op jit(solution)/shard_map/cond/branch_1_fun/cond/branch_0_fun/ppermute | solution.py:343
  169.1 35.6 %collective-permute-start.78 = (f32[24,64,128]{2,1,0:T(8,128)S(1)}, f32[24,64,128]{2,1,0:T(8,128)S(1)}, u32[]{:S(2)}, u32[]{:S(2)}) collective-permute-start(f32[24,64,128]{2,1,0:T(8,128)S(1)} %get-tuple-element.636), channel_id=1, source_target_pairs={{0,16},{8,24},{16,0},{24,8},{1,17},{9,25},{17,1},{25,9},{2,18},{10... | collective-permute-start | bytes 2359304 | tf_op jit(solution)/shard_map/cond/branch_1_fun/cond/branch_0_fun/ppermute | solution.py:343
  170.6 34.3 %collective-permute-start.79 = (f32[24,64,128]{2,1,0:T(8,128)S(1)}, f32[24,64,128]{2,1,0:T(8,128)S(1)}, u32[]{:S(2)}, u32[]{:S(2)}) collective-permute-start(f32[24,64,128]{2,1,0:T(8,128)S(1)} %get-tuple-element.637), channel_id=1, source_target_pairs={{0,24},{8,16},{16,8},{24,0},{1,25},{9,17},{17,9},{25,1},{2,26},{10... | collective-permute-start | bytes 2359304 | tf_op jit(solution)/shard_map/cond/branch_1_fun/cond/branch_0_fun/ppermute | solution.py:343
  180.7 38.3 %collective-permute-start.82 = (f32[32,64,128]{2,1,0:T(8,128)}, f32[32,64,128]{2,1,0:T(8,128)S(1)}, u32[]{:S(2)}, u32[]{:S(2)}) collective-permute-start(f32[32,64,128]{2,1,0:T(8,128)} %get-tuple-element.625.refs_12_), channel_id=1, source_target_pairs={{0,1},{1,0},{2,3},{3,2},{4,5},{5,4},{6,7},{7,6},{8,9},{9,8},{10,11... | collective-permute-start | bytes 3145736 | tf_op jit(solution)/shard_map/cond/branch_1_fun/cond/branch_0_fun/ppermute | solution.py:371
  203.8 15.7 %collective-permute-start.87 = (f32[32,64,128]{2,1,0:T(8,128)S(1)}, f32[32,64,128]{2,1,0:T(8,128)S(1)}, u32[]{:S(2)}, u32[]{:S(2)}) collective-permute-start(f32[32,64,128]{2,1,0:T(8,128)S(1)} %get-tuple-element.632.w_ref.refs_5_.refs_23_), channel_id=1, source_target_pairs={{0,1},{1,0},{2,3},{3,2},{4,5},{5,4},{6,7},{7,6},{8,9},{9,8},{10,11... | collective-permute-start | bytes 3145736 | tf_op jit(solution)/shard_map/cond/branch_1_fun/cond/branch_0_fun/ppermute | solution.py:371
  204.7 15.7 %collective-permute-start.84 = (f32[32,64,128]{2,1,0:T(8,128)S(1)}, f32[32,64,128]{2,1,0:T(8,128)}, u32[]{:S(2)}, u32[]{:S(2)}) collective-permute-start(f32[32,64,128]{2,1,0:T(8,128)S(1)} %collective-permute-done.74.refs_14_), channel_id=1, source_target_pairs={{0,1},{1,0},{2,3},{3,2},{4,5},{5,4},{6,7},{7,6},{8,9},{9,8},{10,11... | collective-permute-start | bytes 3145736 | tf_op jit(solution)/shard_map/cond/branch_1_fun/cond/branch_0_fun/ppermute | solution.py:371
  255.3 16.8 %collective-permute-start.94 = (f32[17,64,128]{2,1,0:T(8,128)S(1)}, f32[17,64,128]{2,1,0:T(8,128)S(1)}, u32[]{:S(2)}, u32[]{:S(2)}) collective-permute-start(f32[17,64,128]{2,1,0:T(8,128)S(1)} %get-tuple-element.932), channel_id=1, source_target_pairs={{0,6},{1,7},{2,0},{3,1},{4,2},{5,3},{6,4},{7,5},{8,14},{9,15},{10,... | collective-permute-start | bytes 1671176 | tf_op jit(solution)/shard_map/cond/branch_1_fun/cond/branch_0_fun/ppermute | solution.py:417
  258.0 46.7 %collective-permute-start.93 = (f32[17,64,128]{2,1,0:T(8,128)S(1)}, f32[17,64,128]{2,1,0:T(8,128)S(1)}, u32[]{:S(2)}, u32[]{:S(2)}) collective-permute-start(f32[17,64,128]{2,1,0:T(8,128)S(1)} %get-tuple-element.933), channel_id=1, source_target_pairs={{0,4},{1,5},{2,6},{3,7},{4,0},{5,1},{6,2},{7,3},{8,12},{9,13},{10,... | collective-permute-start | bytes 1671176 | tf_op jit(solution)/shard_map/cond/branch_1_fun/cond/branch_0_fun/ppermute | solution.py:417
  258.0 46.7 %collective-permute-start.92 = (f32[17,64,128]{2,1,0:T(8,128)S(1)}, f32[17,64,128]{2,1,0:T(8,128)S(1)}, u32[]{:S(2)}, u32[]{:S(2)}) collective-permute-start(f32[17,64,128]{2,1,0:T(8,128)S(1)} %get-tuple-element.934), channel_id=1, source_target_pairs={{0,2},{1,3},{2,4},{3,5},{4,6},{5,7},{6,0},{7,1},{8,10},{9,11},{10,... | collective-permute-start | bytes 1671176 | tf_op jit(solution)/shard_map/cond/branch_1_fun/cond/branch_0_fun/ppermute | solution.py:417
  307.7 17.7 %collective-permute-start.95 = (f32[17,64,128]{2,1,0:T(8,128)}, f32[17,64,128]{2,1,0:T(8,128)S(1)}, u32[]{:S(2)}, u32[]{:S(2)}) collective-permute-start(f32[17,64,128]{2,1,0:T(8,128)} %get-tuple-element.661), channel_id=1, source_target_pairs={{0,2},{1,3},{2,4},{3,5},{4,6},{5,7},{6,0},{7,1},{8,10},{9,11},{10,... | collective-permute-start | bytes 1671176 | tf_op jit(solution)/shard_map/cond/branch_1_fun/cond/branch_0_fun/ppermute | solution.py:417
  309.7 37.9 %collective-permute-start.96 = (f32[17,64,128]{2,1,0:T(8,128)S(1)}, f32[17,64,128]{2,1,0:T(8,128)S(1)}, u32[]{:S(2)}, u32[]{:S(2)}) collective-permute-start(f32[17,64,128]{2,1,0:T(8,128)S(1)} %get-tuple-element.662), channel_id=1, source_target_pairs={{0,4},{1,5},{2,6},{3,7},{4,0},{5,1},{6,2},{7,3},{8,12},{9,13},{10,... | collective-permute-start | bytes 1671176 | tf_op jit(solution)/shard_map/cond/branch_1_fun/cond/branch_0_fun/ppermute | solution.py:417
  311.6 45.4 %collective-permute-start.97 = (f32[24,64,128]{2,1,0:T(8,128)S(1)}, f32[24,64,128]{2,1,0:T(8,128)S(1)}, u32[]{:S(2)}, u32[]{:S(2)}) collective-permute-start(f32[24,64,128]{2,1,0:T(8,128)S(1)} %get-tuple-element.663), channel_id=1, source_target_pairs={{0,8},{8,0},{16,24},{24,16},{1,9},{9,1},{17,25},{25,17},{2,10},{10... | collective-permute-start | bytes 2359304 | tf_op jit(solution)/shard_map/cond/branch_1_fun/cond/branch_0_fun/ppermute | solution.py:343
  313.1 43.9 %collective-permute-start.98 = (f32[24,64,128]{2,1,0:T(8,128)S(1)}, f32[24,64,128]{2,1,0:T(8,128)S(1)}, u32[]{:S(2)}, u32[]{:S(2)}) collective-permute-start(f32[24,64,128]{2,1,0:T(8,128)S(1)} %get-tuple-element.664), channel_id=1, source_target_pairs={{0,16},{8,24},{16,0},{24,8},{1,17},{9,25},{17,1},{25,9},{2,18},{10... | collective-permute-start | bytes 2359304 | tf_op jit(solution)/shard_map/cond/branch_1_fun/cond/branch_0_fun/ppermute | solution.py:343
  314.6 42.4 %collective-permute-start.99 = (f32[24,64,128]{2,1,0:T(8,128)S(1)}, f32[24,64,128]{2,1,0:T(8,128)S(1)}, u32[]{:S(2)}, u32[]{:S(2)}) collective-permute-start(f32[24,64,128]{2,1,0:T(8,128)S(1)} %get-tuple-element.665), channel_id=1, source_target_pairs={{0,24},{8,16},{16,8},{24,0},{1,25},{9,17},{17,9},{25,1},{2,26},{10... | collective-permute-start | bytes 2359304 | tf_op jit(solution)/shard_map/cond/branch_1_fun/cond/branch_0_fun/ppermute | solution.py:343
  325.4 31.5 %collective-permute-start.100 = (f32[17,64,128]{2,1,0:T(8,128)S(1)}, f32[17,64,128]{2,1,0:T(8,128)S(1)}, u32[]{:S(2)}, u32[]{:S(2)}) collective-permute-start(f32[17,64,128]{2,1,0:T(8,128)S(1)} %get-tuple-element.672), channel_id=1, source_target_pairs={{0,6},{1,7},{2,0},{3,1},{4,2},{5,3},{6,4},{7,5},{8,14},{9,15},{10,... | collective-permute-start | bytes 1671176 | tf_op jit(solution)/shard_map/cond/branch_1_fun/cond/branch_0_fun/ppermute | solution.py:417
  (49 other events, 1170.2 us)
